TPU v7x, 32 devices: a whole 2x2x4 slice. The times are simulated.
32 devices in a mesh: ctx: 4 (over x, core), shard: 8 (over z, y).
Axes of the slice: x: 2, y: 2, z: 4, core: 2. Of those that a mesh axis runs over, the one named last changes fastest.
Arguments:
- layer_input: bfloat16 [16, 1024, 1536], P('shard', 'ctx'), may hold values from -6 to 6
- cotangent: bfloat16 [16, 1024, 1536], P('shard', 'ctx'), may hold values from -6 to 6
- seq_lengths: int32 [16], P('shard'), may hold values from 256 to 1024, as said below
- routes: int32 [16, 1024, 4], P('shard', 'ctx'), may hold values from 0 to 15, all different within a row
- drop_order: int32 [16, 1024], P('shard', 'ctx'), may hold values from 0 to 1023, each once within a row
- block_order: int32 [8], replicated, may hold values from 0 to 7, each once
- attn_gain: bfloat16 [1536], P('shard'), may hold values from 0.5 to 1.5
- query_weight: bfloat16 [1536, 1536], P('shard'), may hold values from -0.15625 to 0.15625
- keyval_weight: bfloat16 [1536, 512], P('shard'), may hold values from -0.15625 to 0.15625
- output_weight: bfloat16 [1536, 1536], P('shard'), may hold values from -0.625 to 0.625
- moe_gain: bfloat16 [1536], P('shard'), may hold values from 0.5 to 1.5
- router_weight: bfloat16 [1536, 16], P('shard'), may hold values from -0.078125 to 0.078125
- expert_in: bfloat16 [16, 1536, 1536], P('shard', 'ctx'), may hold values from -0.15625 to 0.15625
- expert_out: bfloat16 [16, 768, 1536], P('shard', 'ctx'), may hold values from -0.21875 to 0.21875
Outputs:
- output: bfloat16 [16, 1024, 1536], P('shard', 'ctx')
- grad_input: bfloat16 [16, 1024, 1536], P('shard', 'ctx')
- grad_attn_gain: float32 [1536], P('shard')
- grad_query_weight: float32 [1536, 1536], P('shard')
- grad_keyval_weight: float32 [1536, 512], P('shard')
- grad_output_weight: float32 [1536, 1536], P('shard')
- grad_moe_gain: float32 [1536], P('shard')
- grad_router_weight: float32 [1536, 16], P('shard')
- grad_expert_in: float32 [16, 1536, 1536], P('shard', 'ctx')
- grad_expert_out: float32 [16, 768, 1536], P('shard', 'ctx')
Inputs may be any that keep to these rules, and one draw needn't show every extreme that they name: `seq_lengths`: among the 2 sequences of each index of shard one has length 1024. `routes`: each token names 4 different experts. `drop_order`: each sequence's row is a permutation. `block_order`: a permutation.
All inputs are finite; a program needn't handle non-finite values.
Results may differ from a plain program's by a relative error of at most 0.022.
Values may be sent and summed in bfloat16 or wider, within the bound.
No kernel may reach another device: no remote copies, remote signals or barrier semaphores. Data moves between devices by JAX's collectives and lax.ppermute only.
A program may use at most 256 MiB of HBM per device.

v0:
```python
import jax
import jax.numpy as jnp
from jax import lax
from jax.sharding import PartitionSpec as P

H = 12
KVH = 2
HD = 128
FF = 768
TOPK = 4


EPSILON = 1e-06
ROPE_BASE = 10000.0
HIGHEST = lax.Precision.HIGHEST
NEG_FILL = -1e30


def as_sent(value):
    return jax.tree.map(lambda a: a.astype(jnp.bfloat16) if a.dtype == jnp.float32 else a, value)


def rope_tables(positions, width):
    half_width = width // 2
    frequency = ROPE_BASE ** (-2.0 * jnp.arange(half_width, dtype=jnp.float32) / width)
    angles = positions.astype(jnp.float32)[:, None] * frequency[None, :]
    return (jnp.cos(angles), jnp.sin(angles))


def rotate(values, cosine_table, sine_table):
    half_width = values.shape[-1] // 2
    first_half = values[..., :half_width]
    second_half = values[..., half_width:]
    cosine_part = cosine_table[:, None, :]
    sine_part = sine_table[:, None, :]
    return jnp.concatenate(
        [
            first_half * cosine_part - second_half * sine_part,
            second_half * cosine_part + first_half * sine_part,
        ],
        axis=-1,
    )


def place_blocks(block_order, storage, sub_len):
    blocks = storage // sub_len
    matches = blocks[:, None] == jnp.arange(block_order.shape[0], dtype=jnp.int32)[None, :]
    return (
        jnp.sum(jnp.where(matches, block_order[None, :], 0), axis=1) * sub_len + storage % sub_len
    )


def norm_back(grad_normed, gain, normed, inverse):
    scaled = grad_normed * gain
    return inverse * (scaled - normed * jnp.mean(scaled * normed, axis=-1, keepdims=True))


def per_device(
    layer_input,
    cotangent,
    seq_lengths,
    routes,
    drop_order,
    block_order,
    attn_gain,
    query_weight,
    keyval_weight,
    output_weight,
    moe_gain,
    router_weight,
    expert_in,
    expert_out,
):
    seq_count, block_len, width = layer_input.shape
    ctx_size = lax.axis_size("ctx")
    shard_size = lax.axis_size("shard")
    token_count = seq_count * block_len
    seq_len = block_len * ctx_size
    expert_local = expert_in.shape[0]
    expert_count = expert_local * shard_size
    capacity = (5 * token_count * TOPK + 4 * expert_count - 1) // (4 * expert_count)
    group_ratio = H // KVH
    kv_width = 2 * KVH * HD
    scale = HD ** (-0.5)
    item_count = token_count * TOPK
    gathered = (
        lax.all_gather(query_weight, "shard", axis=0, tiled=True),
        lax.all_gather(keyval_weight, "shard", axis=0, tiled=True),
        lax.all_gather(output_weight, "shard", axis=0, tiled=True),
        lax.all_gather(router_weight, "shard", axis=0, tiled=True),
        lax.all_gather(attn_gain, "shard", axis=0, tiled=True),
        lax.all_gather(moe_gain, "shard", axis=0, tiled=True),
    )
    query_full, keyval_full, output_full, router_full, attn_full, moe_full = gathered
    attn_scale = attn_full.astype(jnp.float32)
    moe_scale = moe_full.astype(jnp.float32)
    expert_in_full, expert_out_full = (
        lax.all_gather(expert_in, "ctx", axis=1, tiled=True),
        lax.all_gather(expert_out, "ctx", axis=1, tiled=True),
    )
    sub_len = seq_len // block_order.shape[0]
    local_pos = place_blocks(
        block_order,
        lax.axis_index("ctx") * block_len + jnp.arange(block_len, dtype=jnp.int32),
        sub_len,
    )
    every_pos = place_blocks(block_order, jnp.arange(seq_len, dtype=jnp.int32), sub_len)
    live = local_pos[None, :] < seq_lengths[:, None]
    key_live = every_pos[None, :] < seq_lengths[:, None]
    live_flat = live.reshape(token_count).astype(jnp.float32)
    inputs_f = layer_input.astype(jnp.float32).reshape(token_count, width)
    inverse_one = lax.rsqrt(jnp.mean(inputs_f * inputs_f, axis=-1, keepdims=True) + EPSILON)
    normed_one = inputs_f * inverse_one
    hidden = (normed_one * attn_scale).astype(jnp.bfloat16)
    cosine_table, sine_table = rope_tables(local_pos, HD)
    query_raw = jnp.dot(hidden, query_full, preferred_element_type=jnp.float32).reshape(
        seq_count, block_len, H, HD
    )
    keyval_raw = jnp.dot(hidden, keyval_full, preferred_element_type=jnp.float32).reshape(
        seq_count, block_len, 2, KVH, HD
    )
    queries = (
        rotate(query_raw, cosine_table, sine_table)
        .astype(jnp.bfloat16)
        .reshape(seq_count, block_len, KVH, group_ratio, HD)
    )
    own_keys = rotate(keyval_raw[:, :, 0], cosine_table, sine_table)
    keyval = (
        jnp.stack([own_keys, keyval_raw[:, :, 1]], axis=2)
        .astype(jnp.bfloat16)
        .reshape(seq_count, block_len, kv_width)
    )
    all_keyval = lax.all_gather(keyval, "ctx", axis=1, tiled=True)

    def block_scores(source_kv, piece_num):
        kv_part = lax.dynamic_slice_in_dim(source_kv, piece_num * block_len, block_len, 1).reshape(
            seq_count, block_len, 2, KVH, HD
        )
        part_pos = lax.dynamic_slice_in_dim(every_pos, piece_num * block_len, block_len, 0)
        part_live = lax.dynamic_slice_in_dim(key_live, piece_num * block_len, block_len, 1)
        scores = (
            jnp.einsum(
                "sqgrd,skgd->sgqrk", queries, kv_part[:, :, 0], preferred_element_type=jnp.float32
            )
            * scale
        )
        allowed = (part_pos[None, None, :] <= local_pos[None, :, None]) & part_live[:, None, :]
        return (scores, allowed[:, None, :, None, :], kv_part[:, :, 0], kv_part[:, :, 1])

    start_max = jnp.full((seq_count, KVH, block_len, group_ratio, 1), NEG_FILL, jnp.float32)

    def gather_stats(carry, piece_num):
        row_max, row_sum = carry
        scores, allowed, unused_keys, unused_values = block_scores(all_keyval, piece_num)
        masked = jnp.where(allowed, scores, NEG_FILL)
        new_max = jnp.maximum(row_max, jnp.max(masked, axis=-1, keepdims=True))
        weights = jnp.where(allowed, jnp.exp(masked - new_max), 0.0)
        row_sum = row_sum * jnp.exp(row_max - new_max) + jnp.sum(weights, axis=-1, keepdims=True)
        return ((new_max, row_sum), None)

    (row_max, row_sum), unused = lax.scan(
        gather_stats, (start_max, jnp.zeros_like(start_max)), jnp.arange(ctx_size)
    )

    def probabilities(scores, allowed):
        return (
            jnp.where(allowed, jnp.exp(jnp.where(allowed, scores, NEG_FILL) - row_max), 0.0)
            / row_sum
        )

    def weigh_values(carry, piece_num):
        scores, allowed, unused_keys, part_values = block_scores(all_keyval, piece_num)
        probs_low = probabilities(scores, allowed).astype(jnp.bfloat16)
        return (
            carry
            + jnp.einsum(
                "sgqrk,skgd->sqgrd", probs_low, part_values, preferred_element_type=jnp.float32
            ),
            None,
        )

    attended, unused = lax.scan(
        weigh_values,
        jnp.zeros((seq_count, block_len, KVH, group_ratio, HD), jnp.float32),
        jnp.arange(ctx_size),
    )
    attended_low = attended.astype(jnp.bfloat16).reshape(token_count, H * HD)
    branch = jnp.dot(attended_low, output_full, preferred_element_type=jnp.float32)
    middle = inputs_f + branch
    inverse_two = lax.rsqrt(jnp.mean(middle * middle, axis=-1, keepdims=True) + EPSILON)
    normed_two = middle * inverse_two
    tokens = (normed_two * moe_scale).astype(jnp.bfloat16)
    logits = jnp.dot(tokens, router_full, preferred_element_type=jnp.float32)
    token_routes = routes.reshape(token_count, TOPK)
    route_hit = token_routes[:, :, None] == jnp.arange(expert_count, dtype=jnp.int32)[None, None, :]
    chosen = jnp.sum(jnp.where(route_hit, logits[:, None, :], 0.0), axis=-1)
    gates = jax.nn.softmax(chosen, axis=-1)
    expert_load = jnp.sum((route_hit & (live_flat[:, None, None] > 0)).astype(jnp.float32), axis=1)
    seq_ids = jnp.repeat(jnp.arange(seq_count, dtype=jnp.int32), block_len)
    priority = drop_order.reshape(token_count) * seq_count + seq_ids
    earlier = (priority[None, :] < priority[:, None]).astype(jnp.bfloat16)
    ahead_count = jnp.dot(
        earlier, expert_load.astype(jnp.bfloat16), preferred_element_type=jnp.float32
    )
    slot_of = jnp.sum(jnp.where(route_hit, ahead_count[:, None, :], 0.0), axis=-1).astype(jnp.int32)
    is_kept = (live_flat[:, None] > 0) & (slot_of < capacity)
    kept_float = is_kept.astype(jnp.float32)
    target = jnp.where(is_kept, token_routes * capacity + slot_of, 0).reshape(-1)
    slot_target = jnp.where(
        is_kept, token_routes * capacity + slot_of, expert_count * capacity
    ).reshape(-1)
    source = jnp.full((expert_count * capacity + 1,), item_count, jnp.int32)
    source = source.at[slot_target].set(jnp.arange(item_count, dtype=jnp.int32))[
        : expert_count * capacity
    ]
    padded = jnp.concatenate([tokens, jnp.zeros((1, width), jnp.bfloat16)], axis=0)
    outgoing = padded[source // TOPK].reshape(shard_size, expert_local, capacity, width)
    received = lax.all_to_all(outgoing, "shard", split_axis=0, concat_axis=2, tiled=True).reshape(
        expert_local, shard_size * capacity, width
    )
    both = jnp.einsum("erd,edf->erf", received, expert_in_full, preferred_element_type=jnp.float32)
    gate_part = both[..., :FF]
    up_part = both[..., FF:]
    sigmoid_gate = jax.nn.sigmoid(gate_part)
    silu_gate = gate_part * sigmoid_gate
    active = (silu_gate * up_part).astype(jnp.bfloat16)
    produced = jnp.einsum(
        "erf,efd->erd", active, expert_out_full, preferred_element_type=jnp.float32
    ).astype(jnp.bfloat16)
    returned = lax.all_to_all(
        produced.reshape(1, expert_local, shard_size * capacity, width),
        "shard",
        split_axis=2,
        concat_axis=0,
        tiled=True,
    ).reshape(expert_count * capacity, width)
    picked = returned[target].reshape(token_count, TOPK, width)
    mix_weight = gates * kept_float
    mixture = jnp.sum(mix_weight[..., None] * picked, axis=1)
    output = (middle + mixture).astype(jnp.bfloat16).reshape(seq_count, block_len, width)
    grad_out = cotangent.astype(jnp.float32).reshape(token_count, width) * live_flat[:, None]
    grad_gate = kept_float * jnp.sum(grad_out[:, None, :] * picked, axis=-1)
    grad_picked = (
        (mix_weight[..., None] * grad_out[:, None, :])
        .astype(jnp.bfloat16)
        .reshape(item_count, width)
    )
    grad_padded = jnp.concatenate([grad_picked, jnp.zeros((1, width), jnp.bfloat16)], axis=0)
    grad_outgoing = grad_padded[source].reshape(shard_size, expert_local, capacity, width)
    grad_produced = lax.all_to_all(
        grad_outgoing, "shard", split_axis=0, concat_axis=2, tiled=True
    ).reshape(expert_local, shard_size * capacity, width)
    grad_active = jnp.einsum(
        "erd,efd->erf", grad_produced, expert_out_full, preferred_element_type=jnp.float32
    )
    grad_expert_out = jnp.einsum(
        "erf,erd->efd", active, grad_produced, preferred_element_type=jnp.float32
    )
    grad_both = jnp.concatenate(
        [
            grad_active * up_part * sigmoid_gate * (1.0 + gate_part * (1.0 - sigmoid_gate)),
            grad_active * silu_gate,
        ],
        axis=-1,
    ).astype(jnp.bfloat16)
    grad_expert_in = jnp.einsum(
        "erd,erf->edf", received, grad_both, preferred_element_type=jnp.float32
    )
    grad_received = jnp.einsum(
        "erf,edf->erd", grad_both, expert_in_full, preferred_element_type=jnp.float32
    ).astype(jnp.bfloat16)
    grad_returned = lax.all_to_all(
        grad_received.reshape(1, expert_local, shard_size * capacity, width),
        "shard",
        split_axis=2,
        concat_axis=0,
        tiled=True,
    ).reshape(expert_count * capacity, width)
    grad_tokens = jnp.sum(
        kept_float[..., None] * grad_returned[target].reshape(token_count, TOPK, width), axis=1
    )
    grad_chosen = gates * (grad_gate - jnp.sum(gates * grad_gate, axis=-1, keepdims=True))
    grad_logits = jnp.sum(jnp.where(route_hit, grad_chosen[:, :, None], 0.0), axis=1)
    grad_router = jnp.dot(tokens.astype(jnp.float32).T, grad_logits, precision=HIGHEST)
    grad_tokens = grad_tokens + jnp.dot(
        grad_logits, router_full.astype(jnp.float32).T, precision=HIGHEST
    )
    grad_moe_gain = jnp.sum(grad_tokens * normed_two, axis=0)
    grad_middle = grad_out + norm_back(grad_tokens, moe_scale, normed_two, inverse_two)
    grad_branch = grad_middle.astype(jnp.bfloat16)
    grad_output_w = jnp.dot(attended_low.T, grad_branch, preferred_element_type=jnp.float32)
    grad_attended = jnp.dot(grad_branch, output_full.T, preferred_element_type=jnp.float32).astype(
        jnp.bfloat16
    )
    grad_heads = grad_attended.reshape(seq_count, block_len, KVH, group_ratio, HD)
    delta = jnp.sum(grad_heads.astype(jnp.float32) * attended, axis=-1)
    delta = jnp.transpose(delta, (0, 2, 1, 3))[..., None]
    back_keyval = lax.all_gather(keyval, "ctx", axis=1, tiled=True)

    def attend_back(grad_query, piece_num):
        scores, allowed, part_keys, part_values = block_scores(back_keyval, piece_num)
        probs = probabilities(scores, allowed)
        grad_probs = jnp.einsum(
            "sqgrd,skgd->sgqrk", grad_heads, part_values, preferred_element_type=jnp.float32
        )
        grad_scores = (probs * (grad_probs - delta)).astype(jnp.bfloat16)
        grad_query = grad_query + jnp.einsum(
            "sgqrk,skgd->sqgrd", grad_scores, part_keys, preferred_element_type=jnp.float32
        )
        grad_keys = (
            jnp.einsum(
                "sgqrk,sqgrd->skgd", grad_scores, queries, preferred_element_type=jnp.float32
            )
            * scale
        )
        grad_values = jnp.einsum(
            "sgqrk,sqgrd->skgd",
            probs.astype(jnp.bfloat16),
            grad_heads,
            preferred_element_type=jnp.float32,
        )
        return (
            grad_query,
            jnp.stack([grad_keys, grad_values], axis=2).reshape(seq_count, block_len, kv_width),
        )

    grad_query, kv_terms = lax.scan(
        attend_back,
        jnp.zeros((seq_count, block_len, KVH, group_ratio, HD), jnp.float32),
        jnp.arange(ctx_size),
    )
    grad_keyval = (
        lax.psum_scatter(kv_terms.astype(jnp.bfloat16), "ctx", scatter_dimension=0, tiled=True)
        .astype(jnp.float32)
        .reshape(seq_count, block_len, 2, KVH, HD)
    )
    grad_key_raw = rotate(grad_keyval[:, :, 0], cosine_table, -sine_table)
    grad_keyval_raw = (
        jnp.stack([grad_key_raw, grad_keyval[:, :, 1]], axis=2)
        .astype(jnp.bfloat16)
        .reshape(token_count, kv_width)
    )
    grad_query_raw = (
        rotate((grad_query * scale).reshape(seq_count, block_len, H, HD), cosine_table, -sine_table)
        .astype(jnp.bfloat16)
        .reshape(token_count, H * HD)
    )
    grad_query_w = jnp.dot(hidden.T, grad_query_raw, preferred_element_type=jnp.float32)
    grad_keyval_w = jnp.dot(hidden.T, grad_keyval_raw, preferred_element_type=jnp.float32)
    grad_hidden = jnp.dot(
        grad_query_raw, query_full.T, preferred_element_type=jnp.float32
    ) + jnp.dot(grad_keyval_raw, keyval_full.T, preferred_element_type=jnp.float32)
    grad_attn_gain = jnp.sum(grad_hidden * normed_one, axis=0)
    grad_input = (
        (grad_middle + norm_back(grad_hidden, attn_scale, normed_one, inverse_one))
        .astype(jnp.bfloat16)
        .reshape(seq_count, block_len, width)
    )
    summed = (
        lax.psum_scatter(
            grad_attn_gain.astype(jnp.bfloat16), "shard", scatter_dimension=0, tiled=True
        ).astype(jnp.float32),
        lax.psum_scatter(
            grad_query_w.astype(jnp.bfloat16), "shard", scatter_dimension=0, tiled=True
        ).astype(jnp.float32),
        lax.psum_scatter(
            grad_keyval_w.astype(jnp.bfloat16), "shard", scatter_dimension=0, tiled=True
        ).astype(jnp.float32),
        lax.psum_scatter(
            grad_output_w.astype(jnp.bfloat16), "shard", scatter_dimension=0, tiled=True
        ).astype(jnp.float32),
        lax.psum_scatter(
            grad_moe_gain.astype(jnp.bfloat16), "shard", scatter_dimension=0, tiled=True
        ).astype(jnp.float32),
        lax.psum_scatter(
            grad_router.astype(jnp.bfloat16), "shard", scatter_dimension=0, tiled=True
        ).astype(jnp.float32),
    )
    summed = jax.tree.map(
        lambda part: part.astype(jnp.float32), lax.psum(as_sent(tuple(summed)), "ctx")
    )
    expert_grads = (
        lax.psum_scatter(
            grad_expert_in.astype(jnp.bfloat16), "ctx", scatter_dimension=1, tiled=True
        ).astype(jnp.float32),
        lax.psum_scatter(
            grad_expert_out.astype(jnp.bfloat16), "ctx", scatter_dimension=1, tiled=True
        ).astype(jnp.float32),
    )
    return (output, grad_input) + tuple(summed) + tuple(expert_grads)


def solution(mesh):
    placed = (
        P("shard", "ctx", None),
        P("shard", "ctx", None),
        P("shard"),
        P("shard", "ctx", None),
        P("shard", "ctx"),
        P(),
        P("shard"),
        P("shard", None),
        P("shard", None),
        P("shard", None),
        P("shard"),
        P("shard", None),
        P("shard", "ctx", None),
        P("shard", "ctx", None),
    )
    return jax.shard_map(
        per_device,
        mesh=mesh,
        in_specs=placed,
        out_specs=(
            P("shard", "ctx", None),
            P("shard", "ctx", None),
            P("shard"),
            P("shard", None),
            P("shard", None),
            P("shard", None),
            P("shard"),
            P("shard", None),
            P("shard", "ctx", None),
            P("shard", "ctx", None),
        ),
        check_vma=False,
    )
```

profile of v0, /device:TPU:0, one launch (start us, length us, event | category | flops | bytes accessed | tf_op | source)
XLA Modules:
  0.0 1822.1 jit_solution(5284804199249387397)
XLA Ops:
  12.5 23.4 %all-reduce.7 = (bf16[1536]{0:T(1024)(128)(2,1)S(1)}, bf16[1536]{0:T(1024)(128)(2,1)S(1)}) all-reduce(bf16[1536]{0:T(1024)(128)(2,1)S(1)} %dynamic-update-slice, bf16[1536]{0:T(1024)(128)(2,1)S(1)} %dynamic-update-slice.1), channel_id=1, replica_groups=mesh['ctx'=4,'shard'=8] {'shard'}, use_global_device_ids=true, to_apply=%add.2 | all-reduce | flops 3072 | bytes 12288
  63.7 31.0 %all-gather = bf16[8,192,16]{1,2,0:T(8,128)(2,1)S(1)} all-gather(bf16[1,192,16]{1,2,0:T(8,128)(2,1)S(1)} %bitcast.395), channel_id=1, replica_groups=mesh['ctx'=4,'shard'=8] {'shard'}, dimensions={0}, use_global_device_ids=true | all-gather | bytes 55296 | tf_op jit(solution)/shard_map/all_gather | solution.py:90
  161.6 49.6 %while.37 = (s32[]{:T(128)}, f32[2,2,256,6,1]{2,3,1,0,4:T(8,128)S(1)}, f32[2,2,256,6,1]{2,3,1,0,4:T(8,128)S(1)}, s32[4]{0:T(128)S(1)}, s32[1024]{0:T(1024)S(1)},...) while((s32[]{:T(128)}, ...), condition=%wide.region_6.7_spmd.clone, body=%wide.region_3.6_spmd.clone.sunk | while | flops 415463424 | bytes 16348934 | solution.py:161
  211.2 44.4 %while.38 = (s32[]{:T(128)}, f32[2,256,2,6,128]{1,4,3,2,0:T(8,128)}, s32[4]{0:T(128)S(1)}, bf16[2,1024,512]{1,2,0:T(8,128)(2,1)}, s32[1024]{0:T(1024)S(1)}, /*in...) while((s32[]{:T(128)}, ...), condition=%wide.region_8.9_spmd.clone, body=%wide.region_7.8_spmd.clone.sunk | while | flops 816513024 | bytes 9885397 | solution.py:182
  291.4 20.0 %gather_fusion.2 = bf16[2560,1536]{1,0:T(8,128)(2,1)} fusion(bf16[2049,1536]{1,0:T(8,128)(2,1)} %concatenate.34, s32[3072]{0:T(1024)S(1)} %get-tuple-element.564), kind=kCustom, calls=%fused_computation.2 | custom fusion | bytes 15738880 | tf_op jit(solution)/shard_map/gather | solution.py:249
  327.4 161.9 %all-to-all-done.2 = bf16[8,2,160,1536]{3,2,1,0:T(8,128)(2,1)} async-done(((bf16[8,2,160,1536]{3,2,1,0:T(8,128)(2,1)}), bf16[8,2,160,1536]{3,2,1,0:T(8,128)(2,1)}, u32[]{:S(2)}, u32[]{:S(2)}) %all-to-all-start.2) | async-done | bytes 7864352 | tf_op jit(solution)/shard_map/all_to_all | solution.py:250
  502.0 163.7 %all-to-all-done = bf16[8,2,160,1536]{3,2,1,0:T(8,128)(2,1)} async-done(((bf16[8,2,160,1536]{3,2,1,0:T(8,128)(2,1)}), bf16[8,2,160,1536]{3,2,1,0:T(8,128)(2,1)}, u32[]{:S(2)}, u32[]{:S(2)}) %all-to-all-start) | async-done | bytes 7864352 | tf_op jit(solution)/shard_map/all_to_all | solution.py:218
  672.7 19.4 %fusion.70 = f32[2,1280,1536]{2,1,0:T(8,128)} fusion(bf16[2,1280,1536]{2,1,0:T(8,128)(2,1)} %bitcast.358, bf16[2,1536,1536]{2,1,0:T(8,128)(2,1)} %all-gather.16.cloned.1.call-done), kind=kOutput, calls=%fused_computation.203 | convolution fusion | flops 12079595520 | bytes 33030144 | tf_op jit(solution)/shard_map/erd,edf->erf/dot_general | solution.py:221
  718.9 43.7 %copy.196 = bf16[1,2,1280,1536]{3,1,0,2:T(2,128)(2,1)} copy(bf16[1,2,1280,1536]{3,2,1,0:T(8,128)(2,1)S(1)} %fusion.28) | data formatting | bytes 15728640 | tf_op jit(solution)/shard_map/reshape | solution.py:231
  767.7 19.4 %fusion.29 = bf16[1,2,1280,1536]{3,2,1,0:T(8,128)(2,1)} fusion(bf16[2,1536,1536]{2,1,0:T(8,128)(2,1)} %all-gather.16.cloned.1.call-done, bf16[2,1280,768]{2,1,0:T(8,128)(2,1)} %get-tuple-element.537, bf16[2,1280,768]{2,1,0:T(8,128)(2,1)} %get-tuple-element.536), kind=kOutput, calls=%fused_computation.65 | convolution fusion | flops 12099256320 | bytes 25165824 | tf_op jit(solution)/shard_map/erf,edf->erd/dot_general | solution.py:269
  802.7 135.7 %all-to-all-done.1 = bf16[1,2,1280,1536]{3,1,0,2:T(2,128)(2,1)} async-done(((bf16[1,2,1280,1536]{3,1,0,2:T(2,128)(2,1)}), bf16[1,2,1280,1536]{3,1,0,2:T(2,128)(2,1)}, u32[]{:S(2)}, u32[]{:S(2)}) %all-to-all-start.1) | async-done | bytes 7864352 | tf_op jit(solution)/shard_map/all_to_all | solution.py:230
  952.2 17.6 gather_fusion.1
  1000.8 113.6 %all-to-all-done.3 = bf16[1,2,1280,1536]{3,1,0,2:T(2,128)(2,1)} async-done(((bf16[1,2,1280,1536]{3,1,0,2:T(2,128)(2,1)}), bf16[1,2,1280,1536]{3,1,0,2:T(2,128)(2,1)}, u32[]{:S(2)}, u32[]{:S(2)}) %all-to-all-start.3) | async-done | bytes 7864352 | tf_op jit(solution)/shard_map/all_to_all | solution.py:272
  1122.3 17.5 gather_fusion.3
  1152.1 32.7 %multiply_reduce_fusion.1 = f32[512,1536]{1,0:T(8,128)S(1)} fusion(f32[512,4,1536]{2,1,0:T(4,128)} %reshape.833, f32[512,4]{1,0:T(8,128)S(1)} %copy-done.27), kind=kLoop, calls=%fused_computation.58 | loop fusion | flops 5505024 | bytes 15736832 | tf_op jit(solution)/shard_map/reduce_sum | solution.py:279
  1203.1 72.4 %while.39 = (s32[]{:T(128)}, f32[2,256,2,6,128]{1,4,3,2,0:T(8,128)}, bf16[4,2,256,512]{2,3,1,0:T(8,128)(2,1)}, s32[4]{0:T(128)S(1)}, bf16[2,1024,512]{1,2,0:T(8,...) while((s32[]{:T(128)}, ...), condition=%wide.region_24.25_spmd.clone, body=%wide.region_23.24_spmd.clone.sunk | while | flops 2029715456 | bytes 55286052 | solution.py:327
  1328.5 19.4 %convolution_convert_fusion = bf16[2,1536,1536]{2,1,0:T(8,128)(2,1)} fusion(bf16[2,1280,1536]{2,1,0:T(8,128)(2,1)} %bitcast.359, bf16[2,1280,768]{2,1,0:T(8,128)(2,1)} %get-tuple-element.537, bf16[2,1280,768]{2,1,0:T(8,128)(2,1)} %get-tuple-element.536), kind=kOutput, calls=%fused_computation.61 | convolution fusion | flops 12100042752 | bytes 25165824 | tf_op jit(solution)/shard_map/erd,erf->edf/dot_general | solution.py:266
  1366.1 55.0 %reduce-scatter.22.cloned.1.call-done = bf16[192,16]{1,0:T(8,128)(2,1)} async-done(((bf16[1536,16]{1,0:T(8,128)(2,1)}), bf16[192,16]{1,0:T(8,128)(2,1)}) %reduce-scatter.22.cloned.1.call-update) | async-done | bytes 6160
  1427.0 20.1 %all-reduce.6 = (bf16[1536]{0:T(1024)(128)(2,1)S(1)}, bf16[1536]{0:T(1024)(128)(2,1)S(1)}) all-reduce(bf16[1536]{0:T(1024)(128)(2,1)S(1)} %get-tuple-element.452, bf16[1536]{0:T(1024)(128)(2,1)S(1)} %copy-done.61), channel_id=3, replica_groups=mesh['ctx'=4,'shard'=8] {'shard'}, use_global_device_ids=true, to_apply=%region_28.29.clone | all-reduce | flops 3072 | bytes 12288
  1455.2 33.2 %reduce-scatter.14.cloned.1.call-done = bf16[192,512]{1,0:T(8,128)(2,1)} async-done(((bf16[1536,512]{1,0:T(8,128)(2,1)}), bf16[192,512]{1,0:T(8,128)(2,1)}) %reduce-scatter.14.cloned.1.call-update) | async-done | bytes 196624 | tf_op jit(solution)/shard_map/reduce_scatter | solution.py:366
  1488.4 98.3 %reduce-scatter.16.cloned.1.call-done = bf16[192,1536]{1,0:T(8,128)(2,1)} async-done(((bf16[1536,1536]{1,0:T(8,128)(2,1)}), bf16[192,1536]{1,0:T(8,128)(2,1)}) %reduce-scatter.16.cloned.1.call-update) | async-done | bytes 589840 | tf_op jit(solution)/shard_map/reduce_scatter | solution.py:369
  1586.7 99.6 %reduce-scatter.12.cloned.1.call-done = bf16[192,1536]{1,0:T(8,128)(2,1)} async-done(((bf16[1536,1536]{1,0:T(8,128)(2,1)}), bf16[192,1536]{1,0:T(8,128)(2,1)}) %reduce-scatter.12.cloned.1.call-update) | async-done | bytes 589840 | tf_op jit(solution)/shard_map/reduce_scatter | solution.py:363
  1691.1 76.1 %reduce-scatter.18.cloned.1.call-done = bf16[2,384,1536]{2,1,0:T(8,128)(2,1)} async-done(((bf16[2,1536,1536]{2,1,0:T(8,128)(2,1)}), bf16[2,384,1536]{2,1,0:T(8,128)(2,1)}) %reduce-scatter.18.cloned.1.call-update) | async-done | bytes 2359312 | tf_op jit(solution)/shard_map/reduce_scatter | solution.py:383
  1771.7 38.4 %all-reduce.12.cloned.1.call-done = (bf16[192,1536]{1,0:T(8,128)(2,1)}, bf16[192,512]{1,0:T(8,128)(2,1)}, bf16[192,1536]{1,0:T(8,128)(2,1)}) async-done(((bf16[192,1536]{1,0:T(8,128)(2,1)}, bf16[192,512]{1,0:T(8,128)(2,1)}, bf16[192,1536]{1,0:T(8,128)(2,1)}), (bf16[192,1536]{1,0:T(8,128)(2,1)}, bf16[192,512]{1,0:T(8,128)(2,1)}, bf16[192,1536]{1,0:T(8,128)(2,1)})) %all-reduce.12.cloned.1.call-update) | async-done | bytes 1376272 | tf_op jit(solution)/shard_map/psum | solution.py:380
  (478 shorter events, 557.0 us)
Async XLA Ops:
  7.2 49.9 %all-gather.8.cloned.1.call-start = ((), (), s32[]{:S(2)}) async-start(), calls=%async_computation.11 | async-start | bytes 1769472 | tf_op jit(solution)/shard_map/all_gather | solution.py:88
  7.9 130.5 %all-gather.12.cloned.1.call-start = ((), (), s32[]{:S(2)}) async-start(), calls=%async_computation.13 | async-start | bytes 5308416 | tf_op jit(solution)/shard_map/all_gather | solution.py:87
  8.7 152.9 %all-gather.10.cloned.1.call-start = ((), (), s32[]{:S(2)}) async-start(), calls=%async_computation.12 | async-start | bytes 2621440 | tf_op jit(solution)/shard_map/all_gather | solution.py:133
  40.6 109.3 %copy-start.21 = (f32[256,64]{0,1:T(8,128)}, f32[256,64]{0,1:T(8,128)S(1)}, u32[]{:S(2)}) copy-start(f32[256,64]{0,1:T(8,128)S(1)} %get-tuple-element.557) | copy-start | bytes 196612
  62.3 197.4 %all-gather.14.cloned.1.call-start = ((), (), s32[]{:S(2)}) async-start(), calls=%async_computation.14 | async-start | bytes 5308416 | tf_op jit(solution)/shard_map/all_gather | solution.py:89
  94.8 170.8 %copy-start.31 = (bf16[1536,16]{0,1:T(8,128)(2,1)}, bf16[1536,16]{0,1:T(8,128)(2,1)S(1)}, u32[]{:S(2)}) copy-start(bf16[1536,16]{0,1:T(8,128)(2,1)S(1)} %reshape.885) | copy-start | bytes 147460
  311.4 178.0 %all-to-all-start.2 = ((bf16[8,2,160,1536]{3,2,1,0:T(8,128)(2,1)}), bf16[8,2,160,1536]{3,2,1,0:T(8,128)(2,1)}, u32[]{:S(2)}, u32[]{:S(2)}) async-start(bf16[8,2,160,1536]{3,2,1,0:T(8,128)(2,1)} %bitcast.352), calls=%async_computation.2 | async-start | bytes 15728640 | tf_op jit(solution)/shard_map/all_to_all | solution.py:250
  317.1 355.7 %all-gather.16.cloned.1.call-start = ((), (), s32[]{:S(2)}) async-start(), calls=%async_computation.15 | async-start | bytes 11796480 | tf_op jit(solution)/shard_map/all_gather | solution.py:98
  489.4 176.3 %all-to-all-start = ((bf16[8,2,160,1536]{3,2,1,0:T(8,128)(2,1)}), bf16[8,2,160,1536]{3,2,1,0:T(8,128)(2,1)}, u32[]{:S(2)}, u32[]{:S(2)}) async-start(bf16[8,2,160,1536]{3,2,1,0:T(8,128)(2,1)} %bitcast.351), calls=%async_computation | async-start | bytes 15728640 | tf_op jit(solution)/shard_map/all_to_all | solution.py:218
  494.3 197.8 %all-gather.18.cloned.1.call-start = ((), (), s32[]{:S(2)}) async-start(), calls=%async_computation.16 | async-start | bytes 5898240 | tf_op jit(solution)/shard_map/all_gather | solution.py:99
  762.6 175.7 %all-to-all-start.1 = ((bf16[1,2,1280,1536]{3,1,0,2:T(2,128)(2,1)}), bf16[1,2,1280,1536]{3,1,0,2:T(2,128)(2,1)}, u32[]{:S(2)}, u32[]{:S(2)}) async-start(bf16[1,2,1280,1536]{3,1,0,2:T(2,128)(2,1)} %copy.196), calls=%async_computation.1 | async-start | bytes 15728640 | tf_op jit(solution)/shard_map/all_to_all | solution.py:230
  802.7 140.7 %copy-start.54 = (f32[512,4]{0,1:T(4,128)S(1)}, f32[512,4]{0,1:T(4,128)}, u32[]{:S(2)}) copy-start(f32[512,4]{0,1:T(4,128)} %get-tuple-element.530) | copy-start | bytes 24580
  802.7 141.6 %copy-start.55 = (s32[2048,1]{0,1:T(1,128)S(1)}, s32[2048,1]{0,1:T(1,128)}, u32[]{:S(2)}) copy-start(s32[2048,1]{0,1:T(1,128)} %get-tuple-element.549) | copy-start | bytes 24580
  938.3 176.0 %all-to-all-start.3 = ((bf16[1,2,1280,1536]{3,1,0,2:T(2,128)(2,1)}), bf16[1,2,1280,1536]{3,1,0,2:T(2,128)(2,1)}, u32[]{:S(2)}, u32[]{:S(2)}) async-start(bf16[1,2,1280,1536]{3,1,0,2:T(2,128)(2,1)} %copy.203), calls=%async_computation.3 | async-start | bytes 15728640 | tf_op jit(solution)/shard_map/all_to_all | solution.py:272
  943.3 362.0 %reduce-scatter.10.cloned.1.call-start = ((), (), s32[]{:S(2)}) async-start(), calls=%async_computation.17 | async-start | bytes 2621440 | tf_op jit(solution)/shard_map/reduce_scatter | solution.py:333
  1275.5 80.4 %reduce-scatter.20.cloned.1.call-start = ((), (), s32[]{:S(2)}) async-start(), calls=%async_computation.22 | async-start | bytes 5898240 | tf_op jit(solution)/shard_map/reduce_scatter | solution.py:386
  1287.3 133.8 %reduce-scatter.22.cloned.1.call-start = ((), (), s32[]{:S(2)}) async-start(), calls=%async_computation.23 | async-start | bytes 442368
  1290.3 198.1 %reduce-scatter.14.cloned.1.call-start = ((), (), s32[]{:S(2)}) async-start(), calls=%async_computation.19 | async-start | bytes 1769472 | tf_op jit(solution)/shard_map/reduce_scatter | solution.py:366
  1312.0 274.7 %reduce-scatter.16.cloned.1.call-start = ((), (), s32[]{:S(2)}) async-start(), calls=%async_computation.20 | async-start | bytes 5308416 | tf_op jit(solution)/shard_map/reduce_scatter | solution.py:369
  1318.0 368.2 %reduce-scatter.12.cloned.1.call-start = ((), (), s32[]{:S(2)}) async-start(), calls=%async_computation.18 | async-start | bytes 5308416 | tf_op jit(solution)/shard_map/reduce_scatter | solution.py:363
  1328.5 438.7 %reduce-scatter.18.cloned.1.call-start = ((), (), s32[]{:S(2)}) async-start(), calls=%async_computation.21 | async-start | bytes 11796480 | tf_op jit(solution)/shard_map/reduce_scatter | solution.py:383
  1348.0 462.1 %all-reduce.12.cloned.1.call-start = ((), (), s32[]{:S(2)}) async-start(), calls=%async_computation.24 | async-start | bytes 2752512 | tf_op jit(solution)/shard_map/psum | solution.py:380
  1358.8 63.1 %copy-start.16 = (bf16[1536,512]{1,0:T(8,128)(2,1)S(1)}, bf16[1536,512]{1,0:T(8,128)(2,1)}, u32[]{:S(2)}) copy-start(bf16[1536,512]{1,0:T(8,128)(2,1)} %all-gather.8.cloned.1.call-done) | copy-start | bytes 4718596
  1358.8 63.1 %copy-start.40 = (f32[1536]{0:T(1024)S(1)}, f32[1536]{0:T(1024)}, u32[]{:S(2)}) copy-start(f32[1536]{0:T(1024)} %copy-done.39) | copy-start | bytes 18436
  (77 other events, 834.6 us)
Sparse Core Ops, SparseCore 0:
  10.2 46.8 all-gather.7
  59.3 79.1 all-gather.11
  140.6 20.9 all-gather.9
  163.6 79.8 all-gather.13
  319.2 64.7 all-gather.15
  496.4 37.8 all-gather.17
  1275.6 29.6 reduce-scatter.9
  1308.0 47.8 reduce-scatter.19
  1359.7 61.3 reduce-scatter.21
  1424.4 63.9 reduce-scatter.13
  1492.5 94.1 reduce-scatter.15
  1591.2 95.0 reduce-scatter.11
  1689.0 78.1 reduce-scatter.17
  1769.8 40.2 all-reduce.11
where the time goes:
time: 1830 us; the launch traced here: 1820 us
  waiting for transfers between devices  1040 us (57%)
  local copies, waits for them, and re-layouts  290 us (16%)
  matrix products  233 us (13%)
  other arithmetic  132 us (7%)
  blocking collectives  80.7 us (4%)
  starting transfers between devices  21.7 us (1%)
    all_to_all x1, waiting for transfers between devices, per_device(): lax.all_to_all(outgoing, 'shard', split_axis=0, concat_axis=2, tiled=True)  164 us
    all_to_all x1, waiting for transfers between devices, per_device(): lax.all_to_all(grad_outgoing, 'shard', split_axis=0, concat_axis=2, tiled...  162 us
    all_to_all x1, waiting for transfers between devices, per_device(): lax.all_to_all(produced.reshape(1, expert_local, shard_size * capacity, w...  136 us
    all_to_all x1, waiting for transfers between devices, per_device(): lax.all_to_all(grad_received.reshape(1, expert_local, shard_size * capaci...  114 us
    reduce_scatter x1, waiting for transfers between devices, per_device(): lax.psum_scatter(grad_query_w.astype(jnp.bfloat16), 'shard', scatter_dime...  99.6 us
    reduce_scatter x1, waiting for transfers between devices, per_device(): lax.psum_scatter(grad_output_w.astype(jnp.bfloat16), 'shard', scatter_dim...  98.3 us
    reduce_scatter x1, waiting for transfers between devices, per_device(): lax.psum_scatter(grad_expert_in.astype(jnp.bfloat16), 'ctx', scatter_dime...  76.1 us
    unnamed x15, waiting for transfers between devices  57.7 us
  transfers between devices with their start and end apart: 18, of which 15 were waited for; matrix products, arithmetic and copies ran while one was open for 20% of the time, Pallas kernels for 0%

commit v1 on v0

v1 whole, which is shorter than its diff:
```python
import functools

import jax
import jax.numpy as jnp
from jax import lax
from jax.experimental import pallas as pl
from jax.experimental.pallas import tpu as pltpu
from jax.sharding import Mesh
from jax.sharding import PartitionSpec as P

H = 12
KVH = 2
HD = 128
FF = 768
TOPK = 4
GROUP = H // KVH

EPSILON = 1e-06
ROPE_BASE = 10000.0
HIGHEST = lax.Precision.HIGHEST
NEG_FILL = -1e30
LOG2E = 1.4426950408889634
SCALE = HD ** (-0.5)
VMEM_LIMIT = 60 * 1024 * 1024
F32 = jnp.float32
BF16 = jnp.bfloat16


def params(limit=VMEM_LIMIT):
    return pltpu.CompilerParams(vmem_limit_bytes=limit)


def nt(a, b, precision=None):
    return lax.dot_general(
        a, b, (((1,), (1,)), ((), ())), precision=precision, preferred_element_type=F32
    )


def tn(a, b, precision=None):
    return lax.dot_general(
        a, b, (((0,), (0,)), ((), ())), precision=precision, preferred_element_type=F32
    )


def nn(a, b, precision=None):
    return jnp.dot(a, b, precision=precision, preferred_element_type=F32)


def swap(value, axis, bit=1):
    size = lax.axis_size(axis)
    return lax.ppermute(value, axis, [(i, i ^ bit) for i in range(size)])


def bits_of(axis):
    size = lax.axis_size(axis)
    return [1 << k for k in range(size.bit_length() - 1)]


def add_low(a, b):
    return (a.astype(F32) + b.astype(F32)).astype(BF16)


def pick(value, index, axis):
    return lax.dynamic_index_in_dim(value, index, axis, keepdims=False)


def gather_group(part, low_first):
    bits = bits_of("l")
    count = len(bits)
    value = part.reshape((1,) * count + part.shape)
    order = range(count) if low_first else reversed(range(count))
    for k in order:
        value = jnp.concatenate([value, swap(value, "l", bits[k])], axis=count - 1 - k)
    return value.reshape((1 << count,) + part.shape)


def reduce_group(value, low_first):
    bits = bits_of("l")
    count = len(bits)
    order = list(range(count) if low_first else reversed(range(count)))
    rest = value.shape[1:]
    value = value.reshape((2,) * count + rest)
    for k in order:
        axis = count - 1 - k
        keep = lax.slice_in_dim(value, 0, 1, axis=axis)
        send = lax.slice_in_dim(value, 1, 2, axis=axis)
        value = add_low(keep, swap(send, "l", bits[k]))
    return value.reshape(rest)


def gather_expert(weight):
    local, rows, columns = weight.shape
    half = local // 2
    core, high = lax.axis_index("c"), lax.axis_index("h")
    keep = lax.dynamic_slice_in_dim(weight, core * half, half, 0)
    send = lax.dynamic_slice_in_dim(weight, (1 - core) * half, half, 0)
    other = swap(send, "c")
    pair = jnp.where(
        core == 0, jnp.stack([keep, other], axis=1), jnp.stack([other, keep], axis=1)
    )
    pieces = [jnp.stack([pair])]
    far = swap(pair, "t")
    n_high = lax.axis_size("h")
    whole = jnp.zeros((2, half, n_high, 2, rows, columns), weight.dtype)
    for t, piece in enumerate((pair, far)):
        pieces = [piece]
        for bit in bits_of("h"):
            pieces = pieces + [swap(p, "h", bit) for p in pieces]
        for r, p in enumerate(pieces):
            whole = lax.dynamic_update_slice(
                whole, p[None, :, None], (t, 0, high ^ r, 0, 0, 0)
            )
    return whole.reshape(2 * half, n_high * 2 * rows, columns)


def reduce_expert(grad, local):
    half = local // 2
    core, high = lax.axis_index("c"), lax.axis_index("h")
    n_high = lax.axis_size("h")
    rows = grad.shape[1] // (2 * n_high)
    value = grad.reshape(2, half, n_high, 2, rows, grad.shape[2])
    width = n_high
    for bit in reversed(bits_of("h")):
        width //= 2
        side = (high & bit) // bit
        keep = lax.dynamic_slice_in_dim(value, side * width, width, 2)
        send = lax.dynamic_slice_in_dim(value, (1 - side) * width, width, 2)
        value = add_low(keep, swap(send, "h", bit))
    value = value.reshape(2, half, 2, rows, grad.shape[2])
    value = add_low(value[0], swap(value[1], "t"))
    keep = pick(value, core, 1)
    other = swap(pick(value, 1 - core, 1), "c")
    return jnp.where(
        core == 0, jnp.concatenate([keep, other]), jnp.concatenate([other, keep])
    ).astype(F32)


def reduce_weight(grad):
    core = lax.axis_index("c")
    low, top = lax.axis_index("l"), lax.axis_index("t")
    n_low = lax.axis_size("l")
    rows, columns = grad.shape[0] // (4 * n_low), grad.shape[1]
    value = grad.reshape(2, n_low, 2, rows, columns)
    value = add_low(pick(value, core, 2), swap(pick(value, 1 - core, 2), "c"))
    count = n_low
    for bit in bits_of("l"):
        count //= 2
        value = value.reshape(2, count, 2, rows, columns)
        side = (low & bit) // bit
        value = add_low(pick(value, side, 2), swap(pick(value, 1 - side, 2), "l", bit))
    value = value.reshape(2, rows, columns)
    value = add_low(pick(value, top, 0), swap(pick(value, 1 - top, 0), "t"))
    for bit in bits_of("h"):
        value = add_low(value, swap(value, "h", bit))
    other = swap(value, "c")
    return jnp.where(
        core == 0, jnp.concatenate([value, other]), jnp.concatenate([other, value])
    ).astype(F32)


def norm_back(grad_normed, gain, normed, inverse):
    scaled = grad_normed * gain
    return inverse * (scaled - normed * jnp.mean(scaled * normed, axis=-1, keepdims=True))


def turn(values, cosine, sine):
    return values * cosine + pltpu.roll(values, HD // 2, 1) * sine


def project_kernel(x_ref, gain_ref, w_ref, cos_ref, sin_ref, hidden_ref, out_ref):
    step = pl.program_id(0)

    @pl.when(step == 0)
    def _():
        x = x_ref[...].astype(F32)
        inverse = lax.rsqrt(jnp.mean(x * x, axis=-1, keepdims=True) + EPSILON)
        hidden_ref[...] = ((x * inverse) * gain_ref[...]).astype(BF16)

    raw = nn(hidden_ref[...], w_ref[...])
    per_step = raw.shape[1] // HD
    for k in range(per_step):
        head = raw[:, k * HD : (k + 1) * HD]
        turned = turn(head, cos_ref[...], sin_ref[...])
        is_value = step * per_step + k >= H + KVH
        out_ref[:, k * HD : (k + 1) * HD] = jnp.where(is_value, head, turned).astype(BF16)


def project(x, gain, weight, cosine, sine):
    rows, width = x.shape
    columns = weight.shape[1]
    block = 512
    return pl.pallas_call(
        project_kernel,
        grid=(columns // block,),
        in_specs=[
            pl.BlockSpec((rows, width), lambda i: (0, 0)),
            pl.BlockSpec((1, width), lambda i: (0, 0)),
            pl.BlockSpec((width, block), lambda i: (0, i)),
            pl.BlockSpec((rows, HD), lambda i: (0, 0)),
            pl.BlockSpec((rows, HD), lambda i: (0, 0)),
        ],
        out_specs=[
            pl.BlockSpec((rows, width), lambda i: (0, 0)),
            pl.BlockSpec((rows, block), lambda i: (0, i)),
        ],
        out_shape=[
            jax.ShapeDtypeStruct((rows, width), BF16),
            jax.ShapeDtypeStruct((rows, columns), BF16),
        ],
        compiler_params=params(),
        cost_estimate=pl.CostEstimate(
            flops=2 * rows * width * columns,
            bytes_accessed=2 * (2 * rows * width + width * columns + rows * columns),
            transcendentals=0,
        ),
        name="project",
    )(x, gain, weight, cosine, sine)


def set_bias(len_ref, posk_ref, posq_ref, bias):
    seq = pl.program_id(0)

    @pl.when((pl.program_id(1) == 0) & (pl.program_id(2) == 0))
    def _():
        posk = posk_ref[...]
        allowed = (posk <= posq_ref[...]) & (posk < len_ref[seq])
        bias[...] = jnp.where(allowed, 0.0, NEG_FILL)


def attend_kernel(len_ref, q_ref, k_ref, v_ref, posk_ref, posq_ref, out_ref, lse_ref, bias, turned):
    set_bias(len_ref, posk_ref, posq_ref, bias)

    @pl.when(pl.program_id(2) == 0)
    def _():
        turned[...] = v_ref[0].T

    scores = nt(k_ref[0], q_ref[...]) * (SCALE * LOG2E) + bias[...]
    top = jnp.max(scores, axis=0, keepdims=True)
    weights = jnp.exp2(scores - top)
    total = jnp.sum(weights, axis=0, keepdims=True)
    mixed = nn(turned[...], weights.astype(BF16)) * (1.0 / total)
    out_ref[...] = mixed.T.astype(BF16)
    lse_ref[0, 0] = top + jnp.log2(total)


def attend(lengths, qkv, keyval, posk, posq):
    seqs, keys, _ = keyval.shape
    rows = qkv.shape[0] // seqs
    return pl.pallas_call(
        attend_kernel,
        grid_spec=pltpu.PrefetchScalarGridSpec(
            num_scalar_prefetch=1,
            grid=(seqs, KVH, GROUP),
            in_specs=[
                pl.BlockSpec((rows, HD), lambda s, g, h, n: (s, g * GROUP + h)),
                pl.BlockSpec((1, keys, HD), lambda s, g, h, n: (s, 0, g)),
                pl.BlockSpec((1, keys, HD), lambda s, g, h, n: (s, 0, KVH + g)),
                pl.BlockSpec((keys, 1), lambda s, g, h, n: (0, 0)),
                pl.BlockSpec((1, rows), lambda s, g, h, n: (0, 0)),
            ],
            out_specs=[
                pl.BlockSpec((rows, HD), lambda s, g, h, n: (s, g * GROUP + h)),
                pl.BlockSpec((1, 1, 1, rows), lambda s, g, h, n: (s, g * GROUP + h, 0, 0)),
            ],
            scratch_shapes=[pltpu.VMEM((keys, rows), F32), pltpu.VMEM((HD, keys), BF16)],
        ),
        out_shape=[
            jax.ShapeDtypeStruct((seqs * rows, H * HD), BF16),
            jax.ShapeDtypeStruct((seqs, H, 1, rows), F32),
        ],
        compiler_params=params(),
        cost_estimate=pl.CostEstimate(
            flops=4 * seqs * H * rows * keys * HD,
            bytes_accessed=4 * seqs * (rows * H * HD + keys * 2 * KVH * HD),
            transcendentals=seqs * H * rows * keys,
        ),
        name="attend",
    )(lengths, qkv, keyval, keyval, posk, posq)


def attend_back_kernel(
    len_ref, q_ref, k_ref, v_ref, posk_ref, posq_ref, grad_ref, out_ref, lse_ref, cos_ref, sin_ref,
    dq_ref, dkv_ref, bias, turned, dk, dv,
):
    set_bias(len_ref, posk_ref, posq_ref, bias)
    head = pl.program_id(2)

    @pl.when(head == 0)
    def _():
        turned[...] = k_ref[0].T
        dk[...] = jnp.zeros_like(dk)
        dv[...] = jnp.zeros_like(dv)

    q, grad = q_ref[...], grad_ref[...]
    scores = nt(k_ref[0], q) * (SCALE * LOG2E) + bias[...]
    probs = jnp.exp2(scores - lse_ref[0, 0])
    grad_probs = nt(v_ref[0], grad)
    product = grad.astype(F32) * out_ref[...].astype(F32)
    delta = jnp.sum(product.T, axis=0, keepdims=True)
    grad_scores = (probs * (grad_probs - delta)).astype(BF16)
    dv[...] += nn(probs.astype(BF16), grad)
    dk[...] += nn(grad_scores, q)
    dq = nn(turned[...], grad_scores).T * SCALE
    dq_ref[...] = turn(dq, cos_ref[...], -sin_ref[...]).astype(BF16)

    @pl.when(head == GROUP - 1)
    def _():
        dkv_ref[0, 0] = (dk[...] * SCALE).astype(BF16)
        dkv_ref[1, 0] = dv[...].astype(BF16)


def attend_back(lengths, qkv, keyval, posk, posq, grad, attended, lse, cosine, sine):
    seqs, keys, _ = keyval.shape
    rows = qkv.shape[0] // seqs
    heads = pl.BlockSpec((rows, HD), lambda s, g, h, n: (s, g * GROUP + h))
    table = pl.BlockSpec((rows, HD), lambda s, g, h, n: (0, 0))
    return pl.pallas_call(
        attend_back_kernel,
        grid_spec=pltpu.PrefetchScalarGridSpec(
            num_scalar_prefetch=1,
            grid=(seqs, KVH, GROUP),
            in_specs=[
                heads,
                pl.BlockSpec((1, keys, HD), lambda s, g, h, n: (s, 0, g)),
                pl.BlockSpec((1, keys, HD), lambda s, g, h, n: (s, 0, KVH + g)),
                pl.BlockSpec((keys, 1), lambda s, g, h, n: (0, 0)),
                pl.BlockSpec((1, rows), lambda s, g, h, n: (0, 0)),
                heads,
                heads,
                pl.BlockSpec((1, 1, 1, rows), lambda s, g, h, n: (s, g * GROUP + h, 0, 0)),
                table,
                table,
            ],
            out_specs=[
                heads,
                pl.BlockSpec((2, 1, keys, HD), lambda s, g, h, n: (0, s, 0, g)),
            ],
            scratch_shapes=[
                pltpu.VMEM((keys, rows), F32),
                pltpu.VMEM((HD, keys), BF16),
                pltpu.VMEM((keys, HD), F32),
                pltpu.VMEM((keys, HD), F32),
            ],
        ),
        out_shape=[
            jax.ShapeDtypeStruct((seqs * rows, H * HD), BF16),
            jax.ShapeDtypeStruct((2, seqs, keys, KVH * HD), BF16),
        ],
        compiler_params=params(),
        cost_estimate=pl.CostEstimate(
            flops=10 * seqs * H * rows * keys * HD,
            bytes_accessed=4 * seqs * (2 * rows * H * HD + keys * 2 * KVH * HD),
            transcendentals=seqs * H * rows * keys,
        ),
        name="attend_back",
    )(lengths, qkv, keyval, keyval, posk, posq, grad, attended, lse, cosine, sine)


def route_kernel(
    att_ref, w_ref, x_ref, gain_ref, router_ref, hit_ref, middle_ref, first_ref, second_ref, gates_ref
):
    rows = x_ref.shape[0]
    experts = hit_ref.shape[0]
    middle = x_ref[...].astype(F32) + nn(att_ref[...], w_ref[...])
    middle_ref[...] = middle
    inverse = lax.rsqrt(jnp.mean(middle * middle, axis=-1, keepdims=True) + EPSILON)
    tokens = ((middle * inverse) * gain_ref[...]).astype(BF16)
    first_ref[...] = tokens[: rows // 2]
    second_ref[: rows // 2] = tokens[rows // 2 :]
    hit = hit_ref[...] > 0
    logits = jnp.where(hit, nt(router_ref[...], tokens), NEG_FILL)
    raised = jnp.where(hit, jnp.exp(logits - jnp.max(logits, axis=0, keepdims=True)), 0.0)
    gates = raised / jnp.sum(raised, axis=0, keepdims=True)
    gates_ref[...] = gates
    coarse = gates.astype(BF16)
    fine = (gates - coarse.astype(F32)).astype(BF16)
    second_ref[rows // 2 :, :rows] = coarse
    second_ref[rows // 2 :, rows : 2 * rows] = fine
    second_ref[rows // 2 :, 2 * rows :] = jnp.zeros(
        (experts, second_ref.shape[1] - 2 * rows), BF16
    )


def route(attended, weight, x, gain, router, hit):
    rows, width = x.shape
    experts = hit.shape[0]
    return pl.pallas_call(
        route_kernel,
        out_shape=[
            jax.ShapeDtypeStruct((rows, width), F32),
            jax.ShapeDtypeStruct((rows // 2, width), BF16),
            jax.ShapeDtypeStruct((rows // 2 + experts, width), BF16),
            jax.ShapeDtypeStruct((experts, rows), F32),
        ],
        compiler_params=params(),
        cost_estimate=pl.CostEstimate(
            flops=2 * rows * width * (width + HD),
            bytes_accessed=2 * width * (width + 5 * rows),
            transcendentals=experts * rows,
        ),
        name="route",
    )(attended, weight, x, gain, router, hit)


def expert_kernel(
    cap, ids_ref, tok_a, tok_b, cot_a, cot_b, win_ref, wout_ref, *refs
):
    x_ref, active_ref, both_ref, grad_ref, mix_ref, back_ref = refs[-6:]
    number = pl.program_id(1)
    mine = ids_ref[number]
    half = tok_a.shape[1]
    rows = 2 * half
    experts = tok_b.shape[1] - half
    width = tok_a.shape[2]
    row_is_mine = lax.broadcasted_iota(jnp.int32, (experts, 1), 0) == mine

    def own_row(values):
        return jnp.sum(jnp.where(row_is_mine, values.astype(F32), 0.0), axis=0, keepdims=True)

    hits, spreads, gates, picked, grads = [], [], [], [], []
    for g in range(2):
        slot = own_row(cot_b[g, half:, :rows]).astype(jnp.int32)
        gate_row = own_row(
            tok_b[g, half:, :rows].astype(F32) + tok_b[g, half:, rows : 2 * rows].astype(F32)
        )
        hit = lax.broadcasted_iota(jnp.int32, (cap, rows), 0) == slot
        spread = jnp.where(hit, 1.0, 0.0).astype(BF16)
        hits.append(hit)
        spreads.append(spread)
        gates.append(jnp.sum(jnp.where(hit, gate_row, 0.0), axis=1, keepdims=True))
        picked.append(nn(spread[:, :half], tok_a[g]) + nn(spread[:, half:], tok_b[g, :half]))
        grads.append(nn(spread[:, :half], cot_a[g]) + nn(spread[:, half:], cot_b[g, :half]))
    tokens = jnp.concatenate(picked, axis=0).astype(BF16)
    grad_out = jnp.concatenate(grads, axis=0)
    gate = jnp.concatenate(gates, axis=0)
    x_ref[0, 0] = tokens.reshape(2, cap, width)
    both = nn(tokens, win_ref[0])
    gate_part, up_part = both[:, :FF], both[:, FF:]
    sigmoid = 1.0 / (1.0 + jnp.exp(-gate_part))
    silu = gate_part * sigmoid
    active = (silu * up_part).astype(BF16)
    active_ref[0, 0] = active.reshape(2, cap, FF)
    produced = nn(active, wout_ref[0]).astype(BF16).astype(F32)
    grad_gate = jnp.sum(produced * grad_out, axis=1, keepdims=True)
    weighed = (produced * gate).astype(BF16)
    grad_produced = (grad_out * gate).astype(BF16)
    grad_ref[0, 0] = grad_produced.reshape(2, cap, width)
    grad_active = nt(grad_produced, wout_ref[0])
    grad_both = jnp.concatenate(
        [
            grad_active * up_part * sigmoid * (1.0 + gate_part * (1.0 - sigmoid)),
            grad_active * silu,
        ],
        axis=1,
    ).astype(BF16)
    both_ref[0, 0] = grad_both.reshape(2, cap, 2 * FF)
    grad_rows = nt(grad_both, win_ref[0]).astype(BF16)

    @pl.when(number == 0)
    def _():
        mix_ref[...] = jnp.zeros_like(mix_ref)
        back_ref[...] = jnp.zeros_like(back_ref)

    for g in range(2):
        part = slice(g * cap, (g + 1) * cap)
        mix_ref[g] = (mix_ref[g].astype(F32) + tn(spreads[g], weighed[part])).astype(BF16)
        back_ref[g, :rows] = (
            back_ref[g, :rows].astype(F32) + tn(spreads[g], grad_rows[part])
        ).astype(BF16)
        dense = jnp.sum(jnp.where(hits[g], grad_gate[part], 0.0), axis=0, keepdims=True)
        coarse = dense.astype(BF16).astype(F32)
        fine = dense - coarse
        back_ref[g, rows:, :rows] += jnp.where(row_is_mine, coarse, 0.0).astype(BF16)
        back_ref[g, rows:, rows : 2 * rows] += jnp.where(row_is_mine, fine, 0.0).astype(BF16)


def experts_step(ids, cap, side, tok_a, tok_b, cot_a, cot_b, win, wout, earlier):
    n_low, half, width = tok_a.shape
    experts = tok_b.shape[1] - half
    local = win.shape[0]
    tokens = lambda n: pl.BlockSpec((2, n, width), lambda i, j, ids: (i, 0, 0))
    rows = lambda n: pl.BlockSpec((1, 1, 2, cap, n), lambda i, j, ids: (j, side, i, 0, 0))
    rows_shape = lambda n: jax.ShapeDtypeStruct((local, 2, n_low, cap, n), BF16)
    earlier = tuple(earlier)
    n_rows = local * n_low * cap
    return pl.pallas_call(
        functools.partial(expert_kernel, cap),
        grid_spec=pltpu.PrefetchScalarGridSpec(
            num_scalar_prefetch=1,
            grid=(n_low // 2, local),
            in_specs=[
                tokens(half),
                tokens(half + experts),
                tokens(half),
                tokens(half + experts),
                pl.BlockSpec((1,) + win.shape[1:], lambda i, j, ids: (j, 0, 0)),
                pl.BlockSpec((1,) + wout.shape[1:], lambda i, j, ids: (j, 0, 0)),
            ]
            + [pl.BlockSpec(memory_space=pl.ANY)] * len(earlier),
            out_specs=[
                rows(width),
                rows(FF),
                rows(2 * FF),
                rows(width),
                tokens(2 * half),
                tokens(2 * half + experts),
            ],
        ),
        out_shape=[
            rows_shape(width),
            rows_shape(FF),
            rows_shape(2 * FF),
            rows_shape(width),
            jax.ShapeDtypeStruct((n_low, 2 * half, width), BF16),
            jax.ShapeDtypeStruct((n_low, 2 * half + experts, width), BF16),
        ],
        input_output_aliases={7 + k: k for k in range(len(earlier))},
        compiler_params=params(),
        cost_estimate=pl.CostEstimate(
            flops=n_rows * (12 * width * FF + 16 * half * width),
            bytes_accessed=2 * (n_low * half * width * 8 + n_rows * 4 * width + 6 * FF * width * local),
            transcendentals=n_rows * FF,
        ),
        name="experts",
    )(ids, tok_a, tok_b, cot_a, cot_b, win, wout, *earlier)


def unroute_kernel(
    first_ref, second_ref, gates_ref, middle_ref, gain_ref, router_ref, cot_ref, w_ref,
    grad_ref, branch_ref, att_ref, router_grad_ref, gain_grad_ref,
):
    rows = middle_ref.shape[0]
    half = rows // 2
    gates = gates_ref[...]
    grad_gate = second_ref[half:, :rows].astype(F32) + second_ref[half:, rows : 2 * rows].astype(F32)
    grad_logits = gates * (grad_gate - jnp.sum(gates * grad_gate, axis=0, keepdims=True))
    middle = middle_ref[...]
    inverse = lax.rsqrt(jnp.mean(middle * middle, axis=-1, keepdims=True) + EPSILON)
    normed = middle * inverse
    tokens = (normed * gain_ref[...]).astype(BF16).astype(F32)
    router_grad_ref[...] = nn(grad_logits, tokens, HIGHEST)
    grad_tokens = jnp.concatenate([first_ref[...], second_ref[:half]], axis=0).astype(F32)
    grad_tokens = grad_tokens + nn(grad_logits.T, router_ref[...].astype(F32), HIGHEST)
    gain_grad_ref[...] = jnp.sum(grad_tokens * normed, axis=0, keepdims=True)
    grad_middle = cot_ref[...].astype(F32) + norm_back(grad_tokens, gain_ref[...], normed, inverse)
    grad_ref[...] = grad_middle
    branch = grad_middle.astype(BF16)
    branch_ref[...] = branch
    att_ref[...] = nt(branch, w_ref[...]).astype(BF16)


def unroute(first, second, gates, middle, gain, router, cotangent, weight):
    rows, width = middle.shape
    experts = gates.shape[0]
    return pl.pallas_call(
        unroute_kernel,
        out_shape=[
            jax.ShapeDtypeStruct((rows, width), F32),
            jax.ShapeDtypeStruct((rows, width), BF16),
            jax.ShapeDtypeStruct((rows, width), BF16),
            jax.ShapeDtypeStruct((experts, width), F32),
            jax.ShapeDtypeStruct((1, width), F32),
        ],
        compiler_params=params(),
        cost_estimate=pl.CostEstimate(
            flops=2 * rows * width * (width + HD),
            bytes_accessed=2 * width * (width + 8 * rows),
            transcendentals=0,
        ),
        name="unroute",
    )(first, second, gates, middle, gain, router, cotangent, weight)


def unproject_kernel(
    x_ref, gain_ref, grad_ref, dq_ref, dkv_ref, w_ref, cos_ref, sin_ref, out_ref, dkv_raw_ref, gain_grad_ref
):
    rows, width = x_ref.shape
    for k in range(KVH):
        part = slice(k * HD, (k + 1) * HD)
        dkv_raw_ref[:, part] = turn(
            dkv_ref[0, :, part].astype(F32), cos_ref[...], -sin_ref[...]
        ).astype(BF16)
    dkv_raw_ref[:, KVH * HD :] = dkv_ref[1]
    n_query = dq_ref.shape[1]
    grad_hidden = nt(dq_ref[...], w_ref[:, :n_query]) + nt(dkv_raw_ref[...], w_ref[:, n_query:])
    x = x_ref[...].astype(F32)
    inverse = lax.rsqrt(jnp.mean(x * x, axis=-1, keepdims=True) + EPSILON)
    normed = x * inverse
    gain_grad_ref[...] = jnp.sum(grad_hidden * normed, axis=0, keepdims=True)
    out_ref[...] = (
        grad_ref[...] + norm_back(grad_hidden, gain_ref[...], normed, inverse)
    ).astype(BF16)


def unproject(x, gain, grad_middle, dq, dkv, weight, cosine, sine):
    rows, width = x.shape
    return pl.pallas_call(
        unproject_kernel,
        out_shape=[
            jax.ShapeDtypeStruct((rows, width), BF16),
            jax.ShapeDtypeStruct((rows, 2 * KVH * HD), BF16),
            jax.ShapeDtypeStruct((1, width), F32),
        ],
        compiler_params=params(),
        cost_estimate=pl.CostEstimate(
            flops=2 * rows * width * weight.shape[1],
            bytes_accessed=2 * width * (weight.shape[1] + 5 * rows),
            transcendentals=0,
        ),
        name="unproject",
    )(x, gain, grad_middle, dq, dkv, weight, cosine, sine)


def place_blocks(block_order, storage, sub_len):
    blocks = storage // sub_len
    matches = blocks[:, None] == jnp.arange(block_order.shape[0], dtype=jnp.int32)[None, :]
    return (
        jnp.sum(jnp.where(matches, block_order[None, :], 0), axis=1) * sub_len + storage % sub_len
    )


def per_device(
    layer_input,
    cotangent,
    seq_lengths,
    routes,
    drop_order,
    block_order,
    attn_gain,
    query_weight,
    keyval_weight,
    output_weight,
    moe_gain,
    router_weight,
    expert_in,
    expert_out,
):
    seqs, block_len, width = layer_input.shape
    core, high = lax.axis_index("c"), lax.axis_index("h")
    top, low = lax.axis_index("t"), lax.axis_index("l")
    n_high, n_low = lax.axis_size("h"), lax.axis_size("l")
    ctx_size, shard_size = 2 * n_high, 2 * n_low
    rows = seqs * block_len
    seq_len = block_len * ctx_size
    local = expert_in.shape[0]
    experts = local * shard_size
    cap = (5 * rows * TOPK + 4 * experts - 1) // (4 * experts)
    half = rows // 2

    small = jnp.concatenate([attn_gain[:, None], moe_gain[:, None], router_weight], axis=1)
    small = jnp.pad(small, ((0, 0), (0, HD - small.shape[1])))
    first_pack = jnp.concatenate([query_weight, keyval_weight, small], axis=1)

    def gather_weight(part):
        own = pick(part.reshape(2, part.shape[0] // 2, part.shape[1]), core, 0)
        return lax.all_gather(own, ("t", "l", "c"), axis=0, tiled=True)

    first_full = gather_weight(first_pack)
    output_full = gather_weight(output_weight)
    n_qkv = query_weight.shape[1] + keyval_weight.shape[1]
    qkv_full = first_full[:, :n_qkv]
    small_full = first_full[:, n_qkv:].T
    attn_scale = small_full[0:1].astype(F32)
    moe_scale = small_full[1:2].astype(F32)
    router_full = small_full[2 : 2 + experts]

    sub_len = seq_len // block_order.shape[0]
    inner = jnp.arange(block_len, dtype=jnp.int32)
    local_pos = place_blocks(block_order, (high * 2 + core) * block_len + inner, sub_len)
    relative = jnp.arange(ctx_size, dtype=jnp.int32)
    key_ctx = ((relative // 2) ^ high) * 2 + ((relative % 2) ^ core)
    key_pos = place_blocks(
        block_order, (key_ctx[:, None] * block_len + inner[None, :]).reshape(-1), sub_len
    )
    live = (local_pos[None, :] < seq_lengths[:, None]).reshape(rows)
    token_routes = routes.reshape(rows, TOPK).T
    hit = jnp.any(
        token_routes[None, :, :] == jnp.arange(experts, dtype=jnp.int32)[:, None, None], axis=1
    )
    load = hit & live[None, :]
    seq_ids = jnp.repeat(jnp.arange(seqs, dtype=jnp.int32), block_len)
    priority = drop_order.reshape(rows) * seqs + seq_ids
    earlier = (priority[:, None] < priority[None, :]).astype(BF16)
    ahead = jnp.dot(load.astype(BF16), earlier, preferred_element_type=F32)
    slots = jnp.where(load & (ahead < cap), ahead, -1.0).astype(BF16)

    angles = local_pos.astype(F32)[:, None] * (
        ROPE_BASE ** (-2.0 * jnp.arange(HD // 2, dtype=F32) / HD)
    )
    cosine, sine = jnp.cos(angles), jnp.sin(angles)
    cosine = jnp.concatenate([cosine, cosine], axis=1)
    sine = jnp.concatenate([-sine, sine], axis=1)
    cosine_rows, sine_rows = jnp.tile(cosine, (seqs, 1)), jnp.tile(sine, (seqs, 1))

    win = gather_expert(expert_in)
    wout = gather_expert(expert_out)

    x = layer_input.reshape(rows, width)
    hidden, qkv = project(x, attn_scale, qkv_full, cosine_rows, sine_rows)
    keyval = qkv[:, H * HD :].reshape(seqs, 1, 1, block_len, 2 * KVH * HD)
    for bit in bits_of("h"):
        keyval = jnp.concatenate([keyval, swap(keyval, "h", bit)], axis=1)
    keyval = jnp.concatenate([keyval, swap(keyval, "c")], axis=2)
    keyval = keyval.reshape(seqs, seq_len, 2 * KVH * HD)
    posk, posq = key_pos[:, None], local_pos[None, :]
    attended, lse = attend(seq_lengths, qkv, keyval, posk, posq)
    middle, tok_a, tok_b, gates = route(
        attended, output_full, x, moe_scale, router_full, hit.astype(F32)
    )

    grad_out = cotangent.reshape(rows, width) * live[:, None].astype(BF16)
    extra = jnp.pad(slots, ((0, 0), (0, width - rows)))
    cot_b = jnp.concatenate([grad_out[half:], extra], axis=0)
    cot_a, cot_b, _ = lax.optimization_barrier((grad_out[:half], cot_b, qkv))

    def to_group(part_a, part_b):
        near_a, near_b = gather_group(part_a, True), gather_group(part_b, False)
        return (near_a, near_b), (swap(near_a, "c"), swap(near_b, "c"))

    cot_near, cot_far = to_group(cot_a, cot_b)
    tok_near, tok_far = to_group(tok_a, tok_b)

    number = jnp.arange(local, dtype=jnp.int32)
    per_core = local // 2
    ids = ((top ^ (number // per_core)) * n_low + low) * local + core * per_core + number % per_core
    step = functools.partial(experts_step, ids, cap)
    *saved, mix_near, back_near = step(0, *tok_near, *cot_near, win, wout, ())
    *saved, mix_far, back_far = step(1, *tok_far, *cot_far, win, wout, saved)
    picked, active, grad_both, grad_produced = (
        s.reshape(local, 2 * n_low * cap, s.shape[-1]) for s in saved
    )

    def from_group(near, far):
        total = add_low(near, swap(far, "c"))
        return reduce_group(total[:, :half], True), reduce_group(total[:, half:], False)

    back_a, back_b = from_group(back_near, back_far)
    mix_near, mix_far, _ = lax.optimization_barrier((mix_near, mix_far, back_a))
    mix_a, mix_b = from_group(mix_near, mix_far)
    output = (middle + jnp.concatenate([mix_a, mix_b], axis=0).astype(F32)).astype(BF16)

    grad_expert_out = jnp.einsum(
        "erf,erd->efd", active, grad_produced, preferred_element_type=F32
    ).astype(BF16)
    grad_expert_in = jnp.einsum(
        "erd,erf->edf", picked, grad_both, preferred_element_type=F32
    ).astype(BF16)
    expert_out_sum = reduce_expert(grad_expert_out, local)
    expert_in_sum = reduce_expert(grad_expert_in, local)

    grad_middle, branch, grad_attended, router_grad, moe_gain_grad = unroute(
        back_a, back_b, gates, middle, moe_scale, router_full, grad_out, output_full
    )
    grad_output_weight = jnp.dot(attended.T, branch, preferred_element_type=F32).astype(BF16)
    output_sum = reduce_weight(grad_output_weight)
    dq, dkv = attend_back(
        seq_lengths, qkv, keyval, posk, posq, grad_attended, attended, lse, cosine, sine
    )
    grad_query_weight = jnp.dot(hidden.T, dq, preferred_element_type=F32).astype(BF16)
    query_sum = reduce_weight(grad_query_weight)
    dkv = dkv.reshape(2, seqs, n_high, 2, block_len, KVH * HD)
    dkv = add_low(dkv[:, :, :, 0], swap(dkv[:, :, :, 1], "c"))
    for bit in reversed(bits_of("h")):
        count = dkv.shape[2] // 2
        dkv = add_low(dkv[:, :, :count], swap(dkv[:, :, count:], "h", bit))
    dkv = dkv.reshape(2, rows, KVH * HD)
    grad_input, dkv_raw, attn_gain_grad = unproject(
        x, attn_scale, grad_middle, dq, dkv, qkv_full, cosine_rows, sine_rows
    )
    grad_keyval_weight = jnp.dot(hidden.T, dkv_raw, preferred_element_type=F32).astype(BF16)
    small_grad = jnp.concatenate([attn_gain_grad, moe_gain_grad, router_grad], axis=0)
    small_grad = jnp.pad(small_grad, ((0, HD - small_grad.shape[0]), (0, 0))).astype(BF16).T
    last_sum = reduce_weight(jnp.concatenate([grad_keyval_weight, small_grad], axis=1))
    n_kv = keyval_weight.shape[1]
    shape = (seqs, block_len, width)
    return (
        output.reshape(shape),
        grad_input.reshape(shape),
        last_sum[:, n_kv],
        query_sum,
        last_sum[:, :n_kv],
        output_sum,
        last_sum[:, n_kv + 1],
        last_sum[:, n_kv + 2 : n_kv + 2 + experts],
        expert_in_sum,
        expert_out_sum,
    )


def solution(mesh):
    ctx, shard = mesh.shape["ctx"], mesh.shape["shard"]
    cut = Mesh(mesh.devices.reshape(ctx // 2, 2, 2, shard // 2), ("h", "c", "t", "l"))
    c, s = ("h", "c"), ("t", "l")
    placed = (
        P(s, c, None),
        P(s, c, None),
        P(s),
        P(s, c, None),
        P(s, c),
        P(),
        P(s),
        P(s, None),
        P(s, None),
        P(s, None),
        P(s),
        P(s, None),
        P(s, c, None),
        P(s, c, None),
    )
    return jax.shard_map(
        per_device,
        mesh=cut,
        in_specs=placed,
        out_specs=(
            P(s, c, None),
            P(s, c, None),
            P(s),
            P(s, None),
            P(s, None),
            P(s, None),
            P(s),
            P(s, None),
            P(s, c, None),
            P(s, c, None),
        ),
        check_vma=False,
    )
```

time: 1830 us -> 985 us (0.54)
  waiting for transfers between devices: 1040 us -> 529 us
  local copies, waits for them, and re-layouts: 290 us -> 84.3 us
  matrix products: 233 us -> 36 us
  Pallas kernels: 0 us -> 191 us
  blocking collectives: 80.7 us -> 0 us
  other arithmetic: 132 us -> 89.6 us
    all_to_all x4 -> x0, waiting for transfers between devices: 575 us -> none  [the longest x1 164 us: per_device(): lax.all_to_all(outgoing, 'shard', split_axis=0, concat_axis=2, tiled=True)]
    ppermute x0 -> x58, waiting for transfers between devices: none -> 474 us  [swap(): return lax.ppermute(value, axis, [(i, i ^ bit) for i in range(size)])]
    reduce_scatter x6 -> x0, waiting for transfers between devices: 329 us -> none  [the longest x1 99.6 us: per_device(): lax.psum_scatter(grad_query_w.astype(jnp.bfloat16), 'shard', scatter_dime...]
    dot_general x46 -> x5, matrix products: 221 us -> 25.9 us  [the longest x1 17.3 us: per_device(): jnp.einsum('erd,erf->edf', picked, grad_both, preferred_element_type=F32)]
    pallas_call x0 -> x8, Pallas kernels: none -> 191 us  [the longest x2 96.1 us: experts_step(): pl.pallas_call(functools.partial(expert_kernel, cap), grid_spec=pltpu.Pre...]
    reduce_sum x13 -> x0, other arithmetic: 75.4 us -> none  [the longest x1 32.7 us: per_device(): jnp.sum(kept_float[..., None] * grad_returned[target].reshape(token_count...]
    gather x4 -> x0, local copies, waits for them, and re-layouts: 64.8 us -> none  [the longest x1 20 us: per_device(): grad_padded[source].reshape(shard_size, expert_local, capacity, width)]
    reshape x3 -> x0, local copies, waits for them, and re-layouts: 60.1 us -> none  [the longest x1 43.7 us: per_device(): produced.reshape(1, expert_local, shard_size * capacity, width)]
  transfers between devices with their start and end apart: 18 -> 60, of which waited for: 15 -> 28; matrix products, arithmetic and copies ran while one was open for 20% -> 18% of each run, Pallas kernels for 0% -> 14%
where the time goes in v1:
time: 985 us; the launch traced here: 981 us
  waiting for transfers between devices  529 us (54%)
  Pallas kernels  191 us (19%)
  other arithmetic  89.6 us (9%)
  local copies, waits for them, and re-layouts  84.3 us (9%)
  matrix products  36 us (4%)
  starting transfers between devices  35.4 us (4%)
  between operations  15.3 us (2%)
    ppermute x58, waiting for transfers between devices, swap(): return lax.ppermute(value, axis, [(i, i ^ bit) for i in range(size)])  474 us
    pallas_call x2, Pallas kernels, experts_step(): pl.pallas_call(functools.partial(expert_kernel, cap), grid_spec=pltpu.Pre...  96.1 us
    all_gather x2, waiting for transfers between devices, gather_weight(): return lax.all_gather(own, ('t', 'l', 'c'), axis=0, tiled=True)  54.9 us
    convert_element_type x27, other arithmetic, add_low(): return (a.astype(F32) + b.astype(F32)).astype(BF16)  45.5 us
    ppermute x58, starting transfers between devices, swap(): return lax.ppermute(value, axis, [(i, i ^ bit) for i in range(size)])  35.4 us
    pallas_call x1, Pallas kernels, attend_back(): pl.pallas_call(attend_back_kernel, grid_spec=pltpu.PrefetchScalarGridSpec...  29.3 us
    pallas_call x1, Pallas kernels, attend(): pl.pallas_call(attend_kernel, grid_spec=pltpu.PrefetchScalarGridSpec(num_...  25.6 us
  transfers between devices with their start and end apart: 60, of which 28 were waited for; matrix products, arithmetic and copies ran while one was open for 18% of the time, Pallas kernels for 14%

profile of v1, /device:TPU:0, one launch (start us, length us, event | category | flops | bytes accessed | tf_op | source)
XLA Modules:
  0.0 980.9 jit_solution(17933521318645251560)
XLA Ops:
  23.7 54.9 %all-gather.5.cloned.1.call-done = bf16[1,1536,2176]{2,1,0:T(8,128)(2,1)} async-done(((bf16[1,96,2176]{2,1,0:T(8,128)(2,1)}), bf16[1,1536,2176]{2,1,0:T(8,128)(2,1)}) %all-gather.5.cloned.1.call-update) | async-done | bytes 6684688 | tf_op jit(solution)/shard_map/all_gather | solution.py:656
  127.7 13.2 %collective-permute-done.15 = bf16[1,2,192,1536]{3,2,1,0:T(8,128)(2,1)S(1)} collective-permute-done((bf16[1,2,192,1536]{3,2,1,0:T(8,128)(2,1)}, bf16[1,2,192,1536]{3,2,1,0:T(8,128)(2,1)S(1)}, u32[]{:S(2)}, u32[]{:S(2)}) %collective-permute-start.15) | collective-permute-done | bytes 1179680 | tf_op jit(solution)/shard_map/ppermute | solution.py:51
  147.6 31.8 %collective-permute-done.16 = bf16[1,2,192,1536]{3,2,1,0:T(8,128)(2,1)} collective-permute-done((bf16[1,2,192,1536]{3,2,1,0:T(8,128)(2,1)}, bf16[1,2,192,1536]{3,2,1,0:T(8,128)(2,1)}, u32[]{:S(2)}, u32[]{:S(2)}) %collective-permute-start.16) | collective-permute-done | bytes 1179680 | tf_op jit(solution)/shard_map/ppermute | solution.py:51
  183.8 25.6 %attend.1 = (bf16[512,1536]{1,0:T(8,128)(2,1)}, f32[2,12,1,256]{3,2,1,0:T(1,128)}) custom-call(s32[2]{0:T(128)} %len_ref.3, bf16[512,2048]{1,0:T(8,128)(2,1)} %get-tuple-element.44.q_ref, bf16[2,1024,512]{2,1,0:T(8,128)(2,1)} %bitcast.272, bf16[2,1024,512]{2,1,0:T(8,128)(2,1)} %bitcast.273, s32[1024,1]{1,0:T(8,128)} %fusion.35.posk_ref, ...), custom_call_target="tpu_custom_call" | custom-call | flops 3221225472 | bytes 7340032 | tf_op jit(solution)/shard_map/attend/pallas_call | solution.py:249
  224.3 14.3 %collective-permute-done.2 = bf16[1,1,256,1536]{3,2,1,0:T(8,128)(2,1)S(1)} collective-permute-done((bf16[1,1,256,1536]{3,2,1,0:T(8,128)(2,1)}, bf16[1,1,256,1536]{3,2,1,0:T(8,128)(2,1)S(1)}, u32[]{:S(2)}, u32[]{:S(2)}) %collective-permute-start.2) | collective-permute-done | bytes 786464 | tf_op jit(solution)/shard_map/ppermute | solution.py:51
  239.1 50.8 %collective-permute-done.4 = bf16[1,1,272,1536]{3,2,1,0:T(8,128)(2,1)S(1)} collective-permute-done((bf16[1,1,272,1536]{3,2,1,0:T(8,128)(2,1)}, bf16[1,1,272,1536]{3,2,1,0:T(8,128)(2,1)S(1)}, u32[]{:S(2)}, u32[]{:S(2)}) %collective-permute-start.4) | collective-permute-done | bytes 835616 | tf_op jit(solution)/shard_map/ppermute | solution.py:51
  298.3 25.3 %collective-permute-done.7 = bf16[1,2,256,1536]{3,2,1,0:T(8,128)(2,1)S(1)} collective-permute-done((bf16[1,2,256,1536]{3,2,1,0:T(8,128)(2,1)S(1)}, bf16[1,2,256,1536]{3,2,1,0:T(8,128)(2,1)S(1)}, u32[]{:S(2)}, u32[]{:S(2)}) %collective-permute-start.7) | collective-permute-done | bytes 1572896 | tf_op jit(solution)/shard_map/ppermute | solution.py:51
  332.5 23.5 %collective-permute-done.3 = bf16[1,2,256,1536]{3,2,1,0:T(8,128)(2,1)S(1)} collective-permute-done((bf16[1,2,256,1536]{3,2,1,0:T(8,128)(2,1)S(1)}, bf16[1,2,256,1536]{3,2,1,0:T(8,128)(2,1)S(1)}, u32[]{:S(2)}, u32[]{:S(2)}) %collective-permute-start.3) | collective-permute-done | bytes 1572896 | tf_op jit(solution)/shard_map/ppermute | solution.py:51
  368.1 42.6 %experts.2 = (bf16[2,2,4,160,1536]{4,3,2,1,0:T(8,128)(2,1)}, bf16[2,2,4,160,768]{4,3,2,1,0:T(8,128)(2,1)}, bf16[2,2,4,160,1536]{4,3,2,1,0:T(8,128)(2,1)}, bf16[2...) custom-call(s32[2]{0:T(128)} %multiply_add_fusion.ids_ref, ...), custom_call_target="tpu_custom_call" | custom-call | flops 26172456960 | bytes 69206016 | tf_op jit(solution)/shard_map/experts/pallas_call | solution.py:486
  410.8 53.5 %experts.3 = (bf16[2,2,4,160,1536]{4,3,2,1,0:T(8,128)(2,1)}, bf16[2,2,4,160,768]{4,3,2,1,0:T(8,128)(2,1)}, bf16[2,2,4,160,1536]{4,3,2,1,0:T(8,128)(2,1)}, bf16[2...) custom-call(s32[2]{0:T(128)} %multiply_add_fusion.ids_ref, ...), custom_call_target="tpu_custom_call", output_to_operand_aliasing={{0}: (7, {}), {1}: (8, {}), {2}: (9, {}), {3}: (10, {})} | custom-call | flops 26172456960 | bytes 69206016 | tf_op jit(solution)/shard_map/experts/pallas_call | solution.py:486
  476.6 17.3 %convolution_convert_fusion = bf16[2,1536,1536]{2,1,0:T(8,128)(2,1)S(1)} fusion(bf16[2,1280,1536]{2,1,0:T(8,128)(2,1)} %bitcast.295, bf16[2,1280,1536]{2,1,0:T(8,128)(2,1)} %bitcast.296), kind=kOutput, calls=%fused_computation.2 | convolution fusion | flops 12084314112 | bytes 25165824 | tf_op jit(solution)/shard_map/erd,erf->edf/dot_general | solution.py:745
  502.1 28.7 %collective-permute-done.55 = bf16[2,1,1,2,192,1536]{5,4,3,2,0,1:T(8,128)(2,1)} collective-permute-done((bf16[2,1,1,2,192,1536]{5,4,3,2,0,1:T(8,128)(2,1)S(1)}, bf16[2,1,1,2,192,1536]{5,4,3,2,0,1:T(8,128)(2,1)}, u32[]{:S(2)}, u32[]{:S(2)}) %collective-permute-start.55) | collective-permute-done | bytes 2359328 | tf_op jit(solution)/shard_map/ppermute | solution.py:51
  534.2 50.3 %collective-permute-done.56 = bf16[1,2,192,1536]{3,2,1,0:T(8,128)(2,1)} collective-permute-done((bf16[1,2,192,1536]{3,2,1,0:T(8,128)(2,1)}, bf16[1,2,192,1536]{3,2,1,0:T(8,128)(2,1)}, u32[]{:S(2)}, u32[]{:S(2)}) %collective-permute-start.56) | collective-permute-done | bytes 1179680 | tf_op jit(solution)/shard_map/ppermute | solution.py:51
  603.1 27.1 %collective-permute-done.52 = bf16[2,1,1,2,384,1536]{5,4,3,2,0,1:T(8,128)(2,1)} collective-permute-done((bf16[2,1,1,2,384,1536]{5,4,3,2,0,1:T(8,128)(2,1)}, bf16[2,1,1,2,384,1536]{5,4,3,2,0,1:T(8,128)(2,1)}, u32[]{:S(2)}, u32[]{:S(2)}) %collective-permute-start.52) | collective-permute-done | bytes 4718624 | tf_op jit(solution)/shard_map/ppermute | solution.py:51
  643.8 26.2 %collective-permute-done.24 = bf16[1,1,256,1536]{3,2,1,0:T(8,128)(2,1)S(1)} collective-permute-done((bf16[1,1,256,1536]{3,2,1,0:T(8,128)(2,1)S(1)}, bf16[1,1,256,1536]{3,2,1,0:T(8,128)(2,1)S(1)}, u32[]{:S(2)}, u32[]{:S(2)}) %collective-permute-start.24) | collective-permute-done | bytes 786464 | tf_op jit(solution)/shard_map/ppermute | solution.py:51
  672.1 12.9 %unroute.1 = (f32[512,1536]{1,0:T(8,128)}, bf16[512,1536]{1,0:T(8,128)(2,1)}, bf16[512,1536]{1,0:T(8,128)(2,1)}, f32[16,1536]{1,0:T(8,128)}, f32[1,1536]{1,0:T(1,128)}) custom-call(bf16[256,1536]{1,0:T(8,128)(2,1)} %fusion.24.first_ref, bf16[272,1536]{1,0:T(8,128)(2,1)} %fusion.23.second_ref, f32[16,512]{1,0:T(8,128)} %get-tuple-element.61.gates_ref, ...), custom_call_target="tpu_custom_call" | custom-call | flops 2617245696 | bytes 17301504 | tf_op jit(solution)/shard_map/unroute/pallas_call | solution.py:555
  685.0 29.3 %attend_back.1 = (bf16[512,1536]{1,0:T(8,128)(2,1)}, bf16[2,2,1024,256]{3,2,1,0:T(8,128)(2,1)}) custom-call(s32[2]{0:T(128)} %len_ref.3, bf16[512,2048]{1,0:T(8,128)(2,1)} %get-tuple-element.44.q_ref, bf16[2,1024,512]{2,1,0:T(8,128)(2,1)} %bitcast.274, bf16[2,1024,512]{2,1,0:T(8,128)(2,1)} %bitcast.275, s32[1024,1]{1,0:T(8,128)} %fusion.35.posk_ref, ...), custom_call_target="tpu_custom_call" | custom-call | flops 8053063680 | bytes 10485760 | tf_op jit(solution)/shard_map/attend_back/pallas_call | solution.py:317
  716.2 29.8 %collective-permute-done.53 = bf16[1,2,384,1536]{3,2,1,0:T(8,128)(2,1)S(1)} collective-permute-done((bf16[1,2,384,1536]{3,2,1,0:T(8,128)(2,1)}, bf16[1,2,384,1536]{3,2,1,0:T(8,128)(2,1)S(1)}, u32[]{:S(2)}, u32[]{:S(2)}) %collective-permute-start.53) | collective-permute-done | bytes 2359328 | tf_op jit(solution)/shard_map/ppermute | solution.py:51
  802.9 32.6 %collective-permute-done.35 = bf16[2,2,96,640]{3,2,1,0:T(8,128)(2,1)S(1)} collective-permute-done((bf16[2,2,96,640]{3,2,1,0:T(8,128)(2,1)S(1)}, bf16[2,2,96,640]{3,2,1,0:T(8,128)(2,1)S(1)}, u32[]{:S(2)}, u32[]{:S(2)}) %collective-permute-start.35) | collective-permute-done | bytes 491552 | tf_op jit(solution)/shard_map/ppermute | solution.py:51
  851.9 11.6 %collective-permute-done.41 = bf16[2,2,96,1536]{3,2,1,0:T(8,128)(2,1)S(1)} collective-permute-done((bf16[2,2,96,1536]{3,2,1,0:T(8,128)(2,1)S(1)}, bf16[2,2,96,1536]{3,2,1,0:T(8,128)(2,1)S(1)}, u32[]{:S(2)}, u32[]{:S(2)}) %collective-permute-start.41) | collective-permute-done | bytes 1179680 | tf_op jit(solution)/shard_map/ppermute | solution.py:51
  871.2 15.9 %collective-permute-done.42 = bf16[2,1,96,1536]{3,2,1,0:T(8,128)(2,1)} collective-permute-done((bf16[2,1,96,1536]{3,2,1,0:T(8,128)(2,1)}, bf16[2,1,96,1536]{3,2,1,0:T(8,128)(2,1)}, u32[]{:S(2)}, u32[]{:S(2)}) %collective-permute-start.42) | collective-permute-done | bytes 589856 | tf_op jit(solution)/shard_map/ppermute | solution.py:51
  889.1 14.5 %collective-permute-done.43 = bf16[96,1536]{1,0:T(8,128)(2,1)S(1)} collective-permute-done((bf16[96,1536]{1,0:T(8,128)(2,1)S(1)}, bf16[96,1536]{1,0:T(8,128)(2,1)S(1)}, u32[]{:S(2)}, u32[]{:S(2)}) %collective-permute-start.43) | collective-permute-done | bytes 294944 | tf_op jit(solution)/shard_map/ppermute | solution.py:51
  920.3 31.5 %collective-permute-done.26 = bf16[2,1,256,1536]{3,2,1,0:T(8,128)(2,1)S(1)} collective-permute-done((bf16[2,1,256,1536]{3,2,1,0:T(8,128)(2,1)S(1)}, bf16[2,1,256,1536]{3,2,1,0:T(8,128)(2,1)S(1)}, u32[]{:S(2)}, u32[]{:S(2)}) %collective-permute-start.26) | collective-permute-done | bytes 1572896 | tf_op jit(solution)/shard_map/ppermute | solution.py:51
  956.4 14.2 %collective-permute-done.27 = bf16[1,1,256,1536]{3,2,1,0:T(8,128)(2,1)S(1)} collective-permute-done((bf16[1,1,256,1536]{3,2,1,0:T(8,128)(2,1)S(1)}, bf16[1,1,256,1536]{3,2,1,0:T(8,128)(2,1)S(1)}, u32[]{:S(2)}, u32[]{:S(2)}) %collective-permute-start.27) | collective-permute-done | bytes 786464 | tf_op jit(solution)/shard_map/ppermute | solution.py:51
  (339 shorter events, 288.1 us)
Async XLA Ops:
  7.2 71.5 %all-gather.5.cloned.1.call-start = ((), (), s32[]{:S(2)}) async-start(), calls=%async_computation | async-start | bytes 7102464 | tf_op jit(solution)/shard_map/all_gather | solution.py:656
  11.7 197.7 %all-gather.7.cloned.1.call-start = ((), (), s32[]{:S(2)}) async-start(), calls=%async_computation.1 | async-start | bytes 5013504 | tf_op jit(solution)/shard_map/all_gather | solution.py:656
  14.4 102.4 %collective-permute-start.10 = (bf16[1,384,1536]{2,1,0:T(8,128)(2,1)}, bf16[1,384,1536]{2,1,0:T(8,128)(2,1)S(1)}, u32[]{:S(2)}, u32[]{:S(2)}) collective-permute-start(bf16[1,384,1536]{2,1,0:T(8,128)(2,1)} %get-tuple-element.135), channel_id=1, source_target_pairs={{0,8},{8,0},{1,9},{9,1},{2,10},{10,2},{3,11},{11,3},{4,12},{12,4},... | collective-permute-start | bytes 3538952 | tf_op jit(solution)/shard_map/ppermute | solution.py:51
  16.2 86.1 %collective-permute-start.14 = (bf16[1,192,1536]{2,1,0:T(8,128)(2,1)}, bf16[1,192,1536]{2,1,0:T(8,128)(2,1)}, u32[]{:S(2)}, u32[]{:S(2)}) collective-permute-start(bf16[1,192,1536]{2,1,0:T(8,128)(2,1)} %get-tuple-element.144), channel_id=1, source_target_pairs={{0,8},{8,0},{1,9},{9,1},{2,10},{10,2},{3,11},{11,3},{4,12},{12,4},... | collective-permute-start | bytes 1769480 | tf_op jit(solution)/shard_map/ppermute | solution.py:51
  106.3 73.1 %collective-permute-start.16 = (bf16[1,2,192,1536]{3,2,1,0:T(8,128)(2,1)}, bf16[1,2,192,1536]{3,2,1,0:T(8,128)(2,1)}, u32[]{:S(2)}, u32[]{:S(2)}) collective-permute-start(bf16[1,2,192,1536]{3,2,1,0:T(8,128)(2,1)} %maximum_select_fusion.4), channel_id=1, source_target_pairs={{0,4},{4,0},{1,5},{5,1},{2,6},{6,2},{3,7},{7,3},{8,12},{12,8},{9,1... | collective-permute-start | bytes 3538952 | tf_op jit(solution)/shard_map/ppermute | solution.py:51
  116.8 62.6 %collective-permute-start.1 = (bf16[2,2,1,256,512]{4,3,2,1,0:T(8,128)(2,1)}, bf16[2,2,1,256,512]{4,3,2,1,0:T(8,128)(2,1)}, u32[]{:S(2)}, u32[]{:S(2)}) collective-permute-start(bf16[2,2,1,256,512]{4,3,2,1,0:T(8,128)(2,1)} %pad_maximum_fusion.10), channel_id=1, source_target_pairs={{0,8},{8,0},{1,9},{9,1},{2,10},{10,2},{3,11},{11,3},{4,12},{12,4},... | collective-permute-start | bytes 3145736 | tf_op jit(solution)/shard_map/ppermute | solution.py:51
  118.6 172.2 %collective-permute-start.11 = (bf16[1,2,384,1536]{3,2,1,0:T(8,128)(2,1)}, bf16[1,2,384,1536]{3,2,1,0:T(8,128)(2,1)}, u32[]{:S(2)}, u32[]{:S(2)}) collective-permute-start(bf16[1,2,384,1536]{3,2,1,0:T(8,128)(2,1)} %maximum_select_fusion.1), channel_id=1, source_target_pairs={{0,16},{16,0},{1,17},{17,1},{2,18},{18,2},{3,19},{19,3},{4,20},{20... | collective-permute-start | bytes 7077896 | tf_op jit(solution)/shard_map/ppermute | solution.py:51
  126.3 93.4 %collective-permute-start.8 = (bf16[1,1,272,1536]{3,2,1,0:T(8,128)(2,1)S(1)}, bf16[1,1,272,1536]{3,2,1,0:T(8,128)(2,1)}, u32[]{:S(2)}, u32[]{:S(2)}) collective-permute-start(bf16[1,1,272,1536]{3,2,1,0:T(8,128)(2,1)S(1)} %bitcast.239), channel_id=1, source_target_pairs={{0,2},{1,3},{2,0},{3,1},{4,6},{5,7},{6,4},{7,5},{8,10},{9,11},{10,... | collective-permute-start | bytes 2506760 | tf_op jit(solution)/shard_map/ppermute | solution.py:51
  140.9 76.6 %collective-permute-start.6 = (bf16[1,1,256,1536]{3,2,1,0:T(8,128)(2,1)S(1)}, bf16[1,1,256,1536]{3,2,1,0:T(8,128)(2,1)S(1)}, u32[]{:S(2)}, u32[]{:S(2)}) collective-permute-start(bf16[1,1,256,1536]{3,2,1,0:T(8,128)(2,1)S(1)} %bitcast.242), channel_id=1, source_target_pairs={{0,1},{1,0},{2,3},{3,2},{4,5},{5,4},{6,7},{7,6},{8,9},{9,8},{10,11... | collective-permute-start | bytes 2359304 | tf_op jit(solution)/shard_map/ppermute | solution.py:51
  179.4 115.1 %collective-permute-start.12 = (bf16[1,2,384,1536]{3,2,1,0:T(8,128)(2,1)}, bf16[1,2,384,1536]{3,2,1,0:T(8,128)(2,1)}, u32[]{:S(2)}, u32[]{:S(2)}) collective-permute-start(bf16[1,2,384,1536]{3,2,1,0:T(8,128)(2,1)} %maximum_select_fusion.1), channel_id=1, source_target_pairs={{0,4},{4,0},{1,5},{5,1},{2,6},{6,2},{3,7},{7,3},{8,12},{12,8},{9,1... | collective-permute-start | bytes 7077896 | tf_op jit(solution)/shard_map/ppermute | solution.py:51
  179.4 111.3 %collective-permute-start.17 = (bf16[1,2,192,1536]{3,2,1,0:T(8,128)(2,1)}, bf16[1,2,192,1536]{3,2,1,0:T(8,128)(2,1)}, u32[]{:S(2)}, u32[]{:S(2)}) collective-permute-start(bf16[1,2,192,1536]{3,2,1,0:T(8,128)(2,1)} %collective-permute-done.16), channel_id=1, source_target_pairs={{0,16},{16,0},{1,17},{17,1},{2,18},{18,2},{3,19},{19,3},{4,20},{20... | collective-permute-start | bytes 3538952 | tf_op jit(solution)/shard_map/ppermute | solution.py:51
  217.5 72.3 %collective-permute-start.4 = (bf16[1,1,272,1536]{3,2,1,0:T(8,128)(2,1)}, bf16[1,1,272,1536]{3,2,1,0:T(8,128)(2,1)S(1)}, u32[]{:S(2)}, u32[]{:S(2)}) collective-permute-start(bf16[1,1,272,1536]{3,2,1,0:T(8,128)(2,1)} %bitcast.264), channel_id=1, source_target_pairs={{0,2},{1,3},{2,0},{3,1},{4,6},{5,7},{6,4},{7,5},{8,10},{9,11},{10,... | collective-permute-start | bytes 2506760 | tf_op jit(solution)/shard_map/ppermute | solution.py:51
  238.5 85.0 %collective-permute-start.7 = (bf16[1,2,256,1536]{3,2,1,0:T(8,128)(2,1)S(1)}, bf16[1,2,256,1536]{3,2,1,0:T(8,128)(2,1)S(1)}, u32[]{:S(2)}, u32[]{:S(2)}) collective-permute-start(bf16[1,2,256,1536]{3,2,1,0:T(8,128)(2,1)S(1)} %pad_maximum_fusion.9), channel_id=1, source_target_pairs={{0,2},{1,3},{2,0},{3,1},{4,6},{5,7},{6,4},{7,5},{8,10},{9,11},{10,... | collective-permute-start | bytes 4718600 | tf_op jit(solution)/shard_map/ppermute | solution.py:51
  290.7 65.3 %collective-permute-start.3 = (bf16[1,2,256,1536]{3,2,1,0:T(8,128)(2,1)S(1)}, bf16[1,2,256,1536]{3,2,1,0:T(8,128)(2,1)S(1)}, u32[]{:S(2)}, u32[]{:S(2)}) collective-permute-start(bf16[1,2,256,1536]{3,2,1,0:T(8,128)(2,1)S(1)} %pad_maximum_fusion.8), channel_id=1, source_target_pairs={{0,2},{1,3},{2,0},{3,1},{4,6},{5,7},{6,4},{7,5},{8,10},{9,11},{10,... | collective-permute-start | bytes 4718600 | tf_op jit(solution)/shard_map/ppermute | solution.py:51
  290.8 70.9 %collective-permute-start.5 = (bf16[2,1,272,1536]{3,2,1,0:T(8,128)(2,1)S(1)}, bf16[2,1,272,1536]{3,2,1,0:T(8,128)(2,1)S(1)}, u32[]{:S(2)}, u32[]{:S(2)}) collective-permute-start(bf16[2,1,272,1536]{3,2,1,0:T(8,128)(2,1)S(1)} %pad_maximum_fusion.6), channel_id=1, source_target_pairs={{0,1},{1,0},{2,3},{3,2},{4,5},{5,4},{6,7},{7,6},{8,9},{9,8},{10,11... | collective-permute-start | bytes 5013512 | tf_op jit(solution)/shard_map/ppermute | solution.py:51
  294.5 72.0 %collective-permute-start.13 = (bf16[1,2,384,1536]{3,2,1,0:T(8,128)(2,1)}, bf16[1,2,384,1536]{3,2,1,0:T(8,128)(2,1)S(1)}, u32[]{:S(2)}, u32[]{:S(2)}) collective-permute-start(bf16[1,2,384,1536]{3,2,1,0:T(8,128)(2,1)} %collective-permute-done.12), channel_id=1, source_target_pairs={{0,16},{16,0},{1,17},{17,1},{2,18},{18,2},{3,19},{19,3},{4,20},{20... | collective-permute-start | bytes 7077896 | tf_op jit(solution)/shard_map/ppermute | solution.py:51
  325.6 85.1 %collective-permute-start.20 = (bf16[4,256,1536]{2,1,0:T(8,128)(2,1)}, bf16[4,256,1536]{2,1,0:T(8,128)(2,1)}, u32[]{:S(2)}, u32[]{:S(2)}) collective-permute-start(bf16[4,256,1536]{2,1,0:T(8,128)(2,1)} %bitcast.22.cot_a), channel_id=1, source_target_pairs={{0,8},{8,0},{1,9},{9,1},{2,10},{10,2},{3,11},{11,3},{4,12},{12,4},... | collective-permute-start | bytes 9437192 | tf_op jit(solution)/shard_map/ppermute | solution.py:51
  332.5 78.3 %collective-permute-start.21 = (bf16[4,272,1536]{2,1,0:T(8,128)(2,1)}, bf16[4,272,1536]{2,1,0:T(8,128)(2,1)}, u32[]{:S(2)}, u32[]{:S(2)}) collective-permute-start(bf16[4,272,1536]{2,1,0:T(8,128)(2,1)} %bitcast.24.cot_b), channel_id=1, source_target_pairs={{0,8},{8,0},{1,9},{9,1},{2,10},{10,2},{3,11},{11,3},{4,12},{12,4},... | collective-permute-start | bytes 10027016 | tf_op jit(solution)/shard_map/ppermute | solution.py:51
  476.5 54.3 %collective-permute-start.55 = (bf16[2,1,1,2,192,1536]{5,4,3,2,0,1:T(8,128)(2,1)S(1)}, bf16[2,1,1,2,192,1536]{5,4,3,2,0,1:T(8,128)(2,1)}, u32[]{:S(2)}, u32[]{:S(2)}) collective-permute-start(bf16[2,1,1,2,192,1536]{5,4,3,2,0,1:T(8,128)(2,1)S(1)} %constant_dynamic-slice_fusion), channel_id=1, source_target_pairs={{0,16},{16,0},{1,17},{17,1},{2,18},{18,2},{3,19},{19,3},{4,20},{20... | collective-permute-start | bytes 7077896 | tf_op jit(solution)/shard_map/ppermute | solution.py:51
  476.6 109.6 %collective-permute-start.22 = (bf16[4,528,1536]{2,1,0:T(8,128)(2,1)}, bf16[4,528,1536]{2,1,0:T(8,128)(2,1)}, u32[]{:S(2)}, u32[]{:S(2)}) collective-permute-start(bf16[4,528,1536]{2,1,0:T(8,128)(2,1)} %get-tuple-element.58), channel_id=1, source_target_pairs={{0,8},{8,0},{1,9},{9,1},{2,10},{10,2},{3,11},{11,3},{4,12},{12,4},... | collective-permute-start | bytes 19464200 | tf_op jit(solution)/shard_map/ppermute | solution.py:51
  500.2 130.1 %collective-permute-start.52 = (bf16[2,1,1,2,384,1536]{5,4,3,2,0,1:T(8,128)(2,1)}, bf16[2,1,1,2,384,1536]{5,4,3,2,0,1:T(8,128)(2,1)}, u32[]{:S(2)}, u32[]{:S(2)}) collective-permute-start(bf16[2,1,1,2,384,1536]{5,4,3,2,0,1:T(8,128)(2,1)} %constant_dynamic-slice_fusion.1), channel_id=1, source_target_pairs={{0,16},{16,0},{1,17},{17,1},{2,18},{18,2},{3,19},{19,3},{4,20},{20... | collective-permute-start | bytes 14155784 | tf_op jit(solution)/shard_map/ppermute | solution.py:51
  642.0 104.0 %collective-permute-start.53 = (bf16[1,2,384,1536]{3,2,1,0:T(8,128)(2,1)}, bf16[1,2,384,1536]{3,2,1,0:T(8,128)(2,1)S(1)}, u32[]{:S(2)}, u32[]{:S(2)}) collective-permute-start(bf16[1,2,384,1536]{3,2,1,0:T(8,128)(2,1)} %slice_bitcast_fusion), channel_id=1, source_target_pairs={{0,4},{4,0},{1,5},{5,1},{2,6},{6,2},{3,7},{7,3},{8,12},{12,8},{9,1... | collective-permute-start | bytes 7077896 | tf_op jit(solution)/shard_map/ppermute | solution.py:51
  793.3 110.9 %collective-permute-start.25 = (bf16[4,512,1536]{2,1,0:T(8,128)(2,1)}, bf16[4,512,1536]{2,1,0:T(8,128)(2,1)}, u32[]{:S(2)}, u32[]{:S(2)}) collective-permute-start(bf16[4,512,1536]{2,1,0:T(8,128)(2,1)} %get-tuple-element.60), channel_id=1, source_target_pairs={{0,8},{8,0},{1,9},{9,1},{2,10},{10,2},{3,11},{11,3},{4,12},{12,4},... | collective-permute-start | bytes 18874376 | tf_op jit(solution)/shard_map/ppermute | solution.py:51
  796.6 54.9 %collective-permute-start.47 = (bf16[2,2,96,1536]{3,2,1,0:T(8,128)(2,1)S(1)}, bf16[2,2,96,1536]{3,2,1,0:T(8,128)(2,1)S(1)}, u32[]{:S(2)}, u32[]{:S(2)}) collective-permute-start(bf16[2,2,96,1536]{3,2,1,0:T(8,128)(2,1)S(1)} %dynamic-slice_bitcast_fusion.4), channel_id=1, source_target_pairs={{0,1},{1,0},{2,3},{3,2},{4,5},{5,4},{6,7},{7,6},{8,9},{9,8},{10,11... | collective-permute-start | bytes 3538952 | tf_op jit(solution)/shard_map/ppermute | solution.py:51
  (76 other events, 1341.6 us)
Sparse Core Ops, SparseCore 0:
  11.8 66.8 all-gather.4
  81.0 84.3 all-gather.6

commit v2 on v1

--- a/solution.py
+++ b/solution.py
@@ -22,6 +22,7 @@
 LOG2E = 1.4426950408889634
 SCALE = HD ** (-0.5)
 VMEM_LIMIT = 60 * 1024 * 1024
+SMALL = pl.CostEstimate(flops=1000, bytes_accessed=1000, transcendentals=0)
 F32 = jnp.float32
 BF16 = jnp.bfloat16
 
@@ -64,98 +65,115 @@
     return lax.dynamic_index_in_dim(value, index, axis, keepdims=False)
 
 
-def gather_group(part, low_first):
+def after(value, *others):
+    return lax.optimization_barrier((value,) + others)[0]
+
+
+def sync(*values):
+    return lax.optimization_barrier(values)
+
+
+def low_axes(value):
+    return value.reshape((2,) * len(bits_of("l")) + value.shape[1:])
+
+
+def open_low(part):
+    return part.reshape((1,) * len(bits_of("l")) + part.shape)
+
+
+def gather_bit(value, k):
     bits = bits_of("l")
-    count = len(bits)
-    value = part.reshape((1,) * count + part.shape)
-    order = range(count) if low_first else reversed(range(count))
-    for k in order:
-        value = jnp.concatenate([value, swap(value, "l", bits[k])], axis=count - 1 - k)
-    return value.reshape((1 << count,) + part.shape)
-
-
-def reduce_group(value, low_first):
+    return jnp.concatenate([value, swap(value, "l", bits[k])], axis=len(bits) - 1 - k)
+
+
+def total_of(*parts):
+    return sum(p.astype(F32) for p in parts).astype(BF16)
+
+
+def reduce_bit(parts, k):
     bits = bits_of("l")
-    count = len(bits)
-    order = list(range(count) if low_first else reversed(range(count)))
-    rest = value.shape[1:]
-    value = value.reshape((2,) * count + rest)
-    for k in order:
-        axis = count - 1 - k
-        keep = lax.slice_in_dim(value, 0, 1, axis=axis)
-        send = lax.slice_in_dim(value, 1, 2, axis=axis)
-        value = add_low(keep, swap(send, "l", bits[k]))
-    return value.reshape(rest)
-
-
-def gather_expert(weight):
-    local, rows, columns = weight.shape
-    half = local // 2
-    core, high = lax.axis_index("c"), lax.axis_index("h")
-    keep = lax.dynamic_slice_in_dim(weight, core * half, half, 0)
-    send = lax.dynamic_slice_in_dim(weight, (1 - core) * half, half, 0)
-    other = swap(send, "c")
-    pair = jnp.where(
-        core == 0, jnp.stack([keep, other], axis=1), jnp.stack([other, keep], axis=1)
-    )
-    pieces = [jnp.stack([pair])]
-    far = swap(pair, "t")
+    axis = len(bits) - 1 - k
+    send = total_of(*[lax.slice_in_dim(p, 1, 2, axis=axis) for p in parts])
+    keep = [lax.slice_in_dim(p, 0, 1, axis=axis) for p in parts]
+    return total_of(*keep, swap(send, "l", bits[k]))
+
+
+def by_core(own, other, axis):
+    return jnp.where(
+        lax.axis_index("c") == 0,
+        jnp.concatenate([own, other], axis=axis),
+        jnp.concatenate([other, own], axis=axis),
+    )
+
+
+def spread_high(piece):
+    pieces = [piece]
+    for bit in bits_of("h"):
+        pieces = pieces + [swap(p, "h", bit) for p in pieces]
+    return pieces
+
+
+def place_high(whole, far, pieces, first):
+    high = lax.axis_index("h")
+    for r, p in enumerate(pieces):
+        whole = lax.dynamic_update_slice(whole, p[None, :, None], (far, 0, high ^ r, 0, first, 0))
+    return whole
+
+
+def joined(whole):
+    return whole.reshape(whole.shape[0] * whole.shape[1], -1, whole.shape[-1])
+
+
+def scatter_expert(grad, per_core):
     n_high = lax.axis_size("h")
-    whole = jnp.zeros((2, half, n_high, 2, rows, columns), weight.dtype)
-    for t, piece in enumerate((pair, far)):
-        pieces = [piece]
-        for bit in bits_of("h"):
-            pieces = pieces + [swap(p, "h", bit) for p in pieces]
-        for r, p in enumerate(pieces):
-            whole = lax.dynamic_update_slice(
-                whole, p[None, :, None], (t, 0, high ^ r, 0, 0, 0)
-            )
-    return whole.reshape(2 * half, n_high * 2 * rows, columns)
-
-
-def reduce_expert(grad, local):
-    half = local // 2
-    core, high = lax.axis_index("c"), lax.axis_index("h")
-    n_high = lax.axis_size("h")
-    rows = grad.shape[1] // (2 * n_high)
-    value = grad.reshape(2, half, n_high, 2, rows, grad.shape[2])
-    width = n_high
-    for bit in reversed(bits_of("h")):
-        width //= 2
-        side = (high & bit) // bit
-        keep = lax.dynamic_slice_in_dim(value, side * width, width, 2)
-        send = lax.dynamic_slice_in_dim(value, (1 - side) * width, width, 2)
-        value = add_low(keep, swap(send, "h", bit))
-    value = value.reshape(2, half, 2, rows, grad.shape[2])
-    value = add_low(value[0], swap(value[1], "t"))
-    keep = pick(value, core, 1)
+    grad = grad.reshape(2, per_core, n_high, -1, grad.shape[-1])
+    grad = jnp.swapaxes(grad, 1, 2)
+    grad = grad.reshape((2 * n_high,) + grad.shape[2:])
+    total = lax.psum_scatter(grad, ("t", "h"), scatter_dimension=0, tiled=True)
+    return total.reshape(per_core, 2, -1, total.shape[-1])
+
+
+def reduce_core(value):
+    core = lax.axis_index("c")
     other = swap(pick(value, 1 - core, 1), "c")
-    return jnp.where(
-        core == 0, jnp.concatenate([keep, other]), jnp.concatenate([other, keep])
-    ).astype(F32)
-
-
-def reduce_weight(grad):
-    core = lax.axis_index("c")
-    low, top = lax.axis_index("l"), lax.axis_index("t")
-    n_low = lax.axis_size("l")
-    rows, columns = grad.shape[0] // (4 * n_low), grad.shape[1]
-    value = grad.reshape(2, n_low, 2, rows, columns)
-    value = add_low(pick(value, core, 2), swap(pick(value, 1 - core, 2), "c"))
-    count = n_low
+    return by_core(pick(value, core, 1), other, 0).astype(F32)
+
+
+def weight_core(grad):
+    core, n_low = lax.axis_index("c"), lax.axis_size("l")
+    value = grad.reshape(2, n_low, 2, -1, grad.shape[1])
+    return add_low(pick(value, core, 2), swap(pick(value, 1 - core, 2), "c"))
+
+
+def weight_low(value):
+    value = lax.all_to_all(value, "l", split_axis=1, concat_axis=1, tiled=True)
+    return jnp.sum(value.astype(F32), axis=1).astype(BF16)
+
+
+def weight_bits(value):
+    low = lax.axis_index("l")
+    count = lax.axis_size("l")
     for bit in bits_of("l"):
         count //= 2
-        value = value.reshape(2, count, 2, rows, columns)
+        value = value.reshape((2, count, 2) + value.shape[-2:])
         side = (low & bit) // bit
         value = add_low(pick(value, side, 2), swap(pick(value, 1 - side, 2), "l", bit))
-    value = value.reshape(2, rows, columns)
-    value = add_low(pick(value, top, 0), swap(pick(value, 1 - top, 0), "t"))
+    return value.reshape((2,) + value.shape[-2:])
+
+
+def weight_top(value):
+    top = lax.axis_index("t")
+    return add_low(pick(value, top, 0), swap(pick(value, 1 - top, 0), "t"))
+
+
+def weight_high(value):
     for bit in bits_of("h"):
         value = add_low(value, swap(value, "h", bit))
-    other = swap(value, "c")
-    return jnp.where(
-        core == 0, jnp.concatenate([value, other]), jnp.concatenate([other, value])
-    ).astype(F32)
+    return value
+
+
+def weight_done(value):
+    return by_core(value, swap(value, "c"), 0).astype(F32)
 
 
 def norm_back(grad_normed, gain, normed, inverse):
@@ -187,7 +205,7 @@
 
 def project(x, gain, weight, cosine, sine):
     rows, width = x.shape
-    columns = weight.shape[1]
+    columns = (H + 2 * KVH) * HD
     block = 512
     return pl.pallas_call(
         project_kernel,
@@ -208,11 +226,7 @@
             jax.ShapeDtypeStruct((rows, columns), BF16),
         ],
         compiler_params=params(),
-        cost_estimate=pl.CostEstimate(
-            flops=2 * rows * width * columns,
-            bytes_accessed=2 * (2 * rows * width + width * columns + rows * columns),
-            transcendentals=0,
-        ),
+        cost_estimate=SMALL,
         name="project",
     )(x, gain, weight, cosine, sine)
 
@@ -269,11 +283,7 @@
             jax.ShapeDtypeStruct((seqs, H, 1, rows), F32),
         ],
         compiler_params=params(),
-        cost_estimate=pl.CostEstimate(
-            flops=4 * seqs * H * rows * keys * HD,
-            bytes_accessed=4 * seqs * (rows * H * HD + keys * 2 * KVH * HD),
-            transcendentals=seqs * H * rows * keys,
-        ),
+        cost_estimate=SMALL,
         name="attend",
     )(lengths, qkv, keyval, keyval, posk, posq)
 
@@ -347,11 +357,7 @@
             jax.ShapeDtypeStruct((2, seqs, keys, KVH * HD), BF16),
         ],
         compiler_params=params(),
-        cost_estimate=pl.CostEstimate(
-            flops=10 * seqs * H * rows * keys * HD,
-            bytes_accessed=4 * seqs * (2 * rows * H * HD + keys * 2 * KVH * HD),
-            transcendentals=seqs * H * rows * keys,
-        ),
+        cost_estimate=SMALL,
         name="attend_back",
     )(lengths, qkv, keyval, keyval, posk, posq, grad, attended, lse, cosine, sine)
 
@@ -393,11 +399,7 @@
             jax.ShapeDtypeStruct((experts, rows), F32),
         ],
         compiler_params=params(),
-        cost_estimate=pl.CostEstimate(
-            flops=2 * rows * width * (width + HD),
-            bytes_accessed=2 * width * (width + 5 * rows),
-            transcendentals=experts * rows,
-        ),
+        cost_estimate=SMALL,
         name="route",
     )(attended, weight, x, gain, router, hit)
 
@@ -405,7 +407,7 @@
 def expert_kernel(
     cap, ids_ref, tok_a, tok_b, cot_a, cot_b, win_ref, wout_ref, *refs
 ):
-    x_ref, active_ref, both_ref, grad_ref, mix_ref, back_ref = refs[-6:]
+    x_ref, active_ref, both_ref, grad_ref, mix_ref, back_a, back_b = refs[-7:]
     number = pl.program_id(1)
     mine = ids_ref[number]
     half = tok_a.shape[1]
@@ -459,19 +461,20 @@
     @pl.when(number == 0)
     def _():
         mix_ref[...] = jnp.zeros_like(mix_ref)
-        back_ref[...] = jnp.zeros_like(back_ref)
+        back_a[...] = jnp.zeros_like(back_a)
+        back_b[...] = jnp.zeros_like(back_b)
 
     for g in range(2):
         part = slice(g * cap, (g + 1) * cap)
         mix_ref[g] = (mix_ref[g].astype(F32) + tn(spreads[g], weighed[part])).astype(BF16)
-        back_ref[g, :rows] = (
-            back_ref[g, :rows].astype(F32) + tn(spreads[g], grad_rows[part])
-        ).astype(BF16)
+        back = tn(spreads[g], grad_rows[part])
+        back_a[g] = (back_a[g].astype(F32) + back[:half]).astype(BF16)
+        back_b[g, :half] = (back_b[g, :half].astype(F32) + back[half:]).astype(BF16)
         dense = jnp.sum(jnp.where(hits[g], grad_gate[part], 0.0), axis=0, keepdims=True)
         coarse = dense.astype(BF16).astype(F32)
         fine = dense - coarse
-        back_ref[g, rows:, :rows] += jnp.where(row_is_mine, coarse, 0.0).astype(BF16)
-        back_ref[g, rows:, rows : 2 * rows] += jnp.where(row_is_mine, fine, 0.0).astype(BF16)
+        back_b[g, half:, :rows] += jnp.where(row_is_mine, coarse, 0.0).astype(BF16)
+        back_b[g, half:, rows : 2 * rows] += jnp.where(row_is_mine, fine, 0.0).astype(BF16)
 
 
 def experts_step(ids, cap, side, tok_a, tok_b, cot_a, cot_b, win, wout, earlier):
@@ -479,8 +482,11 @@
     experts = tok_b.shape[1] - half
     local = win.shape[0]
     tokens = lambda n: pl.BlockSpec((2, n, width), lambda i, j, ids: (i, 0, 0))
-    rows = lambda n: pl.BlockSpec((1, 1, 2, cap, n), lambda i, j, ids: (j, side, i, 0, 0))
+    rows = lambda n: pl.BlockSpec(
+        (1, 1, 2, cap, n), lambda i, j, ids: (ids[local + j], side, i, 0, 0)
+    )
     rows_shape = lambda n: jax.ShapeDtypeStruct((local, 2, n_low, cap, n), BF16)
+    weights = lambda w: pl.BlockSpec((1,) + w.shape[1:], lambda i, j, ids: (j, 0, 0))
     earlier = tuple(earlier)
     n_rows = local * n_low * cap
     return pl.pallas_call(
@@ -493,8 +499,8 @@
                 tokens(half + experts),
                 tokens(half),
                 tokens(half + experts),
-                pl.BlockSpec((1,) + win.shape[1:], lambda i, j, ids: (j, 0, 0)),
-                pl.BlockSpec((1,) + wout.shape[1:], lambda i, j, ids: (j, 0, 0)),
+                weights(win),
+                weights(wout),
             ]
             + [pl.BlockSpec(memory_space=pl.ANY)] * len(earlier),
             out_specs=[
@@ -503,7 +509,8 @@
                 rows(2 * FF),
                 rows(width),
                 tokens(2 * half),
-                tokens(2 * half + experts),
+                tokens(half),
+                tokens(half + experts),
             ],
         ),
         out_shape=[
@@ -512,15 +519,12 @@
             rows_shape(2 * FF),
             rows_shape(width),
             jax.ShapeDtypeStruct((n_low, 2 * half, width), BF16),
-            jax.ShapeDtypeStruct((n_low, 2 * half + experts, width), BF16),
+            jax.ShapeDtypeStruct((n_low, half, width), BF16),
+            jax.ShapeDtypeStruct((n_low, half + experts, width), BF16),
         ],
         input_output_aliases={7 + k: k for k in range(len(earlier))},
         compiler_params=params(),
-        cost_estimate=pl.CostEstimate(
-            flops=n_rows * (12 * width * FF + 16 * half * width),
-            bytes_accessed=2 * (n_low * half * width * 8 + n_rows * 4 * width + 6 * FF * width * local),
-            transcendentals=n_rows * FF,
-        ),
+        cost_estimate=SMALL,
         name="experts",
     )(ids, tok_a, tok_b, cot_a, cot_b, win, wout, *earlier)
 
@@ -562,11 +566,7 @@
             jax.ShapeDtypeStruct((1, width), F32),
         ],
         compiler_params=params(),
-        cost_estimate=pl.CostEstimate(
-            flops=2 * rows * width * (width + HD),
-            bytes_accessed=2 * width * (width + 8 * rows),
-            transcendentals=0,
-        ),
+        cost_estimate=SMALL,
         name="unroute",
     )(first, second, gates, middle, gain, router, cotangent, weight)
 
@@ -582,7 +582,9 @@
         ).astype(BF16)
     dkv_raw_ref[:, KVH * HD :] = dkv_ref[1]
     n_query = dq_ref.shape[1]
-    grad_hidden = nt(dq_ref[...], w_ref[:, :n_query]) + nt(dkv_raw_ref[...], w_ref[:, n_query:])
+    grad_hidden = nt(dq_ref[...], w_ref[:, :n_query]) + nt(
+        dkv_raw_ref[...], w_ref[:, n_query : n_query + 2 * KVH * HD]
+    )
     x = x_ref[...].astype(F32)
     inverse = lax.rsqrt(jnp.mean(x * x, axis=-1, keepdims=True) + EPSILON)
     normed = x * inverse
@@ -602,11 +604,7 @@
             jax.ShapeDtypeStruct((1, width), F32),
         ],
         compiler_params=params(),
-        cost_estimate=pl.CostEstimate(
-            flops=2 * rows * width * weight.shape[1],
-            bytes_accessed=2 * width * (weight.shape[1] + 5 * rows),
-            transcendentals=0,
-        ),
+        cost_estimate=SMALL,
         name="unproject",
     )(x, gain, grad_middle, dq, dkv, weight, cosine, sine)
 
@@ -647,22 +645,42 @@
     cap = (5 * rows * TOPK + 4 * experts - 1) // (4 * experts)
     half = rows // 2
 
+    n_in, n_out = expert_in.shape[1], expert_out.shape[1]
+    per_core = local // 2
+    packed = jnp.concatenate([expert_in, expert_out], axis=1)
+    own = lax.dynamic_slice_in_dim(packed, core * per_core, per_core, 0)
+    away = lax.dynamic_slice_in_dim(packed, (1 - core) * per_core, per_core, 0)
+    other = swap(away, "c")
+    pair = by_core(own[:, None], other[:, None], 1)
+    near = spread_high(pair)
+    unit = (n_in + n_out) // 18
+    cuts = [k * unit for k in (0, 6, 10, 12)] + [n_in + n_out]
+    far_piece = lambda k: swap(pair[:, :, cuts[k] : cuts[k + 1]], "t")
+    empty = lambda n: jnp.zeros((2, per_core, n_high, 2, n, width), BF16)
+
+    def place(whole, far, pieces, first):
+        count = pieces[0].shape[2]
+        split = min(max(n_in - first, 0), count)
+        if split > 0:
+            whole = (place_high(whole[0], far, [p[:, :, :split] for p in pieces], first), whole[1])
+        if split < count:
+            rest = [p[:, :, split:] for p in pieces]
+            whole = (whole[0], place_high(whole[1], far, rest, first + split - n_in))
+        return whole
+
+    far_0 = far_piece(0)
+
     small = jnp.concatenate([attn_gain[:, None], moe_gain[:, None], router_weight], axis=1)
     small = jnp.pad(small, ((0, 0), (0, HD - small.shape[1])))
-    first_pack = jnp.concatenate([query_weight, keyval_weight, small], axis=1)
+    n_q, n_kv = query_weight.shape[1], keyval_weight.shape[1]
 
     def gather_weight(part):
-        own = pick(part.reshape(2, part.shape[0] // 2, part.shape[1]), core, 0)
+        own = pick(part.reshape(2, -1, part.shape[1]), core, 0)
         return lax.all_gather(own, ("t", "l", "c"), axis=0, tiled=True)
 
-    first_full = gather_weight(first_pack)
-    output_full = gather_weight(output_weight)
-    n_qkv = query_weight.shape[1] + keyval_weight.shape[1]
-    qkv_full = first_full[:, :n_qkv]
-    small_full = first_full[:, n_qkv:].T
-    attn_scale = small_full[0:1].astype(F32)
-    moe_scale = small_full[1:2].astype(F32)
-    router_full = small_full[2 : 2 + experts]
+    first_full = gather_weight(
+        after(jnp.concatenate([query_weight, keyval_weight, small], axis=1), other)
+    )
 
     sub_len = seq_len // block_order.shape[0]
     inner = jnp.arange(block_len, dtype=jnp.int32)
@@ -692,86 +710,148 @@
     sine = jnp.concatenate([-sine, sine], axis=1)
     cosine_rows, sine_rows = jnp.tile(cosine, (seqs, 1)), jnp.tile(sine, (seqs, 1))
 
-    win = gather_expert(expert_in)
-    wout = gather_expert(expert_out)
-
     x = layer_input.reshape(rows, width)
-    hidden, qkv = project(x, attn_scale, qkv_full, cosine_rows, sine_rows)
-    keyval = qkv[:, H * HD :].reshape(seqs, 1, 1, block_len, 2 * KVH * HD)
+    grad_out = cotangent.reshape(rows, width) * live[:, None].astype(BF16)
+    extra = jnp.pad(slots, ((0, 0), (0, width - rows)))
+    cot_a, cot_b = grad_out[:half], jnp.concatenate([grad_out[half:], extra], axis=0)
+    low_bits = list(range(len(bits_of("l"))))
+    order_a, order_b = low_bits, low_bits[::-1]
+    flat = lambda value: value.reshape((n_low,) + value.shape[-2:])
+
+    def gather_low(a, b):
+        a, b = open_low(a), open_low(b)
+        for k in low_bits:
+            a, b = gather_bit(a, order_a[k]), gather_bit(b, order_b[k])
+        return flat(a), flat(b)
+
+    cot_a, cot_b = gather_low(cot_a, cot_b)
+
+    first_full, x, cot_a, cot_b, pair, near, far_0, output_weight = sync(
+        first_full, x, cot_a, cot_b, pair, near, far_0, output_weight
+    )
+    small_full = first_full[:, n_q + n_kv :].T
+    attn_scale = small_full[0:1].astype(F32)
+    moe_scale = small_full[1:2].astype(F32)
+    router_full = small_full[2 : 2 + experts]
+    output_full = gather_weight(output_weight)
+    far_1 = far_piece(1)
+    hidden, qkv = project(x, attn_scale, first_full, cosine_rows, sine_rows)
+    keyval = qkv[:, n_q:].reshape(seqs, 1, 1, block_len, n_kv)
     for bit in bits_of("h"):
         keyval = jnp.concatenate([keyval, swap(keyval, "h", bit)], axis=1)
     keyval = jnp.concatenate([keyval, swap(keyval, "c")], axis=2)
-    keyval = keyval.reshape(seqs, seq_len, 2 * KVH * HD)
+    keyval = keyval.reshape(seqs, seq_len, n_kv)
+    qkv, keyval, far_0 = sync(qkv, keyval, far_0)
+    far_0x = spread_high(far_0)
     posk, posq = key_pos[:, None], local_pos[None, :]
     attended, lse = attend(seq_lengths, qkv, keyval, posk, posq)
+
+    attended, far_0x, far_1, pair = sync(attended, far_0x, far_1, pair)
     middle, tok_a, tok_b, gates = route(
         attended, output_full, x, moe_scale, router_full, hit.astype(F32)
     )
-
-    grad_out = cotangent.reshape(rows, width) * live[:, None].astype(BF16)
-    extra = jnp.pad(slots, ((0, 0), (0, width - rows)))
-    cot_b = jnp.concatenate([grad_out[half:], extra], axis=0)
-    cot_a, cot_b, _ = lax.optimization_barrier((grad_out[:half], cot_b, qkv))
-
-    def to_group(part_a, part_b):
-        near_a, near_b = gather_group(part_a, True), gather_group(part_b, False)
-        return (near_a, near_b), (swap(near_a, "c"), swap(near_b, "c"))
-
-    cot_near, cot_far = to_group(cot_a, cot_b)
-    tok_near, tok_far = to_group(tok_a, tok_b)
-
-    number = jnp.arange(local, dtype=jnp.int32)
-    per_core = local // 2
-    ids = ((top ^ (number // per_core)) * n_low + low) * local + core * per_core + number % per_core
+    tok_a, tok_b, near, far_1, pair, cot_a, cot_b = sync(
+        tok_a, tok_b, near, far_1, pair, cot_a, cot_b
+    )
+
+    tok_a, tok_b = gather_bit(open_low(tok_a), order_a[0]), gather_bit(open_low(tok_b), order_b[0])
+    far_2 = far_piece(2)
+    far_1x = spread_high(far_1)
+    cot_far = swap(cot_a, "c"), swap(cot_b, "c")
+    whole = place((empty(n_in), empty(n_out)), 0, near, 0)
+    tok_a, tok_b, far_2, far_1x, pair, whole, cot_far = sync(
+        tok_a, tok_b, far_2, far_1x, pair, whole, cot_far
+    )
+    for k in range(1, len(low_bits)):
+        tok_a, tok_b = gather_bit(tok_a, order_a[k]), gather_bit(tok_b, order_b[k])
+    tok_a, tok_b = flat(tok_a), flat(tok_b)
+    far_3 = far_piece(3)
+    far_2x = spread_high(far_2)
+    whole = place(whole, 1, far_0x, cuts[0])
+    whole = place(whole, 1, far_1x, cuts[1])
+    tok_a, tok_b, far_3, far_2x, whole = sync(tok_a, tok_b, far_3, far_2x, whole)
+    far_3x = spread_high(far_3)
+    tok_far = swap(tok_a, "c"), swap(tok_b, "c")
+    whole = place(whole, 1, far_2x, cuts[2])
+    far_3x, tok_far, whole = sync(far_3x, tok_far, whole)
+    whole = place(whole, 1, far_3x, cuts[3])
+    win, wout = joined(whole[0]), joined(whole[1])
+
+    number = jnp.arange(2 * per_core, dtype=jnp.int32)
+    side = top ^ (number // per_core)
+    ids = (side * n_low + low) * local + core * per_core + number % per_core
+    ids = jnp.concatenate([ids, side * per_core + number % per_core])
     step = functools.partial(experts_step, ids, cap)
-    *saved, mix_near, back_near = step(0, *tok_near, *cot_near, win, wout, ())
-    *saved, mix_far, back_far = step(1, *tok_far, *cot_far, win, wout, saved)
+    *saved, mix_n, back_an, back_bn = step(0, tok_a, tok_b, cot_a, cot_b, win, wout, ())
+    *saved, mix_f, back_af, back_bf = step(1, *tok_far, *cot_far, win, wout, saved)
+
+    back_an, back_bn, back_af, back_bf, mix_f, mix_n, saved = sync(
+        back_an, back_bn, back_af, back_bf, mix_f, mix_n, saved
+    )
+    back_am, back_bm = swap(back_af, "c"), swap(back_bf, "c")
     picked, active, grad_both, grad_produced = (
-        s.reshape(local, 2 * n_low * cap, s.shape[-1]) for s in saved
-    )
-
-    def from_group(near, far):
-        total = add_low(near, swap(far, "c"))
-        return reduce_group(total[:, :half], True), reduce_group(total[:, half:], False)
-
-    back_a, back_b = from_group(back_near, back_far)
-    mix_near, mix_far, _ = lax.optimization_barrier((mix_near, mix_far, back_a))
-    mix_a, mix_b = from_group(mix_near, mix_far)
-    output = (middle + jnp.concatenate([mix_a, mix_b], axis=0).astype(F32)).astype(BF16)
-
-    grad_expert_out = jnp.einsum(
+        v.reshape(local, 2 * n_low * cap, v.shape[-1]) for v in saved
+    )
+    grad_wout = jnp.einsum(
         "erf,erd->efd", active, grad_produced, preferred_element_type=F32
     ).astype(BF16)
-    grad_expert_in = jnp.einsum(
+    back_am, back_bm, grad_wout, picked = sync(back_am, back_bm, grad_wout, picked)
+    out_sum = scatter_expert(grad_wout, per_core)
+    back_a = reduce_bit([low_axes(back_an), low_axes(back_am)], order_a[0])
+    back_b = reduce_bit([low_axes(back_bn), low_axes(back_bm)], order_b[0])
+    grad_win = jnp.einsum(
         "erd,erf->edf", picked, grad_both, preferred_element_type=F32
     ).astype(BF16)
-    expert_out_sum = reduce_expert(grad_expert_out, local)
-    expert_in_sum = reduce_expert(grad_expert_in, local)
-
+    mix_m = swap(mix_f, "c")
+    back_a, back_b, grad_win, mix_m = sync(back_a, back_b, grad_win, mix_m)
+    in_sum = scatter_expert(grad_win, per_core)
+    for k in range(1, len(low_bits)):
+        back_a, back_b = reduce_bit([back_a], order_a[k]), reduce_bit([back_b], order_b[k])
+    back_a, back_b = back_a.reshape(half, width), back_b.reshape(half + experts, width)
+
+    back_a, back_b, mix_n, mix_m, out_sum = sync(back_a, back_b, mix_n, mix_m, out_sum)
     grad_middle, branch, grad_attended, router_grad, moe_gain_grad = unroute(
         back_a, back_b, gates, middle, moe_scale, router_full, grad_out, output_full
     )
-    grad_output_weight = jnp.dot(attended.T, branch, preferred_element_type=F32).astype(BF16)
-    output_sum = reduce_weight(grad_output_weight)
+    mix = reduce_bit([low_axes(p) for p in (mix_n, mix_m)], 0)
+    grad_attended, branch = sync(grad_attended, branch)
+    grad_output_weight = weight_core(
+        jnp.dot(attended.T, branch, preferred_element_type=F32).astype(BF16)
+    )
     dq, dkv = attend_back(
         seq_lengths, qkv, keyval, posk, posq, grad_attended, attended, lse, cosine, sine
     )
-    grad_query_weight = jnp.dot(hidden.T, dq, preferred_element_type=F32).astype(BF16)
-    query_sum = reduce_weight(grad_query_weight)
+    dq, dkv, grad_output_weight = sync(dq, dkv, grad_output_weight)
     dkv = dkv.reshape(2, seqs, n_high, 2, block_len, KVH * HD)
     dkv = add_low(dkv[:, :, :, 0], swap(dkv[:, :, :, 1], "c"))
+    grad_output_weight = weight_low(grad_output_weight)
+    grad_query_weight = jnp.dot(hidden.T, dq, preferred_element_type=F32).astype(BF16)
+    dkv, grad_query_weight = sync(dkv, grad_query_weight)
     for bit in reversed(bits_of("h")):
         count = dkv.shape[2] // 2
         dkv = add_low(dkv[:, :, :count], swap(dkv[:, :, count:], "h", bit))
-    dkv = dkv.reshape(2, rows, KVH * HD)
+    grad_query_weight = weight_core(grad_query_weight)
+    dkv, grad_query_weight, mix = sync(dkv, grad_query_weight, mix)
+    grad_query_weight = weight_bits(grad_query_weight)
     grad_input, dkv_raw, attn_gain_grad = unproject(
-        x, attn_scale, grad_middle, dq, dkv, qkv_full, cosine_rows, sine_rows
+        x, attn_scale, grad_middle, dq, dkv.reshape(2, rows, KVH * HD), first_full,
+        cosine_rows, sine_rows,
     )
     grad_keyval_weight = jnp.dot(hidden.T, dkv_raw, preferred_element_type=F32).astype(BF16)
     small_grad = jnp.concatenate([attn_gain_grad, moe_gain_grad, router_grad], axis=0)
     small_grad = jnp.pad(small_grad, ((0, HD - small_grad.shape[0]), (0, 0))).astype(BF16).T
-    last_sum = reduce_weight(jnp.concatenate([grad_keyval_weight, small_grad], axis=1))
-    n_kv = keyval_weight.shape[1]
+    last = weight_core(jnp.concatenate([grad_keyval_weight, small_grad], axis=1))
+    last, grad_query_weight, grad_output_weight = sync(last, grad_query_weight, grad_output_weight)
+    for k in low_bits[1:]:
+        mix = reduce_bit([mix], k)
+    output = (middle + mix.reshape(rows, width).astype(F32)).astype(BF16)
+    query_output = weight_top(jnp.concatenate([grad_query_weight, grad_output_weight], axis=2))
+    last = weight_bits(last)
+    last, query_output = sync(last, query_output)
+    last_sum = weight_done(weight_high(weight_top(last)))
+    query_output_sum = weight_done(weight_high(query_output))
+    query_sum, output_sum = query_output_sum[:, :n_q], query_output_sum[:, n_q:]
+    expert_out_sum, expert_in_sum = reduce_core(out_sum), reduce_core(in_sum)
     shape = (seqs, block_len, width)
     return (
         output.reshape(shape),

time: 985 us -> 863 us (0.88)
  waiting for transfers between devices: 529 us -> 424 us
  other arithmetic: 89.6 us -> 75.9 us
  local copies, waits for them, and re-layouts: 84.3 us -> 72.6 us
  starting transfers between devices: 35.4 us -> 45.8 us
    all_gather x2, waiting for transfers between devices: 54.9 us -> 0.01 us  [gather_weight(): return lax.all_gather(own, ('t', 'l', 'c'), axis=0, tiled=True)]
    ppermute x58 -> x50, waiting for transfers between devices: 474 us -> 424 us  [swap(): return lax.ppermute(value, axis, [(i, i ^ bit) for i in range(size)])]
    convert_element_type x27 -> x11, other arithmetic: 45.5 us -> 11.1 us  [add_low(): return (a.astype(F32) + b.astype(F32)).astype(BF16)]
    convert_element_type x6 -> x11, other arithmetic: 9.63 us -> 34.8 us  [the longest x6 21.7 us: total_of(): return sum((p.astype(F32) for p in parts)).astype(BF16)]
    ppermute x58 -> x50, starting transfers between devices: 35.4 us -> 40.8 us  [swap(): return lax.ppermute(value, axis, [(i, i ^ bit) for i in range(size)])]
  transfers between devices with their start and end apart: 60 -> 55, of which waited for: 28 -> 23; matrix products, arithmetic and copies ran while one was open for 18% -> 20% of each run, Pallas kernels for 14% -> 10%
where the time goes in v2:
time: 863 us; the launch traced here: 857 us
  waiting for transfers between devices  424 us (49%)
  Pallas kernels  183 us (21%)
  other arithmetic  75.9 us (9%)
  local copies, waits for them, and re-layouts  72.6 us (8%)
  starting transfers between devices  45.8 us (5%)
  matrix products  40.9 us (5%)
  between operations  15.3 us (2%)
    ppermute x50, waiting for transfers between devices, swap(): return lax.ppermute(value, axis, [(i, i ^ bit) for i in range(size)])  424 us
    pallas_call x2, Pallas kernels, experts_step(): pl.pallas_call(functools.partial(expert_kernel, cap), grid_spec=pltpu.Pre...  88.2 us
    ppermute x50, starting transfers between devices, swap(): return lax.ppermute(value, axis, [(i, i ^ bit) for i in range(size)])  40.8 us
    pallas_call x1, Pallas kernels, attend_back(): pl.pallas_call(attend_back_kernel, grid_spec=pltpu.PrefetchScalarGridSpec...  29.5 us
    pallas_call x1, Pallas kernels, attend(): pl.pallas_call(attend_kernel, grid_spec=pltpu.PrefetchScalarGridSpec(num_...  25.4 us
    convert_element_type x6, other arithmetic, total_of(): return sum((p.astype(F32) for p in parts)).astype(BF16)  21.7 us
    dot_general x1, matrix products, per_device(): jnp.einsum('erd,erf->edf', picked, grad_both, preferred_element_type=F32)  19.4 us
    dynamic_update_slice x12, local copies, waits for them, and re-layouts, place_high(): lax.dynamic_update_slice(whole, p[None, :, None], (far, 0, high ^ r, 0, f...  17.7 us
  transfers between devices with their start and end apart: 55, of which 23 were waited for; matrix products, arithmetic and copies ran while one was open for 20% of the time, Pallas kernels for 10%

profile of v2, /device:TPU:0, one launch (start us, length us, event | category | flops | bytes accessed | tf_op | source)
XLA Modules:
  0.0 857.2 jit_solution(9960917656875410969)
XLA Ops:
  34.2 15.0 %collective-permute-done.1 = bf16[1,1,256,1536]{3,2,1,0:T(8,128)(2,1)} collective-permute-done((bf16[1,1,256,1536]{3,2,1,0:T(8,128)(2,1)S(1)}, bf16[1,1,256,1536]{3,2,1,0:T(8,128)(2,1)}, u32[]{:S(2)}, u32[]{:S(2)}) %collective-permute-start.1) | collective-permute-done | bytes 786464 | tf_op jit(solution)/shard_map/ppermute | solution.py:52
  52.3 13.7 %collective-permute-done.3 = bf16[1,1,272,1536]{3,2,1,0:T(8,128)(2,1)S(1)} collective-permute-done((bf16[1,1,272,1536]{3,2,1,0:T(8,128)(2,1)S(1)}, bf16[1,1,272,1536]{3,2,1,0:T(8,128)(2,1)S(1)}, u32[]{:S(2)}, u32[]{:S(2)}) %collective-permute-start.3) | collective-permute-done | bytes 835616 | tf_op jit(solution)/shard_map/ppermute | solution.py:52
  70.1 81.4 %collective-permute-done.2 = bf16[1,2,256,1536]{3,2,1,0:T(8,128)(2,1)S(1)} collective-permute-done((bf16[1,2,256,1536]{3,2,1,0:T(8,128)(2,1)S(1)}, bf16[1,2,256,1536]{3,2,1,0:T(8,128)(2,1)S(1)}, u32[]{:S(2)}, u32[]{:S(2)}) %collective-permute-start.2) | collective-permute-done | bytes 1572896 | tf_op jit(solution)/shard_map/ppermute | solution.py:52
  172.9 12.7 %collective-permute-done.7 = bf16[2,1,1,256,512]{4,3,2,1,0:T(8,128)(2,1)S(1)} collective-permute-done((bf16[2,1,1,256,512]{4,3,2,1,0:T(8,128)(2,1)S(1)}, bf16[2,1,1,256,512]{4,3,2,1,0:T(8,128)(2,1)S(1)}, u32[]{:S(2)}, u32[]{:S(2)}) %collective-permute-start.7) | collective-permute-done | bytes 524320 | tf_op jit(solution)/shard_map/ppermute | solution.py:52
  199.5 25.4 %attend.1 = (bf16[512,1536]{1,0:T(8,128)(2,1)}, f32[2,12,1,256]{3,2,1,0:T(1,128)}) custom-call(s32[2]{0:T(128)} %len_ref.3, bf16[512,2048]{1,0:T(8,128)(2,1)} %get-tuple-element.134.q_ref, bf16[2,1024,512]{2,1,0:T(8,128)(2,1)} %bitcast.207, bf16[2,1024,512]{2,1,0:T(8,128)(2,1)} %bitcast.208, s32[1024,1]{1,0:T(8,128)} %fusion.28.posk_ref, ...), custom_call_target="tpu_custom_call" | custom-call | flops 1000 | bytes 1000 | tf_op jit(solution)/shard_map/attend/pallas_call | solution.py:263
  224.8 15.7 %collective-permute-done.10 = bf16[1,2,128,1536]{3,2,1,0:T(8,128)(2,1)S(1)} collective-permute-done((bf16[1,2,128,1536]{3,2,1,0:T(8,128)(2,1)}, bf16[1,2,128,1536]{3,2,1,0:T(8,128)(2,1)S(1)}, u32[]{:S(2)}, u32[]{:S(2)}) %collective-permute-start.10) | collective-permute-done | bytes 786464 | tf_op jit(solution)/shard_map/ppermute | solution.py:52
  270.6 17.8 %collective-permute-done.13 = bf16[1,2,64,1536]{3,2,1,0:T(8,128)(2,1)S(1)} collective-permute-done((bf16[1,2,64,1536]{3,2,1,0:T(8,128)(2,1)S(1)}, bf16[1,2,64,1536]{3,2,1,0:T(8,128)(2,1)S(1)}, u32[]{:S(2)}, u32[]{:S(2)}) %collective-permute-start.13) | collective-permute-done | bytes 393248 | tf_op jit(solution)/shard_map/ppermute | solution.py:52
  300.1 50.4 %collective-permute-done.17 = bf16[1,2,256,1536]{3,2,1,0:T(8,128)(2,1)S(1)} collective-permute-done((bf16[1,2,256,1536]{3,2,1,0:T(8,128)(2,1)S(1)}, bf16[1,2,256,1536]{3,2,1,0:T(8,128)(2,1)S(1)}, u32[]{:S(2)}, u32[]{:S(2)}) %collective-permute-start.17) | collective-permute-done | bytes 1572896 | tf_op jit(solution)/shard_map/ppermute | solution.py:52
  360.4 23.2 %collective-permute-done.21 = bf16[1,2,192,1536]{3,2,1,0:T(8,128)(2,1)S(1)} collective-permute-done((bf16[1,2,192,1536]{3,2,1,0:T(8,128)(2,1)S(1)}, bf16[1,2,192,1536]{3,2,1,0:T(8,128)(2,1)S(1)}, u32[]{:S(2)}, u32[]{:S(2)}) %collective-permute-start.21) | collective-permute-done | bytes 1179680 | tf_op jit(solution)/shard_map/ppermute | solution.py:52
  385.8 43.6 %experts.2 = (bf16[2,2,4,160,1536]{4,3,2,1,0:T(8,128)(2,1)}, bf16[2,2,4,160,768]{4,3,2,1,0:T(8,128)(2,1)}, bf16[2,2,4,160,1536]{4,3,2,1,0:T(8,128)(2,1)}, bf16[2...) custom-call(s32[4]{0:T(128)} %pad_add_fusion.ids_ref, ...), custom_call_target="tpu_custom_call" | custom-call | flops 1000 | bytes 1000 | tf_op jit(solution)/shard_map/experts/pallas_call | solution.py:492
  429.4 44.6 %experts.3 = (bf16[2,2,4,160,1536]{4,3,2,1,0:T(8,128)(2,1)}, bf16[2,2,4,160,768]{4,3,2,1,0:T(8,128)(2,1)}, bf16[2,2,4,160,1536]{4,3,2,1,0:T(8,128)(2,1)}, bf16[2...) custom-call(s32[4]{0:T(128)} %pad_add_fusion.ids_ref, ...), custom_call_target="tpu_custom_call", output_to_operand_aliasing={{0}: (7, {}), {1}: (8, {}), {2}: (9, {}), {3}: (10, {})} | custom-call | flops 1000 | bytes 1000 | tf_op jit(solution)/shard_map/experts/pallas_call | solution.py:492
  474.6 11.5 %convolution_convert_fusion.3 = bf16[2,768,1536]{2,1,0:T(8,128)(2,1)} fusion(bf16[2,1280,768]{2,1,0:T(8,128)(2,1)} %bitcast.242, bf16[2,1280,1536]{2,1,0:T(8,128)(2,1)} %bitcast.226), kind=kOutput, calls=%fused_computation.9 | convolution fusion | flops 6042157056 | bytes 16515072 | tf_op jit(solution)/shard_map/erf,erd->efd/dot_general | solution.py:795
  491.6 19.4 %convolution_convert_fusion = bf16[2,1536,1536]{2,1,0:T(8,128)(2,1)} fusion(bf16[2,1280,1536]{2,1,0:T(8,128)(2,1)} %bitcast.224, bf16[2,1280,1536]{2,1,0:T(8,128)(2,1)} %bitcast.225), kind=kOutput, calls=%fused_computation | convolution fusion | flops 12084314112 | bytes 25165824 | tf_op jit(solution)/shard_map/erd,erf->edf/dot_general | solution.py:802
  511.0 16.8 %collective-permute-done.26 = bf16[2,1,256,1536]{3,2,1,0:T(8,128)(2,1)S(1)} collective-permute-done((bf16[2,1,256,1536]{3,2,1,0:T(8,128)(2,1)S(1)}, bf16[2,1,256,1536]{3,2,1,0:T(8,128)(2,1)S(1)}, u32[]{:S(2)}, u32[]{:S(2)}) %collective-permute-start.26) | collective-permute-done | bytes 1572896 | tf_op jit(solution)/shard_map/ppermute | solution.py:52
  531.0 22.3 %collective-permute-done.27 = bf16[1,2,272,1536]{3,2,1,0:T(8,128)(2,1)S(1)} collective-permute-done((bf16[1,2,272,1536]{3,2,1,0:T(8,128)(2,1)S(1)}, bf16[1,2,272,1536]{3,2,1,0:T(8,128)(2,1)S(1)}, u32[]{:S(2)}, u32[]{:S(2)}) %collective-permute-start.27) | collective-permute-done | bytes 1671200 | tf_op jit(solution)/shard_map/ppermute | solution.py:52
  558.1 29.5 %collective-permute-done.29 = bf16[1,1,256,1536]{3,2,1,0:T(8,128)(2,1)S(1)} collective-permute-done((bf16[1,1,256,1536]{3,2,1,0:T(8,128)(2,1)S(1)}, bf16[1,1,256,1536]{3,2,1,0:T(8,128)(2,1)S(1)}, u32[]{:S(2)}, u32[]{:S(2)}) %collective-permute-start.29) | collective-permute-done | bytes 786464 | tf_op jit(solution)/shard_map/ppermute | solution.py:52
  589.8 12.7 %unroute.1 = (f32[512,1536]{1,0:T(8,128)}, bf16[512,1536]{1,0:T(8,128)(2,1)}, bf16[512,1536]{1,0:T(8,128)(2,1)}, f32[16,1536]{1,0:T(8,128)}, f32[1,1536]{1,0:T(1,128)}) custom-call(bf16[256,1536]{1,0:T(8,128)(2,1)} %fusion.22.first_ref, bf16[272,1536]{1,0:T(8,128)(2,1)} %fusion.21.second_ref, f32[16,512]{1,0:T(8,128)} %get-tuple-element.216.gates_ref, ...), custom_call_target="tpu_custom_call" | custom-call | flops 1000 | bytes 1000 | tf_op jit(solution)/shard_map/unroute/pallas_call | solution.py:559
  615.3 29.5 %attend_back.1 = (bf16[512,1536]{1,0:T(8,128)(2,1)}, bf16[2,2,1024,256]{3,2,1,0:T(8,128)(2,1)}) custom-call(s32[2]{0:T(128)} %len_ref.3, bf16[512,2048]{1,0:T(8,128)(2,1)} %get-tuple-element.134.q_ref, bf16[2,1024,512]{2,1,0:T(8,128)(2,1)} %bitcast.209, bf16[2,1024,512]{2,1,0:T(8,128)(2,1)} %bitcast.210, s32[1024,1]{1,0:T(8,128)} %fusion.28.posk_ref, ...), custom_call_target="tpu_custom_call" | custom-call | flops 1000 | bytes 1000 | tf_op jit(solution)/shard_map/attend_back/pallas_call | solution.py:327
  662.4 29.5 %collective-permute-done.35 = bf16[2,1,512,1536]{3,2,1,0:T(8,128)(2,1)} collective-permute-done((bf16[2,1,512,1536]{3,2,1,0:T(8,128)(2,1)}, bf16[2,1,512,1536]{3,2,1,0:T(8,128)(2,1)}, u32[]{:S(2)}, u32[]{:S(2)}) %collective-permute-start.35) | collective-permute-done | bytes 3145760 | tf_op jit(solution)/shard_map/ppermute | solution.py:52
  704.0 10.2 %unproject.1 = (bf16[512,1536]{1,0:T(8,128)(2,1)}, bf16[512,512]{1,0:T(8,128)(2,1)}, f32[1,1536]{1,0:T(1,128)}) custom-call(bf16[512,1536]{1,0:T(8,128)(2,1)} %bitcast.220, f32[1,1536]{1,0:T(1,128)} %copy.188.gain_ref, f32[512,1536]{1,0:T(8,128)} %get-tuple-element.232.grad_ref, bf16[512,1536]{1,0:T(8,128)(2,1)} %get-tuple-element.226.dq_ref, ...), custom_call_target="tpu_custom_call" | custom-call | flops 1000 | bytes 1000 | tf_op jit(solution)/shard_map/unproject/pallas_call | solution.py:599
  725.5 10.3 %collective-permute-done.38 = bf16[2,2,96,1536]{3,2,1,0:T(8,128)(2,1)} collective-permute-done((bf16[2,2,96,1536]{3,2,1,0:T(8,128)(2,1)}, bf16[2,2,96,1536]{3,2,1,0:T(8,128)(2,1)}, u32[]{:S(2)}, u32[]{:S(2)}) %collective-permute-start.38) | collective-permute-done | bytes 1179680 | tf_op jit(solution)/shard_map/ppermute | solution.py:52
  750.0 17.4 %collective-permute-done.39 = bf16[2,1,96,1536]{3,2,1,0:T(8,128)(2,1)} collective-permute-done((bf16[2,1,96,1536]{3,2,1,0:T(8,128)(2,1)}, bf16[2,1,96,1536]{3,2,1,0:T(8,128)(2,1)}, u32[]{:S(2)}, u32[]{:S(2)}) %collective-permute-start.39) | collective-permute-done | bytes 589856 | tf_op jit(solution)/shard_map/ppermute | solution.py:52
  782.2 21.8 %collective-permute-done.42 = bf16[96,3072]{1,0:T(8,128)(2,1)S(1)} collective-permute-done((bf16[96,3072]{1,0:T(8,128)(2,1)S(1)}, bf16[96,3072]{1,0:T(8,128)(2,1)S(1)}, u32[]{:S(2)}, u32[]{:S(2)}) %collective-permute-start.42) | collective-permute-done | bytes 589856 | tf_op jit(solution)/shard_map/ppermute | solution.py:52
  804.1 14.7 %collective-permute-done.41 = bf16[2,1,96,640]{3,2,1,0:T(8,128)(2,1)S(1)} collective-permute-done((bf16[2,1,96,640]{3,2,1,0:T(8,128)(2,1)S(1)}, bf16[2,1,96,640]{3,2,1,0:T(8,128)(2,1)S(1)}, u32[]{:S(2)}, u32[]{:S(2)}) %collective-permute-start.41) | collective-permute-done | bytes 245792 | tf_op jit(solution)/shard_map/ppermute | solution.py:52
  (325 shorter events, 252.8 us)
Async XLA Ops:
  7.2 149.5 %all-gather.5.cloned.1.call-start = ((), (), s32[]{:S(2)}) async-start(), calls=%async_computation.5 | async-start | bytes 7102464 | tf_op jit(solution)/shard_map/all_gather | solution.py:679
  20.6 219.8 %all-gather.7.cloned.1.call-start = ((), (), s32[]{:S(2)}) async-start(), calls=%async_computation.6 | async-start | bytes 5013504 | tf_op jit(solution)/shard_map/all_gather | solution.py:679
  30.6 126.1 %collective-permute-start.5 = (bf16[1,2,576,1536]{3,2,1,0:T(8,128)(2,1)S(1)}, bf16[1,2,576,1536]{3,2,1,0:T(8,128)(2,1)}, u32[]{:S(2)}, u32[]{:S(2)}) collective-permute-start(bf16[1,2,576,1536]{3,2,1,0:T(8,128)(2,1)S(1)} %maximum_select_fusion), channel_id=1, source_target_pairs={{0,16},{16,0},{1,17},{17,1},{2,18},{18,2},{3,19},{19,3},{4,20},{20... | collective-permute-start | bytes 10616840 | tf_op jit(solution)/shard_map/ppermute | solution.py:52
  50.5 101.1 %collective-permute-start.2 = (bf16[1,2,256,1536]{3,2,1,0:T(8,128)(2,1)S(1)}, bf16[1,2,256,1536]{3,2,1,0:T(8,128)(2,1)S(1)}, u32[]{:S(2)}, u32[]{:S(2)}) collective-permute-start(bf16[1,2,256,1536]{3,2,1,0:T(8,128)(2,1)S(1)} %pad_maximum_fusion.8), channel_id=1, source_target_pairs={{0,2},{1,3},{2,0},{3,1},{4,6},{5,7},{6,4},{7,5},{8,10},{9,11},{10,... | collective-permute-start | bytes 4718600 | tf_op jit(solution)/shard_map/ppermute | solution.py:52
  66.2 88.5 %collective-permute-start.4 = (bf16[2,1,272,1536]{3,2,1,0:T(8,128)(2,1)S(1)}, bf16[2,1,272,1536]{3,2,1,0:T(8,128)(2,1)S(1)}, u32[]{:S(2)}, u32[]{:S(2)}) collective-permute-start(bf16[2,1,272,1536]{3,2,1,0:T(8,128)(2,1)S(1)} %pad_maximum_fusion.6), channel_id=1, source_target_pairs={{0,1},{1,0},{2,3},{3,2},{4,5},{5,4},{6,7},{7,6},{8,9},{9,8},{10,11... | collective-permute-start | bytes 5013512 | tf_op jit(solution)/shard_map/ppermute | solution.py:52
  67.6 89.1 %collective-permute-start.6 = (bf16[1,2,192,1536]{3,2,1,0:T(8,128)(2,1)S(1)}, bf16[1,2,192,1536]{3,2,1,0:T(8,128)(2,1)}, u32[]{:S(2)}, u32[]{:S(2)}) collective-permute-start(bf16[1,2,192,1536]{3,2,1,0:T(8,128)(2,1)S(1)} %slice.178), channel_id=1, source_target_pairs={{0,4},{4,0},{1,5},{5,1},{2,6},{6,2},{3,7},{7,3},{8,12},{12,8},{9,1... | collective-permute-start | bytes 3538952 | tf_op jit(solution)/shard_map/ppermute | solution.py:52
  157.4 432.4 %reduce-scatter.3.cloned.1.call-start = ((), (), s32[]{:S(2)}) async-start(), calls=%async_computation.3 | async-start | bytes 5898240 | tf_op jit(solution)/shard_map/reduce_scatter | solution.py:132
  190.0 50.5 %collective-permute-start.9 = (bf16[1,2,192,1536]{3,2,1,0:T(8,128)(2,1)}, bf16[1,2,192,1536]{3,2,1,0:T(8,128)(2,1)}, u32[]{:S(2)}, u32[]{:S(2)}) collective-permute-start(bf16[1,2,192,1536]{3,2,1,0:T(8,128)(2,1)} %collective-permute-done.6), channel_id=1, source_target_pairs={{0,16},{16,0},{1,17},{17,1},{2,18},{18,2},{3,19},{19,3},{4,20},{20... | collective-permute-start | bytes 3538952 | tf_op jit(solution)/shard_map/ppermute | solution.py:52
  193.0 47.5 %collective-permute-start.10 = (bf16[1,2,128,1536]{3,2,1,0:T(8,128)(2,1)}, bf16[1,2,128,1536]{3,2,1,0:T(8,128)(2,1)S(1)}, u32[]{:S(2)}, u32[]{:S(2)}) collective-permute-start(bf16[1,2,128,1536]{3,2,1,0:T(8,128)(2,1)} %slice.139), channel_id=1, source_target_pairs={{0,4},{4,0},{1,5},{5,1},{2,6},{6,2},{3,7},{7,3},{8,12},{12,8},{9,1... | collective-permute-start | bytes 2359304 | tf_op jit(solution)/shard_map/ppermute | solution.py:52
  248.6 39.8 %collective-permute-start.16 = (bf16[4,272,1536]{2,1,0:T(8,128)(2,1)}, bf16[4,272,1536]{2,1,0:T(8,128)(2,1)}, u32[]{:S(2)}, u32[]{:S(2)}) collective-permute-start(bf16[4,272,1536]{2,1,0:T(8,128)(2,1)} %bitcast.9.cot_b), channel_id=1, source_target_pairs={{0,8},{8,0},{1,9},{9,1},{2,10},{10,2},{3,11},{11,3},{4,12},{12,4},... | collective-permute-start | bytes 10027016 | tf_op jit(solution)/shard_map/ppermute | solution.py:52
  248.7 39.8 %collective-permute-start.15 = (bf16[4,256,1536]{2,1,0:T(8,128)(2,1)}, bf16[4,256,1536]{2,1,0:T(8,128)(2,1)}, u32[]{:S(2)}, u32[]{:S(2)}) collective-permute-start(bf16[4,256,1536]{2,1,0:T(8,128)(2,1)} %bitcast.5.cot_a), channel_id=1, source_target_pairs={{0,8},{8,0},{1,9},{9,1},{2,10},{10,2},{3,11},{11,3},{4,12},{12,4},... | collective-permute-start | bytes 9437192 | tf_op jit(solution)/shard_map/ppermute | solution.py:52
  250.5 37.9 %collective-permute-start.14 = (bf16[1,2,128,1536]{3,2,1,0:T(8,128)(2,1)S(1)}, bf16[1,2,128,1536]{3,2,1,0:T(8,128)(2,1)S(1)}, u32[]{:S(2)}, u32[]{:S(2)}) collective-permute-start(bf16[1,2,128,1536]{3,2,1,0:T(8,128)(2,1)S(1)} %collective-permute-done.10), channel_id=1, source_target_pairs={{0,16},{16,0},{1,17},{17,1},{2,18},{18,2},{3,19},{19,3},{4,20},{20... | collective-permute-start | bytes 2359304 | tf_op jit(solution)/shard_map/ppermute | solution.py:52
  288.5 64.0 %collective-permute-start.18 = (bf16[2,1,272,1536]{3,2,1,0:T(8,128)(2,1)S(1)}, bf16[2,1,272,1536]{3,2,1,0:T(8,128)(2,1)S(1)}, u32[]{:S(2)}, u32[]{:S(2)}) collective-permute-start(bf16[2,1,272,1536]{3,2,1,0:T(8,128)(2,1)S(1)} %pad_maximum_fusion.7), channel_id=1, source_target_pairs={{0,1},{1,0},{2,3},{3,2},{4,5},{5,4},{6,7},{7,6},{8,9},{9,8},{10,11... | collective-permute-start | bytes 5013512 | tf_op jit(solution)/shard_map/ppermute | solution.py:52
  289.9 60.5 %collective-permute-start.17 = (bf16[1,2,256,1536]{3,2,1,0:T(8,128)(2,1)S(1)}, bf16[1,2,256,1536]{3,2,1,0:T(8,128)(2,1)S(1)}, u32[]{:S(2)}, u32[]{:S(2)}) collective-permute-start(bf16[1,2,256,1536]{3,2,1,0:T(8,128)(2,1)S(1)} %pad_maximum_fusion.9), channel_id=1, source_target_pairs={{0,2},{1,3},{2,0},{3,1},{4,6},{5,7},{6,4},{7,5},{8,10},{9,11},{10,... | collective-permute-start | bytes 4718600 | tf_op jit(solution)/shard_map/ppermute | solution.py:52
  290.0 64.5 %collective-permute-start.19 = (bf16[1,2,192,1536]{3,2,1,0:T(8,128)(2,1)S(1)}, bf16[1,2,192,1536]{3,2,1,0:T(8,128)(2,1)S(1)}, u32[]{:S(2)}, u32[]{:S(2)}) collective-permute-start(bf16[1,2,192,1536]{3,2,1,0:T(8,128)(2,1)S(1)} %slice.147), channel_id=1, source_target_pairs={{0,4},{4,0},{1,5},{5,1},{2,6},{6,2},{3,7},{7,3},{8,12},{12,8},{9,1... | collective-permute-start | bytes 3538952 | tf_op jit(solution)/shard_map/ppermute | solution.py:52
  292.0 62.5 %collective-permute-start.20 = (bf16[1,2,64,1536]{3,2,1,0:T(8,128)(2,1)S(1)}, bf16[1,2,64,1536]{3,2,1,0:T(8,128)(2,1)S(1)}, u32[]{:S(2)}, u32[]{:S(2)}) collective-permute-start(bf16[1,2,64,1536]{3,2,1,0:T(8,128)(2,1)S(1)} %collective-permute-done.13), channel_id=1, source_target_pairs={{0,16},{16,0},{1,17},{17,1},{2,18},{18,2},{3,19},{19,3},{4,20},{20... | collective-permute-start | bytes 1179656 | tf_op jit(solution)/shard_map/ppermute | solution.py:52
  486.1 350.9 %reduce-scatter.5.cloned.1.call-start = ((), (), s32[]{:S(2)}) async-start(), calls=%async_computation.4 | async-start | bytes 11796480 | tf_op jit(solution)/shard_map/reduce_scatter | solution.py:132
  486.3 69.0 %collective-permute-start.28 = (bf16[4,512,1536]{2,1,0:T(8,128)(2,1)}, bf16[4,512,1536]{2,1,0:T(8,128)(2,1)}, u32[]{:S(2)}, u32[]{:S(2)}) collective-permute-start(bf16[4,512,1536]{2,1,0:T(8,128)(2,1)} %get-tuple-element.208), channel_id=1, source_target_pairs={{0,8},{8,0},{1,9},{9,1},{2,10},{10,2},{3,11},{11,3},{4,12},{12,4},... | collective-permute-start | bytes 18874376 | tf_op jit(solution)/shard_map/ppermute | solution.py:52
  489.0 64.3 %collective-permute-start.27 = (bf16[1,2,272,1536]{3,2,1,0:T(8,128)(2,1)S(1)}, bf16[1,2,272,1536]{3,2,1,0:T(8,128)(2,1)S(1)}, u32[]{:S(2)}, u32[]{:S(2)}) collective-permute-start(bf16[1,2,272,1536]{3,2,1,0:T(8,128)(2,1)S(1)} %fusion.8), channel_id=1, source_target_pairs={{0,2},{1,3},{2,0},{3,1},{4,6},{5,7},{6,4},{7,5},{8,10},{9,11},{10,... | collective-permute-start | bytes 5013512 | tf_op jit(solution)/shard_map/ppermute | solution.py:52
  614.4 77.6 %collective-permute-start.35 = (bf16[2,1,512,1536]{3,2,1,0:T(8,128)(2,1)}, bf16[2,1,512,1536]{3,2,1,0:T(8,128)(2,1)}, u32[]{:S(2)}, u32[]{:S(2)}) collective-permute-start(bf16[2,1,512,1536]{3,2,1,0:T(8,128)(2,1)} %add_convert_fusion.1), channel_id=1, source_target_pairs={{0,1},{1,0},{2,3},{3,2},{4,5},{5,4},{6,7},{7,6},{8,9},{9,8},{10,11... | collective-permute-start | bytes 9437192 | tf_op jit(solution)/shard_map/ppermute | solution.py:52
  656.3 43.3 %collective-permute-start.34 = (bf16[2,4,96,1536]{3,2,1,0:T(8,128)(2,1)}, bf16[2,4,96,1536]{3,2,1,0:T(8,128)(2,1)}, u32[]{:S(2)}, u32[]{:S(2)}) collective-permute-start(bf16[2,4,96,1536]{3,2,1,0:T(8,128)(2,1)} %dynamic-slice_bitcast_fusion), channel_id=1, source_target_pairs={{0,8},{8,0},{1,9},{9,1},{2,10},{10,2},{3,11},{11,3},{4,12},{12,4},... | collective-permute-start | bytes 7077896 | tf_op jit(solution)/shard_map/ppermute | solution.py:52
  656.3 90.0 %all-to-all-start = ((bf16[2,4,96,1536]{3,2,0,1:T(8,128)(2,1)}), bf16[2,4,96,1536]{3,2,0,1:T(8,128)(2,1)}, u32[]{:S(2)}, u32[]{:S(2)}) async-start(bf16[2,4,96,1536]{3,2,0,1:T(8,128)(2,1)} %fusion.1), calls=%async_computation.1 | async-start | bytes 4718592 | tf_op jit(solution)/shard_map/all_to_all | solution.py:149
  660.8 37.8 %collective-permute-start.33 = (bf16[2,2,1,256,256]{4,3,1,0,2:T(8,128)(2,1)S(1)}, bf16[2,2,1,256,256]{4,3,1,0,2:T(8,128)(2,1)S(1)}, u32[]{:S(2)}, u32[]{:S(2)}) collective-permute-start(bf16[2,2,1,256,256]{4,3,1,0,2:T(8,128)(2,1)S(1)} %slice.163), channel_id=1, source_target_pairs={{0,16},{16,0},{1,17},{17,1},{2,18},{18,2},{3,19},{19,3},{4,20},{20... | collective-permute-start | bytes 1572872 | tf_op jit(solution)/shard_map/ppermute | solution.py:52
  745.6 74.9 %collective-permute-start.36 = (bf16[1,1,512,1536]{3,2,1,0:T(8,128)(2,1)}, bf16[1,1,512,1536]{3,2,1,0:T(8,128)(2,1)}, u32[]{:S(2)}, u32[]{:S(2)}) collective-permute-start(bf16[1,1,512,1536]{3,2,1,0:T(8,128)(2,1)} %slice.169), channel_id=1, source_target_pairs={{0,2},{1,3},{2,0},{3,1},{4,6},{5,7},{6,4},{7,5},{8,10},{9,11},{10,... | collective-permute-start | bytes 4718600 | tf_op jit(solution)/shard_map/ppermute | solution.py:52
  (73 other events, 1220.1 us)
Sparse Core Ops, SparseCore 0:
  20.8 118.4 all-gather.4
  157.6 72.5 all-gather.6
  486.2 93.8 reduce-scatter.2
  583.1 173.0 reduce-scatter.4

commit v3 on v2

--- a/solution.py
+++ b/solution.py
@@ -14,6 +14,7 @@
 FF = 768
 TOPK = 4
 GROUP = H // KVH
+HEADS = 2
 
 EPSILON = 1e-06
 ROPE_BASE = 10000.0
@@ -90,12 +91,22 @@
     return sum(p.astype(F32) for p in parts).astype(BF16)
 
 
+def bit_part(value, k, index):
+    axis = len(bits_of("l")) - 1 - k
+    return lax.slice_in_dim(value, index, index + 1, axis=axis)
+
+
+def send_bit(parts, k):
+    send = total_of(*[bit_part(p, k, 1) for p in parts])
+    return swap(send, "l", bits_of("l")[k])
+
+
+def take_bit(parts, received, k):
+    return total_of(*[bit_part(p, k, 0) for p in parts], received)
+
+
 def reduce_bit(parts, k):
-    bits = bits_of("l")
-    axis = len(bits) - 1 - k
-    send = total_of(*[lax.slice_in_dim(p, 1, 2, axis=axis) for p in parts])
-    keep = [lax.slice_in_dim(p, 0, 1, axis=axis) for p in parts]
-    return total_of(*keep, swap(send, "l", bits[k]))
+    return take_bit(parts, send_bit(parts, k), k)
 
 
 def by_core(own, other, axis):
@@ -248,13 +259,15 @@
     def _():
         turned[...] = v_ref[0].T
 
-    scores = nt(k_ref[0], q_ref[...]) * (SCALE * LOG2E) + bias[...]
-    top = jnp.max(scores, axis=0, keepdims=True)
-    weights = jnp.exp2(scores - top)
-    total = jnp.sum(weights, axis=0, keepdims=True)
-    mixed = nn(turned[...], weights.astype(BF16)) * (1.0 / total)
-    out_ref[...] = mixed.T.astype(BF16)
-    lse_ref[0, 0] = top + jnp.log2(total)
+    for k in range(HEADS):
+        part = slice(k * HD, (k + 1) * HD)
+        scores = nt(k_ref[0], q_ref[:, part]) * (SCALE * LOG2E) + bias[...]
+        top = jnp.max(scores, axis=0, keepdims=True)
+        weights = jnp.exp2(scores - top)
+        total = jnp.sum(weights, axis=0, keepdims=True)
+        mixed = nn(turned[...], weights.astype(BF16)) * (1.0 / total)
+        out_ref[:, part] = mixed.T.astype(BF16)
+        lse_ref[0, k] = top + jnp.log2(total)
 
 
 def attend(lengths, qkv, keyval, posk, posq):
@@ -264,17 +277,17 @@
         attend_kernel,
         grid_spec=pltpu.PrefetchScalarGridSpec(
             num_scalar_prefetch=1,
-            grid=(seqs, KVH, GROUP),
+            grid=(seqs, KVH, GROUP // HEADS),
             in_specs=[
-                pl.BlockSpec((rows, HD), lambda s, g, h, n: (s, g * GROUP + h)),
+                pl.BlockSpec((rows, HEADS * HD), lambda s, g, h, n: (s, g * (GROUP // HEADS) + h)),
                 pl.BlockSpec((1, keys, HD), lambda s, g, h, n: (s, 0, g)),
                 pl.BlockSpec((1, keys, HD), lambda s, g, h, n: (s, 0, KVH + g)),
                 pl.BlockSpec((keys, 1), lambda s, g, h, n: (0, 0)),
                 pl.BlockSpec((1, rows), lambda s, g, h, n: (0, 0)),
             ],
             out_specs=[
-                pl.BlockSpec((rows, HD), lambda s, g, h, n: (s, g * GROUP + h)),
-                pl.BlockSpec((1, 1, 1, rows), lambda s, g, h, n: (s, g * GROUP + h, 0, 0)),
+                pl.BlockSpec((rows, HEADS * HD), lambda s, g, h, n: (s, g * (GROUP // HEADS) + h)),
+                pl.BlockSpec((1, HEADS, 1, rows), lambda s, g, h, n: (s, g * (GROUP // HEADS) + h, 0, 0)),
             ],
             scratch_shapes=[pltpu.VMEM((keys, rows), F32), pltpu.VMEM((HD, keys), BF16)],
         ),
@@ -301,19 +314,21 @@
         dk[...] = jnp.zeros_like(dk)
         dv[...] = jnp.zeros_like(dv)
 
-    q, grad = q_ref[...], grad_ref[...]
-    scores = nt(k_ref[0], q) * (SCALE * LOG2E) + bias[...]
-    probs = jnp.exp2(scores - lse_ref[0, 0])
-    grad_probs = nt(v_ref[0], grad)
-    product = grad.astype(F32) * out_ref[...].astype(F32)
-    delta = jnp.sum(product.T, axis=0, keepdims=True)
-    grad_scores = (probs * (grad_probs - delta)).astype(BF16)
-    dv[...] += nn(probs.astype(BF16), grad)
-    dk[...] += nn(grad_scores, q)
-    dq = nn(turned[...], grad_scores).T * SCALE
-    dq_ref[...] = turn(dq, cos_ref[...], -sin_ref[...]).astype(BF16)
-
-    @pl.when(head == GROUP - 1)
+    for k in range(HEADS):
+        part = slice(k * HD, (k + 1) * HD)
+        q, grad = q_ref[:, part], grad_ref[:, part]
+        scores = nt(k_ref[0], q) * (SCALE * LOG2E) + bias[...]
+        probs = jnp.exp2(scores - lse_ref[0, k])
+        grad_probs = nt(v_ref[0], grad)
+        product = grad.astype(F32) * out_ref[:, part].astype(F32)
+        delta = jnp.sum(product.T, axis=0, keepdims=True)
+        grad_scores = (probs * (grad_probs - delta)).astype(BF16)
+        dv[...] += nn(probs.astype(BF16), grad)
+        dk[...] += nn(grad_scores, q)
+        dq = nn(turned[...], grad_scores).T * SCALE
+        dq_ref[:, part] = turn(dq, cos_ref[...], -sin_ref[...]).astype(BF16)
+
+    @pl.when(head == GROUP // HEADS - 1)
     def _():
         dkv_ref[0, 0] = (dk[...] * SCALE).astype(BF16)
         dkv_ref[1, 0] = dv[...].astype(BF16)
@@ -322,13 +337,13 @@
 def attend_back(lengths, qkv, keyval, posk, posq, grad, attended, lse, cosine, sine):
     seqs, keys, _ = keyval.shape
     rows = qkv.shape[0] // seqs
-    heads = pl.BlockSpec((rows, HD), lambda s, g, h, n: (s, g * GROUP + h))
+    heads = pl.BlockSpec((rows, HEADS * HD), lambda s, g, h, n: (s, g * (GROUP // HEADS) + h))
     table = pl.BlockSpec((rows, HD), lambda s, g, h, n: (0, 0))
     return pl.pallas_call(
         attend_back_kernel,
         grid_spec=pltpu.PrefetchScalarGridSpec(
             num_scalar_prefetch=1,
-            grid=(seqs, KVH, GROUP),
+            grid=(seqs, KVH, GROUP // HEADS),
             in_specs=[
                 heads,
                 pl.BlockSpec((1, keys, HD), lambda s, g, h, n: (s, 0, g)),
@@ -337,7 +352,7 @@
                 pl.BlockSpec((1, rows), lambda s, g, h, n: (0, 0)),
                 heads,
                 heads,
-                pl.BlockSpec((1, 1, 1, rows), lambda s, g, h, n: (s, g * GROUP + h, 0, 0)),
+                pl.BlockSpec((1, HEADS, 1, rows), lambda s, g, h, n: (s, g * (GROUP // HEADS) + h, 0, 0)),
                 table,
                 table,
             ],
@@ -466,8 +481,9 @@
 
     for g in range(2):
         part = slice(g * cap, (g + 1) * cap)
-        mix_ref[g] = (mix_ref[g].astype(F32) + tn(spreads[g], weighed[part])).astype(BF16)
-        back = tn(spreads[g], grad_rows[part])
+        sums = tn(spreads[g], jnp.concatenate([weighed[part], grad_rows[part]], axis=1))
+        mix_ref[g] = (mix_ref[g].astype(F32) + sums[:, :width]).astype(BF16)
+        back = sums[:, width:]
         back_a[g] = (back_a[g].astype(F32) + back[:half]).astype(BF16)
         back_b[g, :half] = (back_b[g, :half].astype(F32) + back[half:]).astype(BF16)
         dense = jnp.sum(jnp.where(hits[g], grad_gate[part], 0.0), axis=0, keepdims=True)
@@ -541,10 +557,12 @@
     middle = middle_ref[...]
     inverse = lax.rsqrt(jnp.mean(middle * middle, axis=-1, keepdims=True) + EPSILON)
     normed = middle * inverse
-    tokens = (normed * gain_ref[...]).astype(BF16).astype(F32)
-    router_grad_ref[...] = nn(grad_logits, tokens, HIGHEST)
+    tokens = (normed * gain_ref[...]).astype(BF16)
+    coarse = grad_logits.astype(BF16)
+    fine = (grad_logits - coarse.astype(F32)).astype(BF16)
+    router_grad_ref[...] = nn(coarse, tokens) + nn(fine, tokens)
     grad_tokens = jnp.concatenate([first_ref[...], second_ref[:half]], axis=0).astype(F32)
-    grad_tokens = grad_tokens + nn(grad_logits.T, router_ref[...].astype(F32), HIGHEST)
+    grad_tokens = grad_tokens + tn(coarse, router_ref[...]) + tn(fine, router_ref[...])
     gain_grad_ref[...] = jnp.sum(grad_tokens * normed, axis=0, keepdims=True)
     grad_middle = cot_ref[...].astype(F32) + norm_back(grad_tokens, gain_ref[...], normed, inverse)
     grad_ref[...] = grad_middle
@@ -653,8 +671,8 @@
     other = swap(away, "c")
     pair = by_core(own[:, None], other[:, None], 1)
     near = spread_high(pair)
-    unit = (n_in + n_out) // 18
-    cuts = [k * unit for k in (0, 6, 10, 12)] + [n_in + n_out]
+    unit = (n_in + n_out) // 36
+    cuts = [k * unit for k in (0, 14, 20, 29)] + [n_in + n_out]
     far_piece = lambda k: swap(pair[:, :, cuts[k] : cuts[k + 1]], "t")
     empty = lambda n: jnp.zeros((2, per_core, n_high, 2, n, width), BF16)
 
@@ -782,38 +800,37 @@
     ids = (side * n_low + low) * local + core * per_core + number % per_core
     ids = jnp.concatenate([ids, side * per_core + number % per_core])
     step = functools.partial(experts_step, ids, cap)
-    *saved, mix_n, back_an, back_bn = step(0, tok_a, tok_b, cot_a, cot_b, win, wout, ())
-    *saved, mix_f, back_af, back_bf = step(1, *tok_far, *cot_far, win, wout, saved)
-
-    back_an, back_bn, back_af, back_bf, mix_f, mix_n, saved = sync(
-        back_an, back_bn, back_af, back_bf, mix_f, mix_n, saved
-    )
-    back_am, back_bm = swap(back_af, "c"), swap(back_bf, "c")
+    *saved, mix_f, back_af, back_bf = step(1, *tok_far, *cot_far, win, wout, ())
+    saved, mix_f, back_af, back_bf = sync(saved, mix_f, back_af, back_bf)
+    back_am, back_bm, mix_m = swap(back_af, "c"), swap(back_bf, "c"), swap(mix_f, "c")
+    *saved, mix_n, back_an, back_bn = step(0, tok_a, tok_b, cot_a, cot_b, win, wout, saved)
+
+    back_an, back_bn, back_am, back_bm, mix_m, mix_n, saved = sync(
+        back_an, back_bn, back_am, back_bm, mix_m, mix_n, saved
+    )
+    back_a = reduce_bit([low_axes(back_an), low_axes(back_am)], order_a[0])
+    back_b = reduce_bit([low_axes(back_bn), low_axes(back_bm)], order_b[0])
     picked, active, grad_both, grad_produced = (
         v.reshape(local, 2 * n_low * cap, v.shape[-1]) for v in saved
     )
     grad_wout = jnp.einsum(
         "erf,erd->efd", active, grad_produced, preferred_element_type=F32
     ).astype(BF16)
-    back_am, back_bm, grad_wout, picked = sync(back_am, back_bm, grad_wout, picked)
     out_sum = scatter_expert(grad_wout, per_core)
-    back_a = reduce_bit([low_axes(back_an), low_axes(back_am)], order_a[0])
-    back_b = reduce_bit([low_axes(back_bn), low_axes(back_bm)], order_b[0])
     grad_win = jnp.einsum(
-        "erd,erf->edf", picked, grad_both, preferred_element_type=F32
+        "erd,erf->edf", picked, after(grad_both, grad_wout), preferred_element_type=F32
     ).astype(BF16)
-    mix_m = swap(mix_f, "c")
-    back_a, back_b, grad_win, mix_m = sync(back_a, back_b, grad_win, mix_m)
+    back_a, back_b, grad_win, mix_n, mix_m = sync(back_a, back_b, grad_win, mix_n, mix_m)
     in_sum = scatter_expert(grad_win, per_core)
+    mix = send_bit([low_axes(p) for p in (mix_n, mix_m)], 0)
     for k in range(1, len(low_bits)):
         back_a, back_b = reduce_bit([back_a], order_a[k]), reduce_bit([back_b], order_b[k])
     back_a, back_b = back_a.reshape(half, width), back_b.reshape(half + experts, width)
 
-    back_a, back_b, mix_n, mix_m, out_sum = sync(back_a, back_b, mix_n, mix_m, out_sum)
+    back_a, back_b, out_sum = sync(back_a, back_b, out_sum)
     grad_middle, branch, grad_attended, router_grad, moe_gain_grad = unroute(
         back_a, back_b, gates, middle, moe_scale, router_full, grad_out, output_full
     )
-    mix = reduce_bit([low_axes(p) for p in (mix_n, mix_m)], 0)
     grad_attended, branch = sync(grad_attended, branch)
     grad_output_weight = weight_core(
         jnp.dot(attended.T, branch, preferred_element_type=F32).astype(BF16)
@@ -821,7 +838,8 @@
     dq, dkv = attend_back(
         seq_lengths, qkv, keyval, posk, posq, grad_attended, attended, lse, cosine, sine
     )
-    dq, dkv, grad_output_weight = sync(dq, dkv, grad_output_weight)
+    dq, dkv, grad_output_weight, mix, mix_n = sync(dq, dkv, grad_output_weight, mix, mix_n)
+    mix = take_bit([low_axes(p) for p in (mix_n, mix_m)], mix, 0)
     dkv = dkv.reshape(2, seqs, n_high, 2, block_len, KVH * HD)
     dkv = add_low(dkv[:, :, :, 0], swap(dkv[:, :, :, 1], "c"))
     grad_output_weight = weight_low(grad_output_weight)
@@ -841,15 +859,17 @@
     small_grad = jnp.concatenate([attn_gain_grad, moe_gain_grad, router_grad], axis=0)
     small_grad = jnp.pad(small_grad, ((0, HD - small_grad.shape[0]), (0, 0))).astype(BF16).T
     last = weight_core(jnp.concatenate([grad_keyval_weight, small_grad], axis=1))
-    last, grad_query_weight, grad_output_weight = sync(last, grad_query_weight, grad_output_weight)
+    last, grad_query_weight, grad_output_weight, mix = sync(
+        last, grad_query_weight, grad_output_weight, mix
+    )
     for k in low_bits[1:]:
         mix = reduce_bit([mix], k)
-    output = (middle + mix.reshape(rows, width).astype(F32)).astype(BF16)
     query_output = weight_top(jnp.concatenate([grad_query_weight, grad_output_weight], axis=2))
     last = weight_bits(last)
-    last, query_output = sync(last, query_output)
+    last, query_output, mix = sync(last, query_output, mix)
     last_sum = weight_done(weight_high(weight_top(last)))
     query_output_sum = weight_done(weight_high(query_output))
+    output = (middle + mix.reshape(rows, width).astype(F32)).astype(BF16)
     query_sum, output_sum = query_output_sum[:, :n_q], query_output_sum[:, n_q:]
     expert_out_sum, expert_in_sum = reduce_core(out_sum), reduce_core(in_sum)
     shape = (seqs, block_len, width)

time: 863 us -> 837 us (0.970)
  waiting for transfers between devices: 424 us -> 408 us
  Pallas kernels: 183 us -> 174 us
    ppermute x50, waiting for transfers between devices: 424 us -> 408 us  [swap(): return lax.ppermute(value, axis, [(i, i ^ bit) for i in range(size)])]
    convert_element_type x6 -> x7, other arithmetic: 21.7 us -> 20.6 us  [total_of(): return sum((p.astype(F32) for p in parts)).astype(BF16)]
    dynamic_update_slice x12 -> x14, local copies, waits for them, and re-layouts: 17.7 us -> 18 us  [place_high(): lax.dynamic_update_slice(whole, p[None, :, None], (far, 0, high ^ r, 0, f...]
  transfers between devices with their start and end apart: 55 -> 55, of which waited for: 23 -> 26; matrix products, arithmetic and copies ran while one was open for 20% -> 19% of each run, Pallas kernels for 10% -> 15%
where the time goes in v3:
time: 837 us; the launch traced here: 832 us
  waiting for transfers between devices  408 us (49%)
  Pallas kernels  174 us (21%)
  other arithmetic  74.4 us (9%)
  local copies, waits for them, and re-layouts  70.3 us (8%)
  starting transfers between devices  47.7 us (6%)
  matrix products  42.7 us (5%)
  between operations  15.3 us (2%)
    ppermute x50, waiting for transfers between devices, swap(): return lax.ppermute(value, axis, [(i, i ^ bit) for i in range(size)])  408 us
    pallas_call x2, Pallas kernels, experts_step(): pl.pallas_call(functools.partial(expert_kernel, cap), grid_spec=pltpu.Pre...  87.9 us
    ppermute x50, starting transfers between devices, swap(): return lax.ppermute(value, axis, [(i, i ^ bit) for i in range(size)])  42.8 us
    pallas_call x1, Pallas kernels, attend_back(): pl.pallas_call(attend_back_kernel, grid_spec=pltpu.PrefetchScalarGridSpec...  24.2 us
    pallas_call x1, Pallas kernels, attend(): pl.pallas_call(attend_kernel, grid_spec=pltpu.PrefetchScalarGridSpec(num_...  23 us
    convert_element_type x7, other arithmetic, total_of(): return sum((p.astype(F32) for p in parts)).astype(BF16)  20.6 us
    dot_general x1, matrix products, per_device(): jnp.einsum('erd,erf->edf', picked, after(grad_both, grad_wout), preferred...  19.7 us
    dynamic_update_slice x14, local copies, waits for them, and re-layouts, place_high(): lax.dynamic_update_slice(whole, p[None, :, None], (far, 0, high ^ r, 0, f...  18 us
  transfers between devices with their start and end apart: 55, of which 26 were waited for; matrix products, arithmetic and copies ran while one was open for 19% of the time, Pallas kernels for 15%

profile of v3, /device:TPU:0, one launch (start us, length us, event | category | flops | bytes accessed | tf_op | source)
XLA Modules:
  0.0 831.8 jit_solution(14167947390181873387)
XLA Ops:
  34.3 14.9 %collective-permute-done.1 = bf16[1,1,256,1536]{3,2,1,0:T(8,128)(2,1)} collective-permute-done((bf16[1,1,256,1536]{3,2,1,0:T(8,128)(2,1)S(1)}, bf16[1,1,256,1536]{3,2,1,0:T(8,128)(2,1)}, u32[]{:S(2)}, u32[]{:S(2)}) %collective-permute-start.1) | collective-permute-done | bytes 786464 | tf_op jit(solution)/shard_map/ppermute | solution.py:53
  52.3 13.7 %collective-permute-done.3 = bf16[1,1,272,1536]{3,2,1,0:T(8,128)(2,1)S(1)} collective-permute-done((bf16[1,1,272,1536]{3,2,1,0:T(8,128)(2,1)S(1)}, bf16[1,1,272,1536]{3,2,1,0:T(8,128)(2,1)S(1)}, u32[]{:S(2)}, u32[]{:S(2)}) %collective-permute-start.3) | collective-permute-done | bytes 835616 | tf_op jit(solution)/shard_map/ppermute | solution.py:53
  70.2 85.6 %collective-permute-done.2 = bf16[1,2,256,1536]{3,2,1,0:T(8,128)(2,1)S(1)} collective-permute-done((bf16[1,2,256,1536]{3,2,1,0:T(8,128)(2,1)S(1)}, bf16[1,2,256,1536]{3,2,1,0:T(8,128)(2,1)S(1)}, u32[]{:S(2)}, u32[]{:S(2)}) %collective-permute-start.2) | collective-permute-done | bytes 1572896 | tf_op jit(solution)/shard_map/ppermute | solution.py:53
  177.3 12.7 %collective-permute-done.7 = bf16[2,1,1,256,512]{4,3,2,1,0:T(8,128)(2,1)S(1)} collective-permute-done((bf16[2,1,1,256,512]{4,3,2,1,0:T(8,128)(2,1)S(1)}, bf16[2,1,1,256,512]{4,3,2,1,0:T(8,128)(2,1)S(1)}, u32[]{:S(2)}, u32[]{:S(2)}) %collective-permute-start.7) | collective-permute-done | bytes 524320 | tf_op jit(solution)/shard_map/ppermute | solution.py:53
  204.1 23.0 %attend.1 = (bf16[512,1536]{1,0:T(8,128)(2,1)}, f32[2,12,1,256]{3,2,1,0:T(1,128)}) custom-call(s32[2]{0:T(128)} %len_ref.3, bf16[512,2048]{1,0:T(8,128)(2,1)} %get-tuple-element.134.q_ref, bf16[2,1024,512]{2,1,0:T(8,128)(2,1)} %bitcast.214, bf16[2,1024,512]{2,1,0:T(8,128)(2,1)} %bitcast.215, s32[1024,1]{1,0:T(8,128)} %fusion.27.posk_ref, ...), custom_call_target="tpu_custom_call" | custom-call | flops 1000 | bytes 1000 | tf_op jit(solution)/shard_map/attend/pallas_call | solution.py:276
  227.1 9.2 %collective-permute-done.10 = bf16[1,2,96,1536]{3,2,1,0:T(8,128)(2,1)S(1)} collective-permute-done((bf16[1,2,96,1536]{3,2,1,0:T(8,128)(2,1)}, bf16[1,2,96,1536]{3,2,1,0:T(8,128)(2,1)S(1)}, u32[]{:S(2)}, u32[]{:S(2)}) %collective-permute-start.10) | collective-permute-done | bytes 589856 | tf_op jit(solution)/shard_map/ppermute | solution.py:53
  279.4 18.3 %collective-permute-done.13 = bf16[1,2,144,1536]{3,2,1,0:T(8,128)(2,1)S(1)} collective-permute-done((bf16[1,2,144,1536]{3,2,1,0:T(8,128)(2,1)S(1)}, bf16[1,2,144,1536]{3,2,1,0:T(8,128)(2,1)S(1)}, u32[]{:S(2)}, u32[]{:S(2)}) %collective-permute-start.13) | collective-permute-done | bytes 884768 | tf_op jit(solution)/shard_map/ppermute | solution.py:53
  308.7 39.6 %collective-permute-done.17 = bf16[1,2,256,1536]{3,2,1,0:T(8,128)(2,1)S(1)} collective-permute-done((bf16[1,2,256,1536]{3,2,1,0:T(8,128)(2,1)S(1)}, bf16[1,2,256,1536]{3,2,1,0:T(8,128)(2,1)S(1)}, u32[]{:S(2)}, u32[]{:S(2)}) %collective-permute-start.17) | collective-permute-done | bytes 1572896 | tf_op jit(solution)/shard_map/ppermute | solution.py:53
  357.7 13.0 %collective-permute-done.21 = bf16[1,2,112,1536]{3,2,1,0:T(8,128)(2,1)S(1)} collective-permute-done((bf16[1,2,112,1536]{3,2,1,0:T(8,128)(2,1)S(1)}, bf16[1,2,112,1536]{3,2,1,0:T(8,128)(2,1)S(1)}, u32[]{:S(2)}, u32[]{:S(2)}) %collective-permute-start.21) | collective-permute-done | bytes 688160 | tf_op jit(solution)/shard_map/ppermute | solution.py:53
  372.4 44.2 %experts.2 = (bf16[2,2,4,160,1536]{4,3,2,1,0:T(8,128)(2,1)}, bf16[2,2,4,160,768]{4,3,2,1,0:T(8,128)(2,1)}, bf16[2,2,4,160,1536]{4,3,2,1,0:T(8,128)(2,1)}, bf16[2...) custom-call(s32[4]{0:T(128)} %pad_add_fusion.ids_ref, ...), custom_call_target="tpu_custom_call" | custom-call | flops 1000 | bytes 1000 | tf_op jit(solution)/shard_map/experts/pallas_call | solution.py:508
  417.3 43.8 %experts.3 = (bf16[2,2,4,160,1536]{4,3,2,1,0:T(8,128)(2,1)}, bf16[2,2,4,160,768]{4,3,2,1,0:T(8,128)(2,1)}, bf16[2,2,4,160,1536]{4,3,2,1,0:T(8,128)(2,1)}, bf16[2...) custom-call(s32[4]{0:T(128)} %pad_add_fusion.ids_ref, ...), custom_call_target="tpu_custom_call", output_to_operand_aliasing={{0}: (7, {}), {1}: (8, {}), {2}: (9, {}), {3}: (10, {})} | custom-call | flops 1000 | bytes 1000 | tf_op jit(solution)/shard_map/experts/pallas_call | solution.py:508
  461.1 12.7 %convolution_convert_fusion.3 = bf16[2,768,1536]{2,1,0:T(8,128)(2,1)} fusion(bf16[2,1280,768]{2,1,0:T(8,128)(2,1)} %bitcast.249, bf16[2,1280,1536]{2,1,0:T(8,128)(2,1)} %bitcast.233), kind=kOutput, calls=%fused_computation.9 | convolution fusion | flops 6042157056 | bytes 16515072 | tf_op jit(solution)/shard_map/erf,erd->efd/dot_general | solution.py:816
  481.1 19.7 %convolution_convert_fusion = bf16[2,1536,1536]{2,1,0:T(8,128)(2,1)} fusion(bf16[2,1280,1536]{2,1,0:T(8,128)(2,1)} %bitcast.231, bf16[2,1280,1536]{2,1,0:T(8,128)(2,1)} %bitcast.232), kind=kOutput, calls=%fused_computation | convolution fusion | flops 12084314112 | bytes 25165824 | tf_op jit(solution)/shard_map/erd,erf->edf/dot_general | solution.py:820
  500.8 16.0 %collective-permute-done.27 = bf16[2,1,256,1536]{3,2,1,0:T(8,128)(2,1)S(1)} collective-permute-done((bf16[2,1,256,1536]{3,2,1,0:T(8,128)(2,1)}, bf16[2,1,256,1536]{3,2,1,0:T(8,128)(2,1)S(1)}, u32[]{:S(2)}, u32[]{:S(2)}) %collective-permute-start.27) | collective-permute-done | bytes 1572896 | tf_op jit(solution)/shard_map/ppermute | solution.py:53
  518.8 21.9 %collective-permute-done.28 = bf16[1,2,272,1536]{3,2,1,0:T(8,128)(2,1)S(1)} collective-permute-done((bf16[1,2,272,1536]{3,2,1,0:T(8,128)(2,1)S(1)}, bf16[1,2,272,1536]{3,2,1,0:T(8,128)(2,1)S(1)}, u32[]{:S(2)}, u32[]{:S(2)}) %collective-permute-start.28) | collective-permute-done | bytes 1671200 | tf_op jit(solution)/shard_map/ppermute | solution.py:53
  551.0 22.3 %collective-permute-done.29 = bf16[1,1,256,1536]{3,2,1,0:T(8,128)(2,1)} collective-permute-done((bf16[1,1,256,1536]{3,2,1,0:T(8,128)(2,1)}, bf16[1,1,256,1536]{3,2,1,0:T(8,128)(2,1)}, u32[]{:S(2)}, u32[]{:S(2)}) %collective-permute-start.29) | collective-permute-done | bytes 786464 | tf_op jit(solution)/shard_map/ppermute | solution.py:53
  576.7 10.9 %unroute.1 = (f32[512,1536]{1,0:T(8,128)}, bf16[512,1536]{1,0:T(8,128)(2,1)}, bf16[512,1536]{1,0:T(8,128)(2,1)}, f32[16,1536]{1,0:T(8,128)}, f32[1,1536]{1,0:T(1,128)}) custom-call(bf16[256,1536]{1,0:T(8,128)(2,1)} %fusion.21.first_ref, bf16[272,1536]{1,0:T(8,128)(2,1)} %fusion.20.second_ref, f32[16,512]{1,0:T(8,128)} %get-tuple-element.213.gates_ref, ...), custom_call_target="tpu_custom_call" | custom-call | flops 1000 | bytes 1000 | tf_op jit(solution)/shard_map/unroute/pallas_call | solution.py:577
  594.0 24.2 %attend_back.1 = (bf16[512,1536]{1,0:T(8,128)(2,1)}, bf16[2,2,1024,256]{3,2,1,0:T(8,128)(2,1)}) custom-call(s32[2]{0:T(128)} %len_ref.3, bf16[512,2048]{1,0:T(8,128)(2,1)} %get-tuple-element.134.q_ref, bf16[2,1024,512]{2,1,0:T(8,128)(2,1)} %bitcast.216, bf16[2,1024,512]{2,1,0:T(8,128)(2,1)} %bitcast.217, s32[1024,1]{1,0:T(8,128)} %fusion.27.posk_ref, ...), custom_call_target="tpu_custom_call" | custom-call | flops 1000 | bytes 1000 | tf_op jit(solution)/shard_map/attend_back/pallas_call | solution.py:342
  622.3 9.0 %collective-permute-done.32 = bf16[2,1,512,1536]{3,2,1,0:T(8,128)(2,1)} collective-permute-done((bf16[2,1,512,1536]{3,2,1,0:T(8,128)(2,1)}, bf16[2,1,512,1536]{3,2,1,0:T(8,128)(2,1)}, u32[]{:S(2)}, u32[]{:S(2)}) %collective-permute-start.32) | collective-permute-done | bytes 3145760 | tf_op jit(solution)/shard_map/ppermute | solution.py:53
  652.2 13.2 %collective-permute-done.34 = bf16[2,2,1,256,256]{4,3,1,0,2:T(8,128)(2,1)S(1)} collective-permute-done((bf16[2,2,1,256,256]{4,3,1,0,2:T(8,128)(2,1)S(1)}, bf16[2,2,1,256,256]{4,3,1,0,2:T(8,128)(2,1)S(1)}, u32[]{:S(2)}, u32[]{:S(2)}) %collective-permute-start.34) | collective-permute-done | bytes 524320 | tf_op jit(solution)/shard_map/ppermute | solution.py:53
  671.3 10.3 %unproject.1 = (bf16[512,1536]{1,0:T(8,128)(2,1)}, bf16[512,512]{1,0:T(8,128)(2,1)}, f32[1,1536]{1,0:T(1,128)}) custom-call(bf16[512,1536]{1,0:T(8,128)(2,1)} %bitcast.227, f32[1,1536]{1,0:T(1,128)} %copy.198.gain_ref, f32[512,1536]{1,0:T(8,128)} %get-tuple-element.214.grad_ref, bf16[512,1536]{1,0:T(8,128)(2,1)} %get-tuple-element.224.dq_ref, ...), custom_call_target="tpu_custom_call" | custom-call | flops 1000 | bytes 1000 | tf_op jit(solution)/shard_map/unproject/pallas_call | solution.py:617
  710.7 21.0 %collective-permute-done.38 = bf16[2,1,96,1536]{3,2,1,0:T(8,128)(2,1)} collective-permute-done((bf16[2,1,96,1536]{3,2,1,0:T(8,128)(2,1)}, bf16[2,1,96,1536]{3,2,1,0:T(8,128)(2,1)}, u32[]{:S(2)}, u32[]{:S(2)}) %collective-permute-start.38) | collective-permute-done | bytes 589856 | tf_op jit(solution)/shard_map/ppermute | solution.py:53
  748.5 32.1 %collective-permute-done.41 = bf16[96,3072]{1,0:T(8,128)(2,1)S(1)} collective-permute-done((bf16[96,3072]{1,0:T(8,128)(2,1)S(1)}, bf16[96,3072]{1,0:T(8,128)(2,1)S(1)}, u32[]{:S(2)}, u32[]{:S(2)}) %collective-permute-start.41) | collective-permute-done | bytes 589856 | tf_op jit(solution)/shard_map/ppermute | solution.py:53
  780.8 12.1 %collective-permute-done.40 = bf16[2,1,96,640]{3,2,1,0:T(8,128)(2,1)S(1)} collective-permute-done((bf16[2,1,96,640]{3,2,1,0:T(8,128)(2,1)S(1)}, bf16[2,1,96,640]{3,2,1,0:T(8,128)(2,1)S(1)}, u32[]{:S(2)}, u32[]{:S(2)}) %collective-permute-start.40) | collective-permute-done | bytes 245792 | tf_op jit(solution)/shard_map/ppermute | solution.py:53
  (332 shorter events, 273.1 us)
Async XLA Ops:
  7.2 153.8 %all-gather.5.cloned.1.call-start = ((), (), s32[]{:S(2)}) async-start(), calls=%async_computation.5 | async-start | bytes 7102464 | tf_op jit(solution)/shard_map/all_gather | solution.py:697
  20.7 215.6 %all-gather.7.cloned.1.call-start = ((), (), s32[]{:S(2)}) async-start(), calls=%async_computation.6 | async-start | bytes 5013504 | tf_op jit(solution)/shard_map/all_gather | solution.py:697
  30.6 130.4 %collective-permute-start.5 = (bf16[1,2,576,1536]{3,2,1,0:T(8,128)(2,1)S(1)}, bf16[1,2,576,1536]{3,2,1,0:T(8,128)(2,1)}, u32[]{:S(2)}, u32[]{:S(2)}) collective-permute-start(bf16[1,2,576,1536]{3,2,1,0:T(8,128)(2,1)S(1)} %maximum_select_fusion), channel_id=1, source_target_pairs={{0,16},{16,0},{1,17},{17,1},{2,18},{18,2},{3,19},{19,3},{4,20},{20... | collective-permute-start | bytes 10616840 | tf_op jit(solution)/shard_map/ppermute | solution.py:53
  50.5 105.3 %collective-permute-start.2 = (bf16[1,2,256,1536]{3,2,1,0:T(8,128)(2,1)S(1)}, bf16[1,2,256,1536]{3,2,1,0:T(8,128)(2,1)S(1)}, u32[]{:S(2)}, u32[]{:S(2)}) collective-permute-start(bf16[1,2,256,1536]{3,2,1,0:T(8,128)(2,1)S(1)} %pad_maximum_fusion.8), channel_id=1, source_target_pairs={{0,2},{1,3},{2,0},{3,1},{4,6},{5,7},{6,4},{7,5},{8,10},{9,11},{10,... | collective-permute-start | bytes 4718600 | tf_op jit(solution)/shard_map/ppermute | solution.py:53
  66.2 92.7 %collective-permute-start.4 = (bf16[2,1,272,1536]{3,2,1,0:T(8,128)(2,1)S(1)}, bf16[2,1,272,1536]{3,2,1,0:T(8,128)(2,1)S(1)}, u32[]{:S(2)}, u32[]{:S(2)}) collective-permute-start(bf16[2,1,272,1536]{3,2,1,0:T(8,128)(2,1)S(1)} %pad_maximum_fusion.6), channel_id=1, source_target_pairs={{0,1},{1,0},{2,3},{3,2},{4,5},{5,4},{6,7},{7,6},{8,9},{9,8},{10,11... | collective-permute-start | bytes 5013512 | tf_op jit(solution)/shard_map/ppermute | solution.py:53
  67.6 93.4 %collective-permute-start.6 = (bf16[1,2,224,1536]{3,2,1,0:T(8,128)(2,1)S(1)}, bf16[1,2,224,1536]{3,2,1,0:T(8,128)(2,1)}, u32[]{:S(2)}, u32[]{:S(2)}) collective-permute-start(bf16[1,2,224,1536]{3,2,1,0:T(8,128)(2,1)S(1)} %slice.194), channel_id=1, source_target_pairs={{0,4},{4,0},{1,5},{5,1},{2,6},{6,2},{3,7},{7,3},{8,12},{12,8},{9,1... | collective-permute-start | bytes 4128776 | tf_op jit(solution)/shard_map/ppermute | solution.py:53
  161.8 414.9 %reduce-scatter.3.cloned.1.call-start = ((), (), s32[]{:S(2)}) async-start(), calls=%async_computation.3 | async-start | bytes 5898240 | tf_op jit(solution)/shard_map/reduce_scatter | solution.py:143
  194.3 42.0 %collective-permute-start.9 = (bf16[1,2,224,1536]{3,2,1,0:T(8,128)(2,1)}, bf16[1,2,224,1536]{3,2,1,0:T(8,128)(2,1)}, u32[]{:S(2)}, u32[]{:S(2)}) collective-permute-start(bf16[1,2,224,1536]{3,2,1,0:T(8,128)(2,1)} %collective-permute-done.6), channel_id=1, source_target_pairs={{0,16},{16,0},{1,17},{17,1},{2,18},{18,2},{3,19},{19,3},{4,20},{20... | collective-permute-start | bytes 4128776 | tf_op jit(solution)/shard_map/ppermute | solution.py:53
  244.7 53.1 %collective-permute-start.16 = (bf16[4,272,1536]{2,1,0:T(8,128)(2,1)}, bf16[4,272,1536]{2,1,0:T(8,128)(2,1)}, u32[]{:S(2)}, u32[]{:S(2)}) collective-permute-start(bf16[4,272,1536]{2,1,0:T(8,128)(2,1)} %bitcast.9.cot_b), channel_id=1, source_target_pairs={{0,8},{8,0},{1,9},{9,1},{2,10},{10,2},{3,11},{11,3},{4,12},{12,4},... | collective-permute-start | bytes 10027016 | tf_op jit(solution)/shard_map/ppermute | solution.py:53
  244.8 52.9 %collective-permute-start.15 = (bf16[4,256,1536]{2,1,0:T(8,128)(2,1)}, bf16[4,256,1536]{2,1,0:T(8,128)(2,1)}, u32[]{:S(2)}, u32[]{:S(2)}) collective-permute-start(bf16[4,256,1536]{2,1,0:T(8,128)(2,1)} %bitcast.5.cot_a), channel_id=1, source_target_pairs={{0,8},{8,0},{1,9},{9,1},{2,10},{10,2},{3,11},{11,3},{4,12},{12,4},... | collective-permute-start | bytes 9437192 | tf_op jit(solution)/shard_map/ppermute | solution.py:53
  297.7 52.4 %collective-permute-start.18 = (bf16[2,1,272,1536]{3,2,1,0:T(8,128)(2,1)S(1)}, bf16[2,1,272,1536]{3,2,1,0:T(8,128)(2,1)S(1)}, u32[]{:S(2)}, u32[]{:S(2)}) collective-permute-start(bf16[2,1,272,1536]{3,2,1,0:T(8,128)(2,1)S(1)} %pad_maximum_fusion.7), channel_id=1, source_target_pairs={{0,1},{1,0},{2,3},{3,2},{4,5},{5,4},{6,7},{7,6},{8,9},{9,8},{10,11... | collective-permute-start | bytes 5013512 | tf_op jit(solution)/shard_map/ppermute | solution.py:53
  298.4 49.8 %collective-permute-start.17 = (bf16[1,2,256,1536]{3,2,1,0:T(8,128)(2,1)S(1)}, bf16[1,2,256,1536]{3,2,1,0:T(8,128)(2,1)S(1)}, u32[]{:S(2)}, u32[]{:S(2)}) collective-permute-start(bf16[1,2,256,1536]{3,2,1,0:T(8,128)(2,1)S(1)} %pad_maximum_fusion.9), channel_id=1, source_target_pairs={{0,2},{1,3},{2,0},{3,1},{4,6},{5,7},{6,4},{7,5},{8,10},{9,11},{10,... | collective-permute-start | bytes 4718600 | tf_op jit(solution)/shard_map/ppermute | solution.py:53
  298.5 53.6 %collective-permute-start.19 = (bf16[1,2,112,1536]{3,2,1,0:T(8,128)(2,1)S(1)}, bf16[1,2,112,1536]{3,2,1,0:T(8,128)(2,1)S(1)}, u32[]{:S(2)}, u32[]{:S(2)}) collective-permute-start(bf16[1,2,112,1536]{3,2,1,0:T(8,128)(2,1)S(1)} %slice.159), channel_id=1, source_target_pairs={{0,4},{4,0},{1,5},{5,1},{2,6},{6,2},{3,7},{7,3},{8,12},{12,8},{9,1... | collective-permute-start | bytes 2064392 | tf_op jit(solution)/shard_map/ppermute | solution.py:53
  300.6 51.5 %collective-permute-start.20 = (bf16[1,2,144,1536]{3,2,1,0:T(8,128)(2,1)S(1)}, bf16[1,2,144,1536]{3,2,1,0:T(8,128)(2,1)S(1)}, u32[]{:S(2)}, u32[]{:S(2)}) collective-permute-start(bf16[1,2,144,1536]{3,2,1,0:T(8,128)(2,1)S(1)} %collective-permute-done.13), channel_id=1, source_target_pairs={{0,16},{16,0},{1,17},{17,1},{2,18},{18,2},{3,19},{19,3},{4,20},{20... | collective-permute-start | bytes 2654216 | tf_op jit(solution)/shard_map/ppermute | solution.py:53
  416.6 44.5 %collective-permute-start.26 = (bf16[4,512,1536]{2,1,0:T(8,128)(2,1)}, bf16[4,512,1536]{2,1,0:T(8,128)(2,1)}, u32[]{:S(2)}, u32[]{:S(2)}) collective-permute-start(bf16[4,512,1536]{2,1,0:T(8,128)(2,1)} %get-tuple-element.192), channel_id=1, source_target_pairs={{0,8},{8,0},{1,9},{9,1},{2,10},{10,2},{3,11},{11,3},{4,12},{12,4},... | collective-permute-start | bytes 18874376 | tf_op jit(solution)/shard_map/ppermute | solution.py:53
  416.7 44.4 %collective-permute-start.25 = (bf16[4,272,1536]{2,1,0:T(8,128)(2,1)}, bf16[4,272,1536]{2,1,0:T(8,128)(2,1)S(1)}, u32[]{:S(2)}, u32[]{:S(2)}) collective-permute-start(bf16[4,272,1536]{2,1,0:T(8,128)(2,1)} %get-tuple-element.191), channel_id=1, source_target_pairs={{0,8},{8,0},{1,9},{9,1},{2,10},{10,2},{3,11},{11,3},{4,12},{12,4},... | collective-permute-start | bytes 10027016 | tf_op jit(solution)/shard_map/ppermute | solution.py:53
  417.2 43.9 %collective-permute-start.24 = (bf16[4,256,1536]{2,1,0:T(8,128)(2,1)}, bf16[4,256,1536]{2,1,0:T(8,128)(2,1)}, u32[]{:S(2)}, u32[]{:S(2)}) collective-permute-start(bf16[4,256,1536]{2,1,0:T(8,128)(2,1)} %get-tuple-element.190), channel_id=1, source_target_pairs={{0,8},{8,0},{1,9},{9,1},{2,10},{10,2},{3,11},{11,3},{4,12},{12,4},... | collective-permute-start | bytes 9437192 | tf_op jit(solution)/shard_map/ppermute | solution.py:53
  473.8 337.8 %reduce-scatter.5.cloned.1.call-start = ((), (), s32[]{:S(2)}) async-start(), calls=%async_computation.4 | async-start | bytes 11796480 | tf_op jit(solution)/shard_map/reduce_scatter | solution.py:143
  476.5 64.2 %collective-permute-start.28 = (bf16[1,2,272,1536]{3,2,1,0:T(8,128)(2,1)S(1)}, bf16[1,2,272,1536]{3,2,1,0:T(8,128)(2,1)S(1)}, u32[]{:S(2)}, u32[]{:S(2)}) collective-permute-start(bf16[1,2,272,1536]{3,2,1,0:T(8,128)(2,1)S(1)} %fusion.8), channel_id=1, source_target_pairs={{0,2},{1,3},{2,0},{3,1},{4,6},{5,7},{6,4},{7,5},{8,10},{9,11},{10,... | collective-permute-start | bytes 5013512 | tf_op jit(solution)/shard_map/ppermute | solution.py:53
  550.2 81.1 %collective-permute-start.32 = (bf16[2,1,512,1536]{3,2,1,0:T(8,128)(2,1)}, bf16[2,1,512,1536]{3,2,1,0:T(8,128)(2,1)}, u32[]{:S(2)}, u32[]{:S(2)}) collective-permute-start(bf16[2,1,512,1536]{3,2,1,0:T(8,128)(2,1)} %add_convert_fusion.1), channel_id=1, source_target_pairs={{0,1},{1,0},{2,3},{3,2},{4,5},{5,4},{6,7},{7,6},{8,9},{9,8},{10,11... | collective-permute-start | bytes 9437192 | tf_op jit(solution)/shard_map/ppermute | solution.py:53
  639.5 67.3 %all-to-all-start = ((bf16[2,4,96,1536]{3,2,0,1:T(8,128)(2,1)}), bf16[2,4,96,1536]{3,2,0,1:T(8,128)(2,1)}, u32[]{:S(2)}, u32[]{:S(2)}) async-start(bf16[2,4,96,1536]{3,2,0,1:T(8,128)(2,1)} %fusion.1), calls=%async_computation.1 | async-start | bytes 4718592 | tf_op jit(solution)/shard_map/all_to_all | solution.py:160
  733.2 59.8 %collective-permute-start.42 = (bf16[1,1,512,1536]{3,2,1,0:T(8,128)(2,1)S(1)}, bf16[1,1,512,1536]{3,2,1,0:T(8,128)(2,1)S(1)}, u32[]{:S(2)}, u32[]{:S(2)}) collective-permute-start(bf16[1,1,512,1536]{3,2,1,0:T(8,128)(2,1)S(1)} %slice.185), channel_id=1, source_target_pairs={{0,2},{1,3},{2,0},{3,1},{4,6},{5,7},{6,4},{7,5},{8,10},{9,11},{10,... | collective-permute-start | bytes 4718600 | tf_op jit(solution)/shard_map/ppermute | solution.py:53
  734.6 46.1 %collective-permute-start.41 = (bf16[96,3072]{1,0:T(8,128)(2,1)S(1)}, bf16[96,3072]{1,0:T(8,128)(2,1)S(1)}, u32[]{:S(2)}, u32[]{:S(2)}) collective-permute-start(bf16[96,3072]{1,0:T(8,128)(2,1)S(1)} %dynamic-slice_bitcast_fusion.8), channel_id=1, source_target_pairs={{0,4},{4,0},{1,5},{5,1},{2,6},{6,2},{3,7},{7,3},{8,12},{12,8},{9,1... | collective-permute-start | bytes 1769480 | tf_op jit(solution)/shard_map/ppermute | solution.py:53
  746.8 46.2 %collective-permute-start.40 = (bf16[2,1,96,640]{3,2,1,0:T(8,128)(2,1)S(1)}, bf16[2,1,96,640]{3,2,1,0:T(8,128)(2,1)S(1)}, u32[]{:S(2)}, u32[]{:S(2)}) collective-permute-start(bf16[2,1,96,640]{3,2,1,0:T(8,128)(2,1)S(1)} %constant_dynamic-slice_fusion), channel_id=1, source_target_pairs={{0,2},{1,3},{2,0},{3,1},{4,6},{5,7},{6,4},{7,5},{8,10},{9,11},{10,... | collective-permute-start | bytes 737288 | tf_op jit(solution)/shard_map/ppermute | solution.py:53
  (75 other events, 1233.8 us)
Sparse Core Ops, SparseCore 0:
  20.8 120.0 all-gather.4
  161.9 68.1 all-gather.6
  473.9 94.6 reduce-scatter.2
  571.6 174.7 reduce-scatter.4
